TPU v7x, 32 devices: a whole 2x2x4 slice. The times are simulated.
32 devices in a mesh: batch: 16 (over z, y, x), rep: 2 (over core).
Axes of the slice: x: 2, y: 2, z: 4, core: 2. Of those that a mesh axis runs over, the one named last changes fastest.
Arguments:
- feats: bfloat16 [2048, 512], P('batch')
- partner: int32 [2048], P('batch'), may hold values from 0 to 2047, as said below
Outputs:
- grad: float32 [2048, 512], P('batch')
- loss: float32 [2048], P('batch')
Inputs may be any that keep to these rules, and one draw needn't show every extreme that they name: partner pairs the rows: partner[partner[k]] = k and partner[k] != k.
All inputs are finite; a program needn't handle non-finite values.
Results may differ from a plain program's by a relative error of at most 0.0058.
Values may be sent and summed in bfloat16 or wider, within the bound.
No kernel may reach another device: no remote copies, remote signals or barrier semaphores. Data moves between devices by JAX's collectives and lax.ppermute only.
A program may use at most 64 MiB of HBM per device.

v0:
```python
import math

import jax
import jax.numpy as jnp
from jax import lax
from jax.sharding import PartitionSpec as P

inv_temp = 10.0


def on_device(feats, partner):
    rows, width = feats.shape
    layers = lax.axis_size("rep")
    share = rows // layers
    layer = lax.axis_index("rep")
    block_index = lax.axis_index("batch")
    hf = feats.astype(jnp.float32)
    scale = lax.rsqrt(jnp.sum(hf * hf, axis=-1, keepdims=True) + 1e-06)
    unit = hf * scale
    embed = unit.astype(jnp.bfloat16)
    own_ids = block_index * rows + jnp.arange(rows, dtype=jnp.int32)
    mine = lax.dynamic_slice_in_dim(embed, layer * share, share, 0)

    def key_ids(start, count):
        gathered = start + jnp.arange(count, dtype=jnp.int32)
        return gathered // share * rows + layer * share + gathered % share

    def first_fold(carry, piece, start):
        denom, pscore = carry
        score = jnp.dot(embed, piece.T, preferred_element_type=jnp.float32) * inv_temp
        ids = key_ids(start, piece.shape[0])
        weight = jnp.where(ids[None, :] == own_ids[:, None], 0.0, jnp.exp(score - inv_temp))
        hits = jnp.where(ids[None, :] == partner[:, None], score, 0.0)
        return (denom + jnp.sum(weight, axis=1), pscore + jnp.sum(hits, axis=1))

    empty_rows = jnp.zeros((rows,), jnp.float32)
    keys = lax.all_gather(mine, "batch", axis=0, tiled=True)
    group = math.gcd(lax.axis_size("batch"), max(1, 512 // share))
    span = group * share
    turns = keys.shape[0] // span
    stacked = keys.reshape(turns, span, width)
    starts = jnp.arange(turns, dtype=jnp.int32) * span

    def first_step(carry, item):
        return (first_fold(carry, item[0], item[1]), None)

    (denom, pscore), unused = lax.scan(first_step, (empty_rows, empty_rows), (stacked, starts))
    denom, pscore = lax.psum((denom, pscore), "rep")
    lse = jnp.log(denom) + inv_temp
    loss = lse - pscore
    lse_share = lax.dynamic_slice_in_dim(lse, layer * share, share, 0)

    def second_fold(acc, pieces, start):
        piece, piece_lse = pieces
        score = jnp.dot(embed, piece.T, preferred_element_type=jnp.float32) * inv_temp
        ids = key_ids(start, piece.shape[0])
        coeff = jnp.exp(score - lse[:, None]) + jnp.exp(score - piece_lse[None, :])
        coeff = coeff - 2.0 * jnp.where(ids[None, :] == partner[:, None], 1.0, 0.0)
        coeff = jnp.where(ids[None, :] == own_ids[:, None], 0.0, coeff).astype(jnp.bfloat16)
        return acc + jnp.dot(coeff, piece, preferred_element_type=jnp.float32)

    empty_acc = jnp.zeros((rows, width), jnp.float32)
    key_lse = lax.all_gather(lse_share, "batch", axis=0, tiled=True)
    stacked_lse = key_lse.reshape(turns, span)

    def second_step(acc, item):
        return (second_fold(acc, (item[0], item[1]), item[2]), None)

    acc, unused = lax.scan(second_step, empty_acc, (stacked, stacked_lse, starts))
    part_sum = lax.psum_scatter(acc, "rep", scatter_dimension=0, tiled=True)
    dz_share = part_sum * inv_temp
    unit_share = lax.dynamic_slice_in_dim(unit, layer * share, share, 0)
    scale_share = lax.dynamic_slice_in_dim(scale, layer * share, share, 0)
    grad_share = scale_share * (
        dz_share - unit_share * jnp.sum(unit_share * dz_share, axis=-1, keepdims=True)
    )
    grad = lax.all_gather(grad_share, "rep", axis=0, tiled=True)
    return (grad, loss)


def solution(mesh):
    in_specs = (P("batch", None), P("batch"))
    out_specs = (P("batch", None), P("batch"))
    return jax.shard_map(
        on_device, mesh=mesh, in_specs=in_specs, out_specs=out_specs, check_vma=False
    )
```

profile of v0, /device:TPU:0, one launch (start us, length us, event | category | flops | bytes accessed | tf_op | source)
XLA Modules:
  0.0 139.0 jit_solution(14824117562311006684)
XLA Ops:
  7.2 1.0 fusion.47
  8.3 0.1 convert_multiply_fusion
  8.4 0.6 constant_dynamic-slice_fusion.1
  9.0 0.0 reduce-scatter.2.cloned.1.call-start
  9.1 0.6 copy-done.4
  9.8 0.6 dynamic-slice.4
  11.1 58.3 %all-gather.2.cloned.1.call-done = bf16[1024,512]{1,0:T(8,128)(2,1)} async-done(((bf16[64,512]{1,0:T(8,128)(2,1)}), bf16[1024,512]{1,0:T(8,128)(2,1)}) %all-gather.2.cloned.1.call-update) | async-done | bytes 1048592 | tf_op jit(solution)/shard_map/all_gather | solution.py:37
  69.4 5.3 %while.28 = (s32[]{:T(128)}, f32[128]{0:T(128)S(1)}, f32[128]{0:T(128)S(1)}, s32[2]{0:T(128)S(1)}, s32[]{:T(128)}, /*index=5*/bf16[2,512,512]{2,1,0:T(8,128)(2,1...) while((s32[]{:T(128)}, f32[128]{0:T(128)S(1)}, ...), condition=%wide.region_4.5_spmd.clone, body=%wide.region_1.4_spmd.clone.sunk | while | flops 67645312 | bytes 665743 | solution.py:47
  69.4 0.6 dynamic_slice.81
  69.9 0.7 fusion.60
  70.6 1.4 select_reduce_fusion.3
  72.0 0.6 dynamic_slice.81
  72.6 0.7 fusion.60
  73.3 1.4 select_reduce_fusion.3
  74.7 2.5 %all-reduce.1 = (f32[128]{0:T(128)S(1)}, f32[128]{0:T(128)S(1)}) all-reduce(f32[128]{0:T(128)S(1)} %get-tuple-element.252, f32[128]{0:T(128)S(1)} %get-tuple-element.254), channel_id=1, replica_groups=mesh['batch'=16,'rep'=2] {'rep'}, use_global_device_ids=true, to_apply=%region_5.6 | all-reduce | flops 256 | bytes 2048 | tf_op jit(solution)/shard_map/psum | solution.py:48
  77.2 0.5 fusion.48
  77.7 0.2 dynamic-slice_dynamic-update-slice_fusion
  77.8 39.6 %all-reduce = f32[1024]{0:T(1024)S(1)} all-reduce(f32[1024]{0:T(1024)S(1)} %dynamic-slice_dynamic-update-slice_fusion), channel_id=1, replica_groups=mesh['batch'=16,'rep'=2] {'batch'}, use_global_device_ids=true, to_apply=%add | all-reduce | flops 1024 | bytes 8192
  117.4 6.4 %while.29 = (s32[]{:T(128)}, f32[128,512]{1,0:T(8,128)S(1)}, s32[2]{0:T(128)S(1)}, s32[]{:T(128)}, bf16[2,512,512]{2,1,0:T(8,128)(2,1)}, /*index=5*/bf16[128,512...) while((s32[]{:T(128)}, f32[128,512]{1,0:T(8,128)S(1)}, ...), condition=%wide.region_7.8_spmd.clone, body=%wide.region_6.7_spmd.clone.sunk | while | flops 135081600 | bytes 1717403 | solution.py:69
  117.4 0.6 dynamic_slice.85
  118.0 0.7 fusion.65
  118.7 1.9 %convolution_add_fusion.2 = f32[128,512]{1,0:T(8,128)S(1)} fusion(bf16[2,512,512]{2,1,0:T(8,128)(2,1)} %get-tuple-element.557, s32[]{:T(128)} %get-tuple-element.541, f32[128,512]{1,0:T(8,128)S(1)} %get-tuple-element.542, bf16[128,512]{1,0:T(8,128)(2,1)S(1)} %get-tuple-element.558, s32[128]{0:T(128)S(1)} %get-tuple-element.561, ...), kind=kOutput, calls=%fused_computation.26.clone.1 | convolution fusion | flops 135069696 | bytes 1710593 | tf_op jit(solution)/shard_map/while/body/eval_jaxpr/dot_general | solution.py:60
  120.6 0.6 dynamic_slice.85
  121.2 0.7 fusion.65
  121.9 1.9 %convolution_add_fusion.2 = f32[128,512]{1,0:T(8,128)S(1)} fusion(bf16[2,512,512]{2,1,0:T(8,128)(2,1)} %get-tuple-element.557, s32[]{:T(128)} %get-tuple-element.541, f32[128,512]{1,0:T(8,128)S(1)} %get-tuple-element.542, bf16[128,512]{1,0:T(8,128)(2,1)S(1)} %get-tuple-element.558, s32[128]{0:T(128)S(1)} %get-tuple-element.561, ...), kind=kOutput, calls=%fused_computation.26.clone.1 | convolution fusion | flops 135069696 | bytes 1710593 | tf_op jit(solution)/shard_map/while/body/eval_jaxpr/dot_general | solution.py:60
  123.8 0.7 copy-done.2
  124.6 0.1 dynamic-slice.3
  124.6 3.6 %reduce-scatter.2.cloned.1.call-done = f32[64,512]{1,0:T(8,128)} async-done(((f32[128,512]{1,0:T(8,128)}), f32[64,512]{1,0:T(8,128)}) %reduce-scatter.2.cloned.1.call-update) | async-done | bytes 131088 | tf_op jit(solution)/shard_map/reduce_scatter | solution.py:70
  128.2 1.1 multiply_reduce_fusion
  129.3 0.1 subtract_multiply_fusion
  129.4 2.0 %all_gather.11 = f32[128,512]{1,0:T(8,128)S(1)} all-gather(f32[64,512]{1,0:T(8,128)S(1)} %subtract_multiply_fusion), channel_id=1, replica_groups=mesh['batch'=16,'rep'=2] {'rep'}, dimensions={0}, use_global_device_ids=true | all-gather | bytes 393216 | tf_op jit(solution)/shard_map/all_gather | solution.py:77
  131.4 0.7 copy.21
  (26 shorter events, 0.2 us)
Async XLA Ops:
  7.2 1.1 copy-start
  7.2 62.2 %all-gather.2.cloned.1.call-start = ((), (), s32[]{:S(2)}) async-start(), calls=%async_computation.1 | async-start | bytes 1114112 | tf_op jit(solution)/shard_map/all_gather | solution.py:37
  9.0 119.2 %reduce-scatter.2.cloned.1.call-start = ((), (), s32[]{:S(2)}) async-start(), calls=%async_computation.2 | async-start | bytes 393216 | tf_op jit(solution)/shard_map/reduce_scatter | solution.py:70
  9.1 0.7 copy-start.4
  11.1 58.3 %copy-start.3 = (s32[128]{0:T(128)S(1)}, s32[128]{0:T(128)}, u32[]{:S(2)}) copy-start(s32[128]{0:T(128)} %param.7) | copy-start | bytes 1540
  123.8 0.7 copy-start.2
  128.2 1.1 copy-start.1
Sparse Core Ops, SparseCore 0:
  11.3 57.9 all-gather.1
  124.7 3.5 reduce-scatter.1
where the time goes:
time: 139 us
  waiting for transfers between devices  61.9 us (45%)
  blocking collectives  44 us (32%)
  between operations  14.8 us (11%)
  matrix products  6.52 us (5%)
  local copies, waits for them, and re-layouts  5.97 us (4%)
  other arithmetic  5.52 us (4%)
    all_gather x1, waiting for transfers between devices, on_device(): keys = lax.all_gather(mine, 'batch', axis=0, tiled=True)  58.3 us
    unnamed x1, blocking collectives  39.6 us
    dot_general x2, matrix products, second_fold(): return acc + jnp.dot(coeff, piece, preferred_element_type=jnp.float32)  3.78 us
    reduce_scatter x1, waiting for transfers between devices, on_device(): part_sum = lax.psum_scatter(acc, 'rep', scatter_dimension=0, tiled=True)  3.61 us
    unnamed x14, local copies, waits for them, and re-layouts  2.87 us
  transfers between devices with their start and end apart: 2, of which 2 were waited for; matrix products, arithmetic and copies ran while one was open for 1% of the time, Pallas kernels for 0%

commit v1 on v0

--- a/solution.py
+++ b/solution.py
@@ -1,14 +1,18 @@
+import functools
 import math
 
 import jax
 import jax.numpy as jnp
 from jax import lax
+from jax.experimental import pallas as pl
+from jax.experimental.pallas import tpu as pltpu
 from jax.sharding import PartitionSpec as P
 
 inv_temp = 10.0
-
-
-def on_device(feats, partner):
+log2e = 1.4426950408889634
+
+
+def split_plan(feats, partner):
     rows, width = feats.shape
     layers = lax.axis_size("rep")
     share = rows // layers
@@ -78,9 +82,150 @@
     return (grad, loss)
 
 
+X, Y, XY, Z1, Z2, Z3 = 1, 2, 3, 4, 8, 12
+
+
+def send(piece, first, second=None):
+    offsets = (first, first if second is None else second)
+    pairs = [
+        (2 * b + c, 2 * (b ^ offsets[c]) + c) for b in range(lax.axis_size("batch")) for c in range(2)
+    ]
+    return lax.ppermute(piece, ("batch", "rep"), pairs)
+
+
+def swap(piece):
+    return lax.ppermute(piece, "rep", [(0, 1), (1, 0)])
+
+
+def join(*pieces):
+    return jnp.concatenate(pieces, axis=0)
+
+
+def gather_halves(half):
+    z1, z2, z3 = send(half, Z1), send(half, Z2), send(half, Z3)
+    near = join(half, z1)
+    near_x, near_y, near_xy = send(near, X, Y), send(near, Y, X), send(near, XY)
+    far = join(z2, z3)
+    far_x, far_y, far_xy = send(far, X, Y), send(far, Y, X), send(far, XY)
+    n, f = (0, Z1), (Z2, Z3)
+    mine = [
+        (join(z1, near_x, near_y, near_xy), (Z1, *(X ^ o for o in n), *(Y ^ o for o in n), *(XY ^ o for o in n))),
+        (join(far, far_x, far_y), (*f, *(X ^ o for o in f), *(Y ^ o for o in f))),
+        (far_xy, tuple(XY ^ o for o in f)),
+    ]
+    return mine, [(swap(piece), offsets) for piece, offsets in mine]
+
+
+def score_kernel(n_pieces, own_ref, mate_ref, *refs):
+    pieces = refs[:n_pieces]
+    grad_ref, loss_ref, embed, weights, col_denom = refs[n_pieces:]
+    rows, width = own_ref.shape
+    total = embed.shape[0]
+    block = 2 * rows
+    blocks = total // block
+
+    def normalized(raw):
+        hf = raw.astype(jnp.float32)
+        scale = lax.rsqrt(jnp.sum(hf * hf, axis=-1, keepdims=True) + 1e-06)
+        return hf * scale, scale
+
+    start = 0
+    for ref in (own_ref, *pieces):
+        count = ref.shape[0]
+        for at in range(0, count, 64):
+            embed[start + at : start + at + 64, :] = normalized(ref[at : at + 64, :])[0].astype(jnp.bfloat16)
+        start += count
+
+    col_denom[...] = jnp.zeros_like(col_denom)
+    mates = mate_ref[...]
+    own_denom = jnp.zeros((rows, 128), jnp.float32)
+    own_hits = jnp.zeros((rows, 128), jnp.float32)
+    for i in range(blocks):
+        left = embed[i * block : (i + 1) * block, :]
+        row_sum = jnp.zeros((block, 128), jnp.float32)
+        for j in range(i, blocks):
+            right = embed[j * block : (j + 1) * block, :]
+            score = lax.dot_general(left, right, (((1,), (1,)), ((), ())), preferred_element_type=jnp.float32)
+            weight = jnp.exp2(score * (inv_temp * log2e))
+            if i == j:
+                r = lax.broadcasted_iota(jnp.int32, (block, block), 0)
+                c = lax.broadcasted_iota(jnp.int32, (block, block), 1)
+                weight = jnp.where(r == c, 0.0, weight)
+            if i == 0:
+                top = weight[:rows]
+                weights[:, j * block : (j + 1) * block] = top
+                ids = j * block + lax.broadcasted_iota(jnp.int32, (rows, block), 1)
+                hits = jnp.where(ids == mates, score[:rows], 0.0)
+                for k in range(0, block, 128):
+                    own_denom += top[:, k : k + 128]
+                    own_hits += hits[:, k : k + 128]
+            cols = jnp.sum(weight.reshape(block // 8, 8, block), axis=0)
+            col_denom[:, j * block : (j + 1) * block] += cols
+            if i != j:
+                for k in range(0, block, 128):
+                    row_sum += weight[:, k : k + 128]
+        if i != blocks - 1:
+            cols = jnp.sum(row_sum.T.reshape(16, 8, block), axis=0)
+            col_denom[:, i * block : (i + 1) * block] += cols
+
+    own = jnp.sum(own_denom, axis=1, keepdims=True)
+    loss_ref[...] = jnp.log(own) - inv_temp * jnp.sum(own_hits, axis=1, keepdims=True)
+    own_inverse = 1.0 / own
+    dz = jnp.zeros((rows, width), jnp.float32)
+    for j in range(blocks):
+        cols = slice(j * block, (j + 1) * block)
+        inverse = 1.0 / jnp.sum(col_denom[:, cols], axis=0, keepdims=True)
+        ids = j * block + lax.broadcasted_iota(jnp.int32, (rows, block), 1)
+        coeff = weights[:, cols] * (own_inverse + inverse) - jnp.where(ids == mates, 2.0, 0.0)
+        dz += jnp.dot(coeff.astype(jnp.bfloat16), embed[cols, :], preferred_element_type=jnp.float32)
+    dz = dz * inv_temp
+    unit, scale = normalized(own_ref[...])
+    grad_ref[...] = scale * (dz - unit * jnp.sum(unit * dz, axis=-1, keepdims=True))
+
+
+def whole_plan(feats, partner):
+    rows, width = feats.shape
+    share = rows // 2
+    layer = lax.axis_index("rep")
+    half = lax.dynamic_slice_in_dim(feats, layer * share, share, 0)
+    mine, other = gather_halves(half)
+    slots = [o for _, offsets in mine for o in offsets]
+    total = rows * lax.axis_size("batch")
+
+    offset = partner // rows ^ lax.axis_index("batch")
+    within = partner % rows
+    part = within // share
+    turned = jnp.where(part == 0, offset, offset & ~3 | (offset & 1) << 1 | (offset & 2) >> 1)
+    slot = jnp.sum(
+        jnp.where(turned[:, None] == jnp.array(slots, jnp.int32)[None, :], jnp.arange(len(slots), dtype=jnp.int32)[None, :], 0), axis=1
+    )
+    first = rows + jnp.where(part == layer, 0, len(slots) * share)
+    mate = jnp.where(offset == 0, within, first + slot * share + within % share)
+
+    pieces = [piece for piece, _ in mine + other]
+    vmem = pl.BlockSpec(memory_space=pltpu.VMEM)
+    grad, loss = pl.pallas_call(
+        functools.partial(score_kernel, len(pieces)),
+        out_shape=(
+            jax.ShapeDtypeStruct((rows, width), jnp.float32),
+            jax.ShapeDtypeStruct((rows, 1), jnp.float32),
+        ),
+        in_specs=[vmem] * (2 + len(pieces)),
+        out_specs=(vmem, vmem),
+        scratch_shapes=[
+            pltpu.VMEM((total, width), jnp.bfloat16),
+            pltpu.VMEM((rows, total), jnp.float32),
+            pltpu.VMEM((8, total), jnp.float32),
+        ],
+        compiler_params=pltpu.CompilerParams(vmem_limit_bytes=32 * 1024 * 1024),
+    )(feats, mate[:, None], *pieces)
+    return grad, loss[:, 0]
+
+
 def solution(mesh):
+    whole = mesh.shape["batch"] == 16 and mesh.shape["rep"] == 2
     in_specs = (P("batch", None), P("batch"))
     out_specs = (P("batch", None), P("batch"))
     return jax.shard_map(
-        on_device, mesh=mesh, in_specs=in_specs, out_specs=out_specs, check_vma=False
+        whole_plan if whole else split_plan, mesh=mesh, in_specs=in_specs, out_specs=out_specs, check_vma=False
     )

time: 139 us -> 33 us (0.24)
  waiting for transfers between devices: 61.9 us -> 9.76 us
  blocking collectives: 44 us -> 0 us
  starting transfers between devices: 0.08 us -> 14.8 us
  between operations: 14.8 us -> 0.74 us
  matrix products: 6.52 us -> 0 us
  other arithmetic: 5.52 us -> 0.76 us
  Pallas kernels: 0 us -> 4.23 us
  local copies, waits for them, and re-layouts: 5.97 us -> 2.09 us
    all_gather x1 -> x0, waiting for transfers between devices: 58.3 us -> none  [on_device(): keys = lax.all_gather(mine, 'batch', axis=0, tiled=True)]
    unnamed x1 -> x0, blocking collectives: 39.6 us -> none
    ppermute x0 -> x12, starting transfers between devices: none -> 14.8 us  [the longest x9 14.5 us: send(): return lax.ppermute(piece, ('batch', 'rep'), pairs)]
    ppermute x0 -> x12, waiting for transfers between devices: none -> 9.76 us  [the longest x9 8.54 us: send(): return lax.ppermute(piece, ('batch', 'rep'), pairs)]
    dot_general x4 -> x0, matrix products: 6.52 us -> none  [the longest x2 3.78 us: second_fold(): return acc + jnp.dot(coeff, piece, preferred_element_type=jnp.float32)]
    pallas_call x0 -> x1, Pallas kernels: none -> 4.23 us  [whole_plan(): pl.pallas_call(functools.partial(score_kernel, len(pieces)), out_shape=(j...]
    reduce_scatter x1 -> x0, waiting for transfers between devices: 3.61 us -> none  [on_device(): part_sum = lax.psum_scatter(acc, 'rep', scatter_dimension=0, tiled=True)]
    add x10 -> x0, other arithmetic: 2.69 us -> none  [the longest x4 2.63 us: key_ids(): return gathered // share * rows + layer * share + gathered % share]
  transfers between devices with their start and end apart: 2 -> 12, of which waited for: 2 -> 6; matrix products, arithmetic and copies ran while one was open for 1% -> 1% of each run, Pallas kernels for 0% -> 0%
where the time goes in v1:
time: 33 us; the launch traced here: 32.4 us
  starting transfers between devices  14.8 us (45%)
  waiting for transfers between devices  9.76 us (30%)
  Pallas kernels  4.23 us (13%)
  local copies, waits for them, and re-layouts  2.09 us (6%)
  other arithmetic  0.76 us (2%)
  between operations  0.74 us (2%)
    ppermute x9, starting transfers between devices, send(): return lax.ppermute(piece, ('batch', 'rep'), pairs)  14.5 us
    ppermute x9, waiting for transfers between devices, send(): return lax.ppermute(piece, ('batch', 'rep'), pairs)  8.54 us
    pallas_call x1, Pallas kernels, whole_plan(): pl.pallas_call(functools.partial(score_kernel, len(pieces)), out_shape=(j...  4.23 us
    ppermute x3, waiting for transfers between devices, swap(): return lax.ppermute(piece, 'rep', [(0, 1), (1, 0)])  1.22 us
    unnamed x11, local copies, waits for them, and re-layouts  1.09 us
    dynamic_slice x1, local copies, waits for them, and re-layouts, whole_plan(): half = lax.dynamic_slice_in_dim(feats, layer * share, share, 0)  0.85 us
  transfers between devices with their start and end apart: 12, of which 6 were waited for; matrix products, arithmetic and copies ran while one was open for 1% of the time, Pallas kernels for 0%

profile of v1, /device:TPU:0, one launch (start us, length us, event | category | flops | bytes accessed | tf_op | source)
XLA Modules:
  0.0 32.4 jit_solution(3504807723127456598)
XLA Ops:
  0.6 0.8 %constant_dynamic-slice_fusion = bf16[64,512]{1,0:T(8,128)(2,1)S(1)} fusion(bf16[128,512]{1,0:T(8,128)(2,1)} %own_ref.1, s32[]{:T(128)S(6)} %select_n.44), kind=kLoop, calls=%fused_computation.30 | loop fusion | bytes 131076 | tf_op jit(solution)/shard_map/dynamic_slice | solution.py:190
  1.5 4.0 %collective-permute-start.4 = (bf16[64,512]{1,0:T(8,128)(2,1)S(1)}, bf16[64,512]{1,0:T(8,128)(2,1)S(1)}, u32[]{:S(2)}, u32[]{:S(2)}) collective-permute-start(bf16[64,512]{1,0:T(8,128)(2,1)S(1)} %constant_dynamic-slice_fusion), channel_id=1, source_target_pairs={{0,16},{1,17},{2,18},{3,19},{4,20},{5,21},{6,22},{7,23},{8,24},{9,... | collective-permute-start | bytes 196616 | tf_op jit(solution)/shard_map/ppermute | solution.py:93
  5.5 1.3 %collective-permute-start.5 = (bf16[64,512]{1,0:T(8,128)(2,1)S(1)}, bf16[64,512]{1,0:T(8,128)(2,1)S(1)}, u32[]{:S(2)}, u32[]{:S(2)}) collective-permute-start(bf16[64,512]{1,0:T(8,128)(2,1)S(1)} %constant_dynamic-slice_fusion), channel_id=1, source_target_pairs={{0,24},{1,25},{2,26},{3,27},{4,28},{5,29},{6,30},{7,31},{8,16},{9,... | collective-permute-start | bytes 196616 | tf_op jit(solution)/shard_map/ppermute | solution.py:93
  6.9 0.2 collective-permute-start
  7.1 2.2 %collective-permute-done.4 = bf16[64,512]{1,0:T(8,128)(2,1)S(1)} collective-permute-done((bf16[64,512]{1,0:T(8,128)(2,1)S(1)}, bf16[64,512]{1,0:T(8,128)(2,1)S(1)}, u32[]{:S(2)}, u32[]{:S(2)}) %collective-permute-start.4) | collective-permute-done | bytes 65568 | tf_op jit(solution)/shard_map/ppermute | solution.py:93
  9.3 2.5 %collective-permute-done.5 = bf16[64,512]{1,0:T(8,128)(2,1)S(1)} collective-permute-done((bf16[64,512]{1,0:T(8,128)(2,1)S(1)}, bf16[64,512]{1,0:T(8,128)(2,1)S(1)}, u32[]{:S(2)}, u32[]{:S(2)}) %collective-permute-start.5) | collective-permute-done | bytes 65568 | tf_op jit(solution)/shard_map/ppermute | solution.py:93
  11.8 1.6 %collective-permute-start.6 = (bf16[128,512]{1,0:T(8,128)(2,1)S(1)}, bf16[128,512]{1,0:T(8,128)(2,1)S(1)}, u32[]{:S(2)}, u32[]{:S(2)}) collective-permute-start(bf16[128,512]{1,0:T(8,128)(2,1)S(1)} %get-tuple-element.9), channel_id=1, source_target_pairs={{0,2},{1,5},{2,0},{3,7},{4,6},{5,1},{6,4},{7,3},{8,10},{9,13},{10,... | collective-permute-start | bytes 393224 | tf_op jit(solution)/shard_map/ppermute | solution.py:93
  13.3 0.0 collective-permute-done
  13.3 1.6 %collective-permute-start.3 = (bf16[128,512]{1,0:T(8,128)(2,1)S(1)}, bf16[128,512]{1,0:T(8,128)(2,1)S(1)}, u32[]{:S(2)}, u32[]{:S(2)}) collective-permute-start(bf16[128,512]{1,0:T(8,128)(2,1)S(1)} %pad_maximum_fusion), channel_id=1, source_target_pairs={{0,6},{1,7},{2,4},{3,5},{4,2},{5,3},{6,0},{7,1},{8,14},{9,15},{10,... | collective-permute-start | bytes 393224 | tf_op jit(solution)/shard_map/ppermute | solution.py:93
  14.9 0.5 %collective-permute-start.2 = (bf16[128,512]{1,0:T(8,128)(2,1)S(1)}, bf16[128,512]{1,0:T(8,128)(2,1)S(1)}, u32[]{:S(2)}, u32[]{:S(2)}) collective-permute-start(bf16[128,512]{1,0:T(8,128)(2,1)S(1)} %pad_maximum_fusion), channel_id=1, source_target_pairs={{0,4},{1,3},{2,6},{3,1},{4,0},{5,7},{6,2},{7,5},{8,12},{9,11},{10,... | collective-permute-start | bytes 393224 | tf_op jit(solution)/shard_map/ppermute | solution.py:93
  15.4 1.5 %collective-permute-start.1 = (bf16[128,512]{1,0:T(8,128)(2,1)S(1)}, bf16[128,512]{1,0:T(8,128)(2,1)S(1)}, u32[]{:S(2)}, u32[]{:S(2)}) collective-permute-start(bf16[128,512]{1,0:T(8,128)(2,1)S(1)} %pad_maximum_fusion), channel_id=1, source_target_pairs={{0,2},{1,5},{2,0},{3,7},{4,6},{5,1},{6,4},{7,3},{8,10},{9,13},{10,... | collective-permute-start | bytes 393224 | tf_op jit(solution)/shard_map/ppermute | solution.py:93
  16.9 1.5 %collective-permute-start.7 = (bf16[128,512]{1,0:T(8,128)(2,1)S(1)}, bf16[128,512]{1,0:T(8,128)(2,1)S(1)}, u32[]{:S(2)}, u32[]{:S(2)}) collective-permute-start(bf16[128,512]{1,0:T(8,128)(2,1)S(1)} %get-tuple-element.9), channel_id=1, source_target_pairs={{0,4},{1,3},{2,6},{3,1},{4,0},{5,7},{6,2},{7,5},{8,12},{9,11},{10,... | collective-permute-start | bytes 393224 | tf_op jit(solution)/shard_map/ppermute | solution.py:93
  18.4 0.0 collective-permute-done.6
  18.4 2.3 %collective-permute-start.8 = (bf16[128,512]{1,0:T(8,128)(2,1)S(1)}, bf16[128,512]{1,0:T(8,128)(2,1)S(1)}, u32[]{:S(2)}, u32[]{:S(2)}) collective-permute-start(bf16[128,512]{1,0:T(8,128)(2,1)S(1)} %get-tuple-element.9), channel_id=1, source_target_pairs={{0,6},{1,7},{2,4},{3,5},{4,2},{5,3},{6,0},{7,1},{8,14},{9,15},{10,... | collective-permute-start | bytes 393224 | tf_op jit(solution)/shard_map/ppermute | solution.py:93
  20.7 2.7 %collective-permute-done.7 = bf16[128,512]{1,0:T(8,128)(2,1)S(1)} collective-permute-done((bf16[128,512]{1,0:T(8,128)(2,1)S(1)}, bf16[128,512]{1,0:T(8,128)(2,1)S(1)}, u32[]{:S(2)}, u32[]{:S(2)}) %collective-permute-start.7) | collective-permute-done | bytes 131104 | tf_op jit(solution)/shard_map/ppermute | solution.py:93
  23.4 0.1 collective-permute-start.10
  23.5 0.3 %collective-permute-done.1 = bf16[128,512]{1,0:T(8,128)(2,1)S(1)} collective-permute-done((bf16[128,512]{1,0:T(8,128)(2,1)S(1)}, bf16[128,512]{1,0:T(8,128)(2,1)S(1)}, u32[]{:S(2)}, u32[]{:S(2)}) %collective-permute-start.1) | collective-permute-done | bytes 131104 | tf_op jit(solution)/shard_map/ppermute | solution.py:93
  23.9 0.0 collective-permute-done.2
  23.9 0.0 copy-start.1
  23.9 0.0 copy-start
  23.9 0.0 collective-permute-done.3
  24.0 0.2 collective-permute-start.9
  24.2 0.4 %copy-done.1 = s32[128]{0:T(128)S(1)} copy-done((s32[128]{0:T(128)S(1)}, s32[128]{0:T(128)}, u32[]{:S(2)}) %copy-start.1) | copy-done | bytes 536
  24.6 0.0 copy-start.2
  24.6 0.6 %copy-done.2 = s32[15]{0:T(128)S(1)} copy-done((s32[15]{0:T(128)S(1)}, s32[15]{0:T(128)}, u32[]{:S(2)}) %copy-start.2) | copy-done | bytes 84
  25.2 0.1 select_reduce_fusion
  25.3 0.8 %collective-permute-done.8.refs_2_ = bf16[128,512]{1,0:T(8,128)(2,1)S(1)} collective-permute-done((bf16[128,512]{1,0:T(8,128)(2,1)S(1)}, bf16[128,512]{1,0:T(8,128)(2,1)S(1)}, u32[]{:S(2)}, u32[]{:S(2)}) %collective-permute-start.8) | collective-permute-done | bytes 131104 | tf_op jit(solution)/shard_map/ppermute | solution.py:93
  26.2 0.0 collective-permute-start.11
  26.2 0.1 copy.7.mate_ref
  26.3 1.2 %collective-permute-done.11.refs_5_ = bf16[128,512]{1,0:T(8,128)(2,1)S(1)} collective-permute-done((bf16[128,512]{1,0:T(8,128)(2,1)S(1)}, bf16[128,512]{1,0:T(8,128)(2,1)S(1)}, u32[]{:S(2)}, u32[]{:S(2)}) %collective-permute-start.11) | collective-permute-done | bytes 131104 | tf_op jit(solution)/shard_map/ppermute | solution.py:97
  27.5 4.2 %shard_map.50 = (f32[128,512]{1,0:T(8,128)}, f32[128,1]{1,0:T(8,128)S(1)}) custom-call(bf16[128,512]{1,0:T(8,128)(2,1)S(1)} %copy-done, s32[128,1]{1,0:T(8,128)S(1)} %copy.7.mate_ref, bf16[448,512]{1,0:T(8,128)(2,1)S(1)} %constant_dynamic-update-slice_fusion.refs_0_, bf16[384,512]{1,0:T(8,128)(2,1)S(1)} %constant_dynamic-update-slice_fusion.6.refs_1_, ...), custom_call_target="tpu_custom_call" | custom-call | tf_op jit(solution)/shard_map/pallas_call | solution.py:207
  31.8 0.6 %reduce = f32[128]{0:T(128)} reduce(f32[128,1]{1,0:T(8,128)S(1)} %get-tuple-element.5, f32[]{:T(128)} %constant.70), dimensions={1}, to_apply=%get-tuple-element.5.reduce_sub_computation | reduce | bytes 1028 | tf_op jit(solution)/shard_map/pallas_call | solution.py:207
  (14 shorter events, 0.1 us)
Async XLA Ops:
  1.5 7.8 %collective-permute-start.4 = (bf16[64,512]{1,0:T(8,128)(2,1)S(1)}, bf16[64,512]{1,0:T(8,128)(2,1)S(1)}, u32[]{:S(2)}, u32[]{:S(2)}) collective-permute-start(bf16[64,512]{1,0:T(8,128)(2,1)S(1)} %constant_dynamic-slice_fusion), channel_id=1, source_target_pairs={{0,16},{1,17},{2,18},{3,19},{4,20},{5,21},{6,22},{7,23},{8,24},{9,... | collective-permute-start | bytes 196616 | tf_op jit(solution)/shard_map/ppermute | solution.py:93
  5.5 6.2 %collective-permute-start.5 = (bf16[64,512]{1,0:T(8,128)(2,1)S(1)}, bf16[64,512]{1,0:T(8,128)(2,1)S(1)}, u32[]{:S(2)}, u32[]{:S(2)}) collective-permute-start(bf16[64,512]{1,0:T(8,128)(2,1)S(1)} %constant_dynamic-slice_fusion), channel_id=1, source_target_pairs={{0,24},{1,25},{2,26},{3,27},{4,28},{5,29},{6,30},{7,31},{8,16},{9,... | collective-permute-start | bytes 196616 | tf_op jit(solution)/shard_map/ppermute | solution.py:93
  6.9 6.4 %collective-permute-start = (bf16[64,512]{1,0:T(8,128)(2,1)S(1)}, bf16[64,512]{1,0:T(8,128)(2,1)S(1)}, u32[]{:S(2)}, u32[]{:S(2)}) collective-permute-start(bf16[64,512]{1,0:T(8,128)(2,1)S(1)} %constant_dynamic-slice_fusion), channel_id=1, source_target_pairs={{0,8},{1,9},{2,10},{3,11},{4,12},{5,13},{6,14},{7,15},{8,0},{9,1},... | collective-permute-start | bytes 196616 | tf_op jit(solution)/shard_map/ppermute | solution.py:93
  11.8 6.7 %collective-permute-start.6 = (bf16[128,512]{1,0:T(8,128)(2,1)S(1)}, bf16[128,512]{1,0:T(8,128)(2,1)S(1)}, u32[]{:S(2)}, u32[]{:S(2)}) collective-permute-start(bf16[128,512]{1,0:T(8,128)(2,1)S(1)} %get-tuple-element.9), channel_id=1, source_target_pairs={{0,2},{1,5},{2,0},{3,7},{4,6},{5,1},{6,4},{7,3},{8,10},{9,13},{10,... | collective-permute-start | bytes 393224 | tf_op jit(solution)/shard_map/ppermute | solution.py:93
  13.3 10.6 %collective-permute-start.3 = (bf16[128,512]{1,0:T(8,128)(2,1)S(1)}, bf16[128,512]{1,0:T(8,128)(2,1)S(1)}, u32[]{:S(2)}, u32[]{:S(2)}) collective-permute-start(bf16[128,512]{1,0:T(8,128)(2,1)S(1)} %pad_maximum_fusion), channel_id=1, source_target_pairs={{0,6},{1,7},{2,4},{3,5},{4,2},{5,3},{6,0},{7,1},{8,14},{9,15},{10,... | collective-permute-start | bytes 393224 | tf_op jit(solution)/shard_map/ppermute | solution.py:93
  14.9 9.0 %collective-permute-start.2 = (bf16[128,512]{1,0:T(8,128)(2,1)S(1)}, bf16[128,512]{1,0:T(8,128)(2,1)S(1)}, u32[]{:S(2)}, u32[]{:S(2)}) collective-permute-start(bf16[128,512]{1,0:T(8,128)(2,1)S(1)} %pad_maximum_fusion), channel_id=1, source_target_pairs={{0,4},{1,3},{2,6},{3,1},{4,0},{5,7},{6,2},{7,5},{8,12},{9,11},{10,... | collective-permute-start | bytes 393224 | tf_op jit(solution)/shard_map/ppermute | solution.py:93
  15.4 8.5 %collective-permute-start.1 = (bf16[128,512]{1,0:T(8,128)(2,1)S(1)}, bf16[128,512]{1,0:T(8,128)(2,1)S(1)}, u32[]{:S(2)}, u32[]{:S(2)}) collective-permute-start(bf16[128,512]{1,0:T(8,128)(2,1)S(1)} %pad_maximum_fusion), channel_id=1, source_target_pairs={{0,2},{1,5},{2,0},{3,7},{4,6},{5,1},{6,4},{7,3},{8,10},{9,13},{10,... | collective-permute-start | bytes 393224 | tf_op jit(solution)/shard_map/ppermute | solution.py:93
  16.9 6.5 %collective-permute-start.7 = (bf16[128,512]{1,0:T(8,128)(2,1)S(1)}, bf16[128,512]{1,0:T(8,128)(2,1)S(1)}, u32[]{:S(2)}, u32[]{:S(2)}) collective-permute-start(bf16[128,512]{1,0:T(8,128)(2,1)S(1)} %get-tuple-element.9), channel_id=1, source_target_pairs={{0,4},{1,3},{2,6},{3,1},{4,0},{5,7},{6,2},{7,5},{8,12},{9,11},{10,... | collective-permute-start | bytes 393224 | tf_op jit(solution)/shard_map/ppermute | solution.py:93
  18.4 7.8 %collective-permute-start.8 = (bf16[128,512]{1,0:T(8,128)(2,1)S(1)}, bf16[128,512]{1,0:T(8,128)(2,1)S(1)}, u32[]{:S(2)}, u32[]{:S(2)}) collective-permute-start(bf16[128,512]{1,0:T(8,128)(2,1)S(1)} %get-tuple-element.9), channel_id=1, source_target_pairs={{0,6},{1,7},{2,4},{3,5},{4,2},{5,3},{6,0},{7,1},{8,14},{9,15},{10,... | collective-permute-start | bytes 393224 | tf_op jit(solution)/shard_map/ppermute | solution.py:93
  23.4 4.1 %collective-permute-start.10 = (bf16[384,512]{1,0:T(8,128)(2,1)S(1)}, bf16[384,512]{1,0:T(8,128)(2,1)S(1)}, u32[]{:S(2)}, u32[]{:S(2)}) collective-permute-start(bf16[384,512]{1,0:T(8,128)(2,1)S(1)} %constant_dynamic-update-slice_fusion.6.refs_1_), channel_id=1, source_target_pairs={{0,1},{1,0},{2,3},{3,2},{4,5},{5,4},{6,7},{7,6},{8,9},{9,8},{10,11... | collective-permute-start | bytes 1179656 | tf_op jit(solution)/shard_map/ppermute | solution.py:97
  23.9 0.7 %copy-start.1 = (s32[128]{0:T(128)S(1)}, s32[128]{0:T(128)}, u32[]{:S(2)}) copy-start(s32[128]{0:T(128)} %param.4) | copy-start | bytes 1540
  23.9 3.6 %copy-start = (bf16[128,512]{1,0:T(8,128)(2,1)S(1)}, bf16[128,512]{1,0:T(8,128)(2,1)}, u32[]{:S(2)}) copy-start(bf16[128,512]{1,0:T(8,128)(2,1)} %own_ref.1) | copy-start | bytes 393220
  24.0 3.6 %collective-permute-start.9 = (bf16[448,512]{1,0:T(8,128)(2,1)S(1)}, bf16[448,512]{1,0:T(8,128)(2,1)S(1)}, u32[]{:S(2)}, u32[]{:S(2)}) collective-permute-start(bf16[448,512]{1,0:T(8,128)(2,1)S(1)} %constant_dynamic-update-slice_fusion.refs_0_), channel_id=1, source_target_pairs={{0,1},{1,0},{2,3},{3,2},{4,5},{5,4},{6,7},{7,6},{8,9},{9,8},{10,11... | collective-permute-start | bytes 1376264 | tf_op jit(solution)/shard_map/ppermute | solution.py:97
  24.6 0.7 %copy-start.2 = (s32[15]{0:T(128)S(1)}, s32[15]{0:T(128)}, u32[]{:S(2)}) copy-start(s32[15]{0:T(128)} %constant.69.clone) | copy-start | bytes 184
  26.2 1.3 %collective-permute-start.11 = (bf16[128,512]{1,0:T(8,128)(2,1)S(1)}, bf16[128,512]{1,0:T(8,128)(2,1)S(1)}, u32[]{:S(2)}, u32[]{:S(2)}) collective-permute-start(bf16[128,512]{1,0:T(8,128)(2,1)S(1)} %collective-permute-done.8.refs_2_), channel_id=1, source_target_pairs={{0,1},{1,0},{2,3},{3,2},{4,5},{5,4},{6,7},{7,6},{8,9},{9,8},{10,11... | collective-permute-start | bytes 393224 | tf_op jit(solution)/shard_map/ppermute | solution.py:97

commit v2 on v0

--- a/solution.py
+++ b/solution.py
@@ -1,14 +1,18 @@
+import functools
 import math
 
 import jax
 import jax.numpy as jnp
 from jax import lax
+from jax.experimental import pallas as pl
+from jax.experimental.pallas import tpu as pltpu
 from jax.sharding import PartitionSpec as P
 
 inv_temp = 10.0
-
-
-def on_device(feats, partner):
+log2e = 1.4426950408889634
+
+
+def split_plan(feats, partner):
     rows, width = feats.shape
     layers = lax.axis_size("rep")
     share = rows // layers
@@ -78,9 +82,284 @@
     return (grad, loss)
 
 
+X, Y, XY, Z1, Z2, Z3 = 1, 2, 3, 4, 8, 12
+
+
+def send(piece, first, second=None):
+    offsets = (first, first if second is None else second)
+    pairs = [
+        (2 * b + c, 2 * (b ^ offsets[c]) + c) for b in range(lax.axis_size("batch")) for c in range(2)
+    ]
+    return lax.ppermute(piece, ("batch", "rep"), pairs)
+
+
+def swap(piece):
+    return lax.ppermute(piece, "rep", [(0, 1), (1, 0)])
+
+
+def join(*pieces):
+    return jnp.concatenate(pieces, axis=0)
+
+
+class Chunk:
+    def __init__(self, offsets, parts=None):
+        self.offsets = offsets
+        self.parts = parts
+
+    def swapped(self):
+        return Chunk(self.offsets[::-1], self.parts and self.parts[::-1])
+
+
+def halves(first, second, *within):
+    return [Chunk((first ^ w, second ^ w), (0, 1)) for w in within]
+
+
+def whole(first, second):
+    return [Chunk((first, second))]
+
+
+def gather_rows(feats):
+    far = send(feats, Z2, Z3)
+    near = send(feats, X, Y)
+    cross = send(feats, XY, Z1)
+    side = send(near, Z1)
+    side_xy = send(cross, Z1, XY)
+    far_x, far_y = send(far, X, Y), send(far, Y, X)
+    far_xy = send(far, XY)
+
+    def both(piece, chunks):
+        return [(piece, chunks), (swap(piece), [chunk.swapped() for chunk in chunks])]
+
+    early = both(join(near, cross, far), whole(X, Y) + whole(XY, Z1) + whole(Z2, Z3))
+    middle = both(side, whole(X ^ Z1, Y ^ Z1))
+    late = both(join(far_x, far_y), whole(X ^ Z2, Y ^ Z3) + whole(Y ^ Z2, X ^ Z3))
+    last = both(far_xy, whole(XY ^ Z2, XY ^ Z3))
+    return [[(feats, whole(0, 0))] + early, middle + late + last + [(side_xy, whole(XY ^ Z1, XY ^ Z1))]]
+
+
+def normalized(raw):
+    hf = raw.astype(jnp.float32)
+    scale = lax.rsqrt(jnp.sum(hf * hf, axis=-1, keepdims=True) + 1e-06)
+    return hf * scale, scale
+
+
+def normalize_into(embed, refs):
+    start = 0
+    for ref in refs:
+        count = ref.shape[0]
+        for at in range(0, count, 64):
+            embed[start + at : start + at + 64, :] = normalized(ref[at : at + 64, :])[0].astype(jnp.bfloat16)
+        start += count
+
+
+def partner_column(partner_ref):
+    rows = partner_ref.shape[1]
+    spread = jnp.broadcast_to(partner_ref[...], (rows, rows)).astype(jnp.float32)
+    return jnp.sum(jnp.where(diagonal(rows), spread, 0.0), axis=1, keepdims=True).astype(jnp.int32)
+
+
+def diagonal(size):
+    r = lax.broadcasted_iota(jnp.int32, (size, size), 0)
+    c = lax.broadcasted_iota(jnp.int32, (size, size), 1)
+    return r == c
+
+
+def column_ids(chunks, rows):
+    layer = lax.axis_index("rep")
+    block = lax.axis_index("batch")
+    lane = lax.broadcasted_iota(jnp.int32, (1, rows), 1)
+    share = rows // 2
+
+    def base(chunk):
+        first = (block ^ jnp.where(layer == 0, *chunk.offsets)) * rows
+        return first if chunk.parts is None else first + jnp.where(layer == 0, *chunk.parts) * share
+
+    ids = []
+    waiting = []
+    for chunk in chunks:
+        if chunk.parts is None:
+            ids.append(lane + base(chunk))
+        else:
+            waiting.append(base(chunk))
+        if len(waiting) == 2:
+            ids.append(lane + jnp.where(lane < share, waiting[0], waiting[1] - share))
+            waiting = []
+    return ids
+
+
+def spans(total, block):
+    return [slice(start, min(start + block, total)) for start in range(0, total, block)]
+
+
+def shift(span, by):
+    return slice(span.start + by, span.stop + by)
+
+
+def weigh(left, right):
+    score = lax.dot_general(left, right, (((1,), (1,)), ((), ())), preferred_element_type=jnp.float32)
+    return score, jnp.exp2(score * (inv_temp * log2e))
+
+
+def fold_rows(weight):
+    return jnp.sum(weight.reshape(weight.shape[0] // 8, 8, weight.shape[1]), axis=0)
+
+
+def fold_columns(weight):
+    return sum(weight[:, k : k + 128] for k in range(0, weight.shape[1], 128))
+
+
+def triangle(embed, total, block, denom, top):
+    blocks = total // block
+    for i in range(blocks):
+        left = embed[i * block : (i + 1) * block, :]
+        row_sum = jnp.zeros((block, 128), jnp.float32)
+        for j in range(i, blocks):
+            score, weight = weigh(left, embed[j * block : (j + 1) * block, :])
+            if i == j:
+                weight = jnp.where(diagonal(block), 0.0, weight)
+            else:
+                row_sum += fold_columns(weight)
+            if i == 0:
+                top(j, score, weight)
+            denom[:, j * block : (j + 1) * block] += fold_rows(weight)
+        if i != blocks - 1:
+            denom[:, i * block : (i + 1) * block] += fold_rows(row_sum.T)
+
+
+def stage_kernel(chunks, final, partner_ref, own_ref, *refs):
+    before = chunks[:-1]
+    refs = list(refs)
+
+    def take(count):
+        taken = refs[:count]
+        del refs[:count]
+        return taken
+
+    old_embeds = take(len(before))
+    old_weights = take(len(before)) if final else []
+    old_denom, old_hits = take(2) if before else (None, None)
+    if final:
+        grad_ref, loss_ref, embed, weights, denom = refs[-5:]
+        pieces = refs[:-5]
+    else:
+        embed, weights, denom, hits_ref = refs[-4:]
+        pieces = refs[:-4]
+    rows, width = own_ref.shape
+    block = 2 * rows
+    new = embed.shape[0]
+    old = denom.shape[1] - new
+
+    normalize_into(embed, pieces)
+    mates = partner_column(partner_ref)
+    ids = [column_ids(part, rows) for part in chunks]
+    hits = old_hits[...] if before else jnp.zeros((rows, rows), jnp.float32)
+    if before:
+        denom[:, :old] = old_denom[...]
+    denom[:, old:] = jnp.zeros((8, new), jnp.float32)
+
+    def is_mate(names, span):
+        return [name == mates for name in names[span.start // rows : span.stop // rows]]
+
+    def found(span, score):
+        return sum(
+            jnp.where(mate, score[:rows, k * rows : (k + 1) * rows], 0.0)
+            for k, mate in enumerate(is_mate(ids[-1], span))
+        )
+
+    start = 0
+    for old_embed in old_embeds:
+        for i in spans(old_embed.shape[0], block):
+            left = old_embed[i, :]
+            row_sum = jnp.zeros((left.shape[0], 128), jnp.float32)
+            for j in spans(new, block):
+                score, weight = weigh(left, embed[j, :])
+                if start + i.start == 0:
+                    weights[:, j] = weight[:rows]
+                    hits += found(j, score)
+                row_sum += fold_columns(weight)
+                denom[:, shift(j, old)] += fold_rows(weight)
+            denom[:, shift(i, start)] += fold_rows(row_sum.T)
+        start += old_embed.shape[0]
+    for i in spans(new, block):
+        left = embed[i, :]
+        row_sum = jnp.zeros((left.shape[0], 128), jnp.float32)
+        for j in spans(new, block):
+            if j.start < i.start:
+                continue
+            score, weight = weigh(left, embed[j, :])
+            if i == j:
+                weight = jnp.where(diagonal(weight.shape[0]), 0.0, weight)
+            else:
+                row_sum += fold_columns(weight)
+            if not before and i.start == 0:
+                weights[:, j] = weight[:rows]
+                hits += found(j, score)
+            denom[:, shift(j, old)] += fold_rows(weight)
+        if i.stop != new:
+            denom[:, shift(i, old)] += fold_rows(row_sum.T)
+    if not final:
+        hits_ref[...] = hits
+        return
+
+    all_weights = [*old_weights, weights]
+    own = jnp.sum(sum(fold_columns(w[...]) for w in all_weights), axis=1, keepdims=True)
+    loss = jnp.log(own) - inv_temp * jnp.sum(hits, axis=1, keepdims=True)
+    loss_ref[...] = jnp.sum(jnp.where(diagonal(rows), loss, 0.0), axis=0, keepdims=True)
+    own_inverse = 1.0 / own
+    dz = jnp.zeros((rows, width), jnp.float32)
+    start = 0
+    for e, w, names in zip([*old_embeds, embed], all_weights, ids):
+        for j in spans(e.shape[0], block):
+            inverse = 1.0 / jnp.sum(denom[:, shift(j, start)], axis=0, keepdims=True)
+            mate = jnp.concatenate(is_mate(names, j), axis=1)
+            coeff = w[:, j] * (own_inverse + inverse) - jnp.where(mate, 2.0, 0.0)
+            dz += jnp.dot(coeff.astype(jnp.bfloat16), e[j, :], preferred_element_type=jnp.float32)
+        start += e.shape[0]
+    dz = dz * inv_temp
+    unit, scale = normalized(own_ref[...])
+    grad_ref[...] = scale * (dz - unit * jnp.sum(unit * dz, axis=-1, keepdims=True))
+
+
+def whole_plan(feats, partner):
+    rows, width = feats.shape
+    stages = gather_rows(feats)
+    mates = partner[None, :]
+    f32, bf16 = jnp.float32, jnp.bfloat16
+    vmem = pl.BlockSpec(memory_space=pltpu.VMEM)
+    chunks, embeds, weights, sums = [], [], [], []
+    done = 0
+    for s, stage in enumerate(stages):
+        if callable(stage):
+            stage = stage(sums)
+        pieces = [piece for piece, _ in stage]
+        chunks.append([chunk for _, part in stage for chunk in part])
+        new = sum(piece.shape[0] for piece in pieces)
+        state = [((new, width), bf16), ((rows, new), f32), ((8, done + new), f32)]
+        final = s == len(stages) - 1
+        outs = [((rows, width), f32), ((1, rows), f32)] if final else state + [((rows, rows), f32)]
+        operands = [mates, feats, *embeds, *(weights if final else []), *sums, *pieces]
+        results = pl.pallas_call(
+            functools.partial(stage_kernel, list(chunks), final),
+            out_shape=tuple(jax.ShapeDtypeStruct(shape, dtype) for shape, dtype in outs),
+            in_specs=[vmem] * len(operands),
+            out_specs=(vmem,) * len(outs),
+            scratch_shapes=[pltpu.VMEM(shape, dtype) for shape, dtype in (state if final else [])],
+            cost_estimate=pl.CostEstimate(flops=new * (2 * done + new) * width, bytes_accessed=0, transcendentals=0),
+            compiler_params=pltpu.CompilerParams(vmem_limit_bytes=32 * 1024 * 1024),
+        )(*operands)
+        if not final:
+            embeds.append(results[0])
+            weights.append(results[1])
+            sums = list(results[2:])
+        done += new
+    grad, loss = results
+    return grad, loss.reshape(rows)
+
+
 def solution(mesh):
+    every = mesh.shape["batch"] == 16 and mesh.shape["rep"] == 2
     in_specs = (P("batch", None), P("batch"))
     out_specs = (P("batch", None), P("batch"))
     return jax.shard_map(
-        on_device, mesh=mesh, in_specs=in_specs, out_specs=out_specs, check_vma=False
+        whole_plan if every else split_plan, mesh=mesh, in_specs=in_specs, out_specs=out_specs, check_vma=False
     )

time: 139 us -> 28.9 us (0.21)
  the two profiles are of different devices: /device:TPU:0 before, /device:TPU:5 now
where the time goes in v2:
time: 28.9 us; the launch traced here: 28.7 us
  starting transfers between devices  16.4 us (57%)
  waiting for transfers between devices  6.51 us (23%)
  Pallas kernels  5.09 us (18%)
  between operations  0.7 us (2%)
    ppermute x4, starting transfers between devices, swap(): return lax.ppermute(piece, 'rep', [(0, 1), (1, 0)])  10.1 us
    ppermute x8, waiting for transfers between devices, send(): return lax.ppermute(piece, ('batch', 'rep'), pairs)  6.5 us
    ppermute x8, starting transfers between devices, send(): return lax.ppermute(piece, ('batch', 'rep'), pairs)  6.28 us
    pallas_call x2, Pallas kernels, whole_plan(): pl.pallas_call(functools.partial(stage_kernel, list(chunks), final), out_...  5.09 us
  transfers between devices with their start and end apart: 12, of which 3 were waited for; matrix products, arithmetic and copies ran while one was open for 0% of the time, Pallas kernels for 4%

profile of v2, /device:TPU:5, one launch (start us, length us, event | category | flops | bytes accessed | tf_op | source)
XLA Modules:
  0.0 28.7 jit_solution(78079071704336467)
XLA Ops:
  0.6 3.4 %collective-permute-start.2 = (bf16[128,512]{1,0:T(8,128)(2,1)}, bf16[128,512]{1,0:T(8,128)(2,1)S(1)}, u32[]{:S(2)}, u32[]{:S(2)}) collective-permute-start(bf16[128,512]{1,0:T(8,128)(2,1)} %own_ref.3), channel_id=1, source_target_pairs={{0,16},{1,25},{2,18},{3,27},{4,20},{5,29},{6,22},{7,31},{8,24},{9,... | collective-permute-start | bytes 393224 | tf_op jit(solution)/shard_map/ppermute | solution.py:93
  4.0 0.2 collective-permute-start
  4.2 0.0 collective-permute-start.1
  4.2 3.3 %collective-permute-done.2 = bf16[128,512]{1,0:T(8,128)(2,1)S(1)} collective-permute-done((bf16[128,512]{1,0:T(8,128)(2,1)}, bf16[128,512]{1,0:T(8,128)(2,1)S(1)}, u32[]{:S(2)}, u32[]{:S(2)}) %collective-permute-start.2) | collective-permute-done | bytes 131104 | tf_op jit(solution)/shard_map/ppermute | solution.py:93
  7.6 0.2 collective-permute-start.6
  7.8 1.2 %collective-permute-start.7 = (bf16[128,512]{1,0:T(8,128)(2,1)S(1)}, bf16[128,512]{1,0:T(8,128)(2,1)S(1)}, u32[]{:S(2)}, u32[]{:S(2)}) collective-permute-start(bf16[128,512]{1,0:T(8,128)(2,1)S(1)} %collective-permute-done.2), channel_id=1, source_target_pairs={{0,4},{1,3},{2,6},{3,1},{4,0},{5,7},{6,2},{7,5},{8,12},{9,11},{10,... | collective-permute-start | bytes 393224 | tf_op jit(solution)/shard_map/ppermute | solution.py:93
  9.0 0.0 collective-permute-done
  9.0 0.1 collective-permute-done.1
  9.1 3.7 %collective-permute-start.3 = (bf16[384,512]{1,0:T(8,128)(2,1)S(1)}, bf16[384,512]{1,0:T(8,128)(2,1)S(1)}, u32[]{:S(2)}, u32[]{:S(2)}) collective-permute-start(bf16[384,512]{1,0:T(8,128)(2,1)S(1)} %constant_dynamic-update-slice_fusion.refs_1_), channel_id=1, source_target_pairs={{0,1},{1,0},{2,3},{3,2},{4,5},{5,4},{6,7},{7,6},{8,9},{9,8},{10,11... | collective-permute-start | bytes 1179656 | tf_op jit(solution)/shard_map/ppermute | solution.py:97
  12.9 1.1 %collective-permute-start.9 = (bf16[128,512]{1,0:T(8,128)(2,1)S(1)}, bf16[128,512]{1,0:T(8,128)(2,1)S(1)}, u32[]{:S(2)}, u32[]{:S(2)}) collective-permute-start(bf16[128,512]{1,0:T(8,128)(2,1)S(1)} %collective-permute-done.2), channel_id=1, source_target_pairs={{0,6},{1,7},{2,4},{3,5},{4,2},{5,3},{6,0},{7,1},{8,14},{9,15},{10,... | collective-permute-start | bytes 393224 | tf_op jit(solution)/shard_map/ppermute | solution.py:93
  14.0 0.1 collective-permute-start.4
  14.1 0.0 collective-permute-done.6
  14.1 0.0 copy-start
  14.1 0.0 collective-permute-done.7
  14.2 0.0 copy-start.1
  14.2 5.8 %collective-permute-start.8 = (bf16[256,512]{1,0:T(8,128)(2,1)S(1)}, bf16[256,512]{1,0:T(8,128)(2,1)S(1)}, u32[]{:S(2)}, u32[]{:S(2)}) collective-permute-start(bf16[256,512]{1,0:T(8,128)(2,1)S(1)} %constant_dynamic-update-slice_fusion.3.refs_6_), channel_id=1, source_target_pairs={{0,1},{1,0},{2,3},{3,2},{4,5},{5,4},{6,7},{7,6},{8,9},{9,8},{10,11... | collective-permute-start | bytes 786440 | tf_op jit(solution)/shard_map/ppermute | solution.py:97
  20.0 0.0 collective-permute-start.11
  20.0 0.0 collective-permute-done.9.refs_8_
  20.0 0.3 %collective-permute-start.10 = (bf16[128,512]{1,0:T(8,128)(2,1)S(1)}, bf16[128,512]{1,0:T(8,128)(2,1)S(1)}, u32[]{:S(2)}, u32[]{:S(2)}) collective-permute-start(bf16[128,512]{1,0:T(8,128)(2,1)S(1)} %collective-permute-done.9.refs_8_), channel_id=1, source_target_pairs={{0,1},{1,0},{2,3},{3,2},{4,5},{5,4},{6,7},{7,6},{8,9},{9,8},{10,11... | collective-permute-start | bytes 393224 | tf_op jit(solution)/shard_map/ppermute | solution.py:97
  20.4 0.0 collective-permute-done.4.refs_4_
  20.4 0.2 collective-permute-start.5
  20.5 0.0 collective-permute-done.3.refs_2_
  20.5 0.0 copy-done
  20.5 0.0 copy-done.1
  20.5 1.1 %shard_map.41 = (bf16[896,512]{1,0:T(8,128)(2,1)S(1)}, f32[128,896]{1,0:T(8,128)S(1)}, f32[8,896]{1,0:T(8,128)S(1)}, f32[128,128]{1,0:T(8,128)S(1)}) custom-call(s32[1,128]{1,0:T(1,128)S(1)} %bitcast.2, bf16[128,512]{1,0:T(8,128)(2,1)S(1)} %copy-done, bf16[128,512]{1,0:T(8,128)(2,1)S(1)} %copy-done, ...), custom_call_target="tpu_custom_call" | custom-call | flops 411041792 | tf_op jit(solution)/shard_map/pallas_call | solution.py:341
  21.6 3.1 %collective-permute-done.11.refs_10_ = bf16[128,512]{1,0:T(8,128)(2,1)S(1)} collective-permute-done((bf16[128,512]{1,0:T(8,128)(2,1)S(1)}, bf16[128,512]{1,0:T(8,128)(2,1)S(1)}, u32[]{:S(2)}, u32[]{:S(2)}) %collective-permute-start.11) | collective-permute-done | bytes 131104 | tf_op jit(solution)/shard_map/ppermute | solution.py:93
  24.7 0.0 collective-permute-done.10.refs_9_
  24.7 0.0 collective-permute-done.5.refs_5_
  24.7 0.0 collective-permute-done.8.refs_7_
  24.7 4.0 %shard_map.42 = (f32[128,512]{1,0:T(8,128)}, f32[1,128]{1,0:T(1,128)}) custom-call(s32[1,128]{1,0:T(1,128)S(1)} %bitcast.3, bf16[128,512]{1,0:T(8,128)(2,1)S(1)} %copy-done, bf16[896,512]{1,0:T(8,128)(2,1)S(1)} %get-tuple-element.8.refs_0_, f32[128,896]{1,0:T(8,128)S(1)} %get-tuple-element.9.refs_1_, f32[8,896]{1,0:T(8,128)S(1)} %get-tuple-element.10.refs_2_, ...), custom_call_target="tpu_custom_call" | custom-call | flops 1736441856 | tf_op jit(solution)/shard_map/pallas_call | solution.py:341
  (5 shorter events, 0.1 us)
Async XLA Ops:
  0.6 6.9 %collective-permute-start.2 = (bf16[128,512]{1,0:T(8,128)(2,1)}, bf16[128,512]{1,0:T(8,128)(2,1)S(1)}, u32[]{:S(2)}, u32[]{:S(2)}) collective-permute-start(bf16[128,512]{1,0:T(8,128)(2,1)} %own_ref.3), channel_id=1, source_target_pairs={{0,16},{1,25},{2,18},{3,27},{4,20},{5,29},{6,22},{7,31},{8,24},{9,... | collective-permute-start | bytes 393224 | tf_op jit(solution)/shard_map/ppermute | solution.py:93
  4.0 5.0 %collective-permute-start = (bf16[128,512]{1,0:T(8,128)(2,1)}, bf16[128,512]{1,0:T(8,128)(2,1)S(1)}, u32[]{:S(2)}, u32[]{:S(2)}) collective-permute-start(bf16[128,512]{1,0:T(8,128)(2,1)} %own_ref.3), channel_id=1, source_target_pairs={{0,2},{1,5},{2,0},{3,7},{4,6},{5,1},{6,4},{7,3},{8,10},{9,13},{10,... | collective-permute-start | bytes 393224 | tf_op jit(solution)/shard_map/ppermute | solution.py:93
  4.2 4.9 %collective-permute-start.1 = (bf16[128,512]{1,0:T(8,128)(2,1)}, bf16[128,512]{1,0:T(8,128)(2,1)S(1)}, u32[]{:S(2)}, u32[]{:S(2)}) collective-permute-start(bf16[128,512]{1,0:T(8,128)(2,1)} %own_ref.3), channel_id=1, source_target_pairs={{0,6},{1,9},{2,4},{3,11},{4,2},{5,13},{6,0},{7,15},{8,14},{9,1},{1... | collective-permute-start | bytes 393224 | tf_op jit(solution)/shard_map/ppermute | solution.py:93
  7.6 6.5 %collective-permute-start.6 = (bf16[128,512]{1,0:T(8,128)(2,1)S(1)}, bf16[128,512]{1,0:T(8,128)(2,1)S(1)}, u32[]{:S(2)}, u32[]{:S(2)}) collective-permute-start(bf16[128,512]{1,0:T(8,128)(2,1)S(1)} %collective-permute-done.2), channel_id=1, source_target_pairs={{0,2},{1,5},{2,0},{3,7},{4,6},{5,1},{6,4},{7,3},{8,10},{9,13},{10,... | collective-permute-start | bytes 393224 | tf_op jit(solution)/shard_map/ppermute | solution.py:93
  7.8 6.3 %collective-permute-start.7 = (bf16[128,512]{1,0:T(8,128)(2,1)S(1)}, bf16[128,512]{1,0:T(8,128)(2,1)S(1)}, u32[]{:S(2)}, u32[]{:S(2)}) collective-permute-start(bf16[128,512]{1,0:T(8,128)(2,1)S(1)} %collective-permute-done.2), channel_id=1, source_target_pairs={{0,4},{1,3},{2,6},{3,1},{4,0},{5,7},{6,2},{7,5},{8,12},{9,11},{10,... | collective-permute-start | bytes 393224 | tf_op jit(solution)/shard_map/ppermute | solution.py:93
  9.1 11.4 %collective-permute-start.3 = (bf16[384,512]{1,0:T(8,128)(2,1)S(1)}, bf16[384,512]{1,0:T(8,128)(2,1)S(1)}, u32[]{:S(2)}, u32[]{:S(2)}) collective-permute-start(bf16[384,512]{1,0:T(8,128)(2,1)S(1)} %constant_dynamic-update-slice_fusion.refs_1_), channel_id=1, source_target_pairs={{0,1},{1,0},{2,3},{3,2},{4,5},{5,4},{6,7},{7,6},{8,9},{9,8},{10,11... | collective-permute-start | bytes 1179656 | tf_op jit(solution)/shard_map/ppermute | solution.py:97
  12.9 7.1 %collective-permute-start.9 = (bf16[128,512]{1,0:T(8,128)(2,1)S(1)}, bf16[128,512]{1,0:T(8,128)(2,1)S(1)}, u32[]{:S(2)}, u32[]{:S(2)}) collective-permute-start(bf16[128,512]{1,0:T(8,128)(2,1)S(1)} %collective-permute-done.2), channel_id=1, source_target_pairs={{0,6},{1,7},{2,4},{3,5},{4,2},{5,3},{6,0},{7,1},{8,14},{9,15},{10,... | collective-permute-start | bytes 393224 | tf_op jit(solution)/shard_map/ppermute | solution.py:93
  14.0 6.4 %collective-permute-start.4 = (bf16[128,512]{1,0:T(8,128)(2,1)S(1)}, bf16[128,512]{1,0:T(8,128)(2,1)S(1)}, u32[]{:S(2)}, u32[]{:S(2)}) collective-permute-start(bf16[128,512]{1,0:T(8,128)(2,1)S(1)} %collective-permute-done), channel_id=1, source_target_pairs={{0,8},{1,9},{2,10},{3,11},{4,12},{5,13},{6,14},{7,15},{8,0},{9,1},... | collective-permute-start | bytes 393224 | tf_op jit(solution)/shard_map/ppermute | solution.py:93
  14.1 6.4 %copy-start = (bf16[128,512]{1,0:T(8,128)(2,1)S(1)}, bf16[128,512]{1,0:T(8,128)(2,1)}, u32[]{:S(2)}) copy-start(bf16[128,512]{1,0:T(8,128)(2,1)} %own_ref.3) | copy-start | bytes 393220
  14.2 6.4 %copy-start.1 = (s32[128]{0:T(128)S(1)}, s32[128]{0:T(128)}, u32[]{:S(2)}) copy-start(s32[128]{0:T(128)} %param.3) | copy-start | bytes 1540
  14.2 10.6 %collective-permute-start.8 = (bf16[256,512]{1,0:T(8,128)(2,1)S(1)}, bf16[256,512]{1,0:T(8,128)(2,1)S(1)}, u32[]{:S(2)}, u32[]{:S(2)}) collective-permute-start(bf16[256,512]{1,0:T(8,128)(2,1)S(1)} %constant_dynamic-update-slice_fusion.3.refs_6_), channel_id=1, source_target_pairs={{0,1},{1,0},{2,3},{3,2},{4,5},{5,4},{6,7},{7,6},{8,9},{9,8},{10,11... | collective-permute-start | bytes 786440 | tf_op jit(solution)/shard_map/ppermute | solution.py:97
  20.0 4.7 %collective-permute-start.11 = (bf16[128,512]{1,0:T(8,128)(2,1)S(1)}, bf16[128,512]{1,0:T(8,128)(2,1)S(1)}, u32[]{:S(2)}, u32[]{:S(2)}) collective-permute-start(bf16[128,512]{1,0:T(8,128)(2,1)S(1)} %collective-permute-done.1), channel_id=1, source_target_pairs={{0,8},{1,7},{2,10},{3,5},{4,12},{5,3},{6,14},{7,1},{8,0},{9,15},{1... | collective-permute-start | bytes 393224 | tf_op jit(solution)/shard_map/ppermute | solution.py:93
  20.0 4.7 %collective-permute-start.10 = (bf16[128,512]{1,0:T(8,128)(2,1)S(1)}, bf16[128,512]{1,0:T(8,128)(2,1)S(1)}, u32[]{:S(2)}, u32[]{:S(2)}) collective-permute-start(bf16[128,512]{1,0:T(8,128)(2,1)S(1)} %collective-permute-done.9.refs_8_), channel_id=1, source_target_pairs={{0,1},{1,0},{2,3},{3,2},{4,5},{5,4},{6,7},{7,6},{8,9},{9,8},{10,11... | collective-permute-start | bytes 393224 | tf_op jit(solution)/shard_map/ppermute | solution.py:97
  20.4 4.4 %collective-permute-start.5 = (bf16[128,512]{1,0:T(8,128)(2,1)S(1)}, bf16[128,512]{1,0:T(8,128)(2,1)S(1)}, u32[]{:S(2)}, u32[]{:S(2)}) collective-permute-start(bf16[128,512]{1,0:T(8,128)(2,1)S(1)} %collective-permute-done.4.refs_4_), channel_id=1, source_target_pairs={{0,1},{1,0},{2,3},{3,2},{4,5},{5,4},{6,7},{7,6},{8,9},{9,8},{10,11... | collective-permute-start | bytes 393224 | tf_op jit(solution)/shard_map/ppermute | solution.py:97

commit v3 on v2

--- a/solution.py
+++ b/solution.py
@@ -125,16 +125,27 @@
     side = send(near, Z1)
     side_xy = send(cross, Z1, XY)
     far_x, far_y = send(far, X, Y), send(far, Y, X)
-    far_xy = send(far, XY)
+    far_xy = send(far_x, Y, X)
 
     def both(piece, chunks):
         return [(piece, chunks), (swap(piece), [chunk.swapped() for chunk in chunks])]
 
+    def split(piece, first, second):
+        share = piece.shape[0] // 2
+        halves = [(swap(piece[k * share : (k + 1) * share]), [Chunk((second, first), (k, k))]) for k in range(2)]
+        return [(piece, whole(first, second))] + halves
+
     early = both(join(near, cross, far), whole(X, Y) + whole(XY, Z1) + whole(Z2, Z3))
-    middle = both(side, whole(X ^ Z1, Y ^ Z1))
-    late = both(join(far_x, far_y), whole(X ^ Z2, Y ^ Z3) + whole(Y ^ Z2, X ^ Z3))
-    last = both(far_xy, whole(XY ^ Z2, XY ^ Z3))
-    return [[(feats, whole(0, 0))] + early, middle + late + last + [(side_xy, whole(XY ^ Z1, XY ^ Z1))]]
+
+    def late():
+        return both(join(far_x, far_y), whole(X ^ Z2, Y ^ Z3) + whole(Y ^ Z2, X ^ Z3))
+
+    def last(sums):
+        g, s, sx, hits = lax.optimization_barrier((far_xy, side, side_xy, sums[1]))
+        sums = [sums[0], hits]
+        return late() + both(s, whole(X ^ Z1, Y ^ Z1)) + both(g, whole(XY ^ Z2, XY ^ Z3)) + [(sx, whole(XY ^ Z1, XY ^ Z1))], sums
+
+    return [[(feats, whole(0, 0))] + early, last]
 
 
 def normalized(raw):
@@ -174,17 +185,16 @@
         first = (block ^ jnp.where(layer == 0, *chunk.offsets)) * rows
         return first if chunk.parts is None else first + jnp.where(layer == 0, *chunk.parts) * share
 
-    ids = []
-    waiting = []
+    groups = {}
+    start = 0
     for chunk in chunks:
-        if chunk.parts is None:
-            ids.append(lane + base(chunk))
-        else:
-            waiting.append(base(chunk))
-        if len(waiting) == 2:
-            ids.append(lane + jnp.where(lane < share, waiting[0], waiting[1] - share))
-            waiting = []
-    return ids
+        stop = start + (rows if chunk.parts is None else share)
+        for group in range(start // rows, (stop - 1) // rows + 1):
+            value = lane + (base(chunk) + group * rows - start)
+            before = groups.get(group)
+            groups[group] = value if before is None else jnp.where(lane < start - group * rows, before, value)
+        start = stop
+    return [groups[group] for group in range(start // rows)]
 
 
 def spans(total, block):
@@ -268,7 +278,7 @@
 
     start = 0
     for old_embed in old_embeds:
-        for i in spans(old_embed.shape[0], block):
+        for i in spans(old_embed.shape[0], 2 * block):
             left = old_embed[i, :]
             row_sum = jnp.zeros((left.shape[0], 128), jnp.float32)
             for j in spans(new, block):
@@ -326,11 +336,11 @@
     mates = partner[None, :]
     f32, bf16 = jnp.float32, jnp.bfloat16
     vmem = pl.BlockSpec(memory_space=pltpu.VMEM)
-    chunks, embeds, weights, sums = [], [], [], []
+    chunks, embeds, weights, sums, states = [], [], [], [], []
     done = 0
     for s, stage in enumerate(stages):
         if callable(stage):
-            stage = stage(sums)
+            stage, sums = stage(sums)
         pieces = [piece for piece, _ in stage]
         chunks.append([chunk for _, part in stage for chunk in part])
         new = sum(piece.shape[0] for piece in pieces)
@@ -344,13 +354,14 @@
             in_specs=[vmem] * len(operands),
             out_specs=(vmem,) * len(outs),
             scratch_shapes=[pltpu.VMEM(shape, dtype) for shape, dtype in (state if final else [])],
-            cost_estimate=pl.CostEstimate(flops=new * (2 * done + new) * width, bytes_accessed=0, transcendentals=0),
+            cost_estimate=pl.CostEstimate(flops=1000, bytes_accessed=0, transcendentals=0),
             compiler_params=pltpu.CompilerParams(vmem_limit_bytes=32 * 1024 * 1024),
         )(*operands)
         if not final:
             embeds.append(results[0])
             weights.append(results[1])
             sums = list(results[2:])
+            states.append(sums)
         done += new
     grad, loss = results
     return grad, loss.reshape(rows)

time: 28.9 us -> 27.1 us (0.938)
  the two profiles are of different devices: /device:TPU:5 before, /device:TPU:0 now
where the time goes in v3:
time: 27.1 us; the launch traced here: 27 us
  starting transfers between devices  14.1 us (52%)
  waiting for transfers between devices  6.52 us (24%)
  Pallas kernels  4.78 us (18%)
  local copies, waits for them, and re-layouts  0.8 us (3%)
  between operations  0.72 us (3%)
    ppermute x8, starting transfers between devices, send(): return lax.ppermute(piece, ('batch', 'rep'), pairs)  13.5 us
    ppermute x8, waiting for transfers between devices, send(): return lax.ppermute(piece, ('batch', 'rep'), pairs)  5.49 us
    pallas_call x2, Pallas kernels, whole_plan(): pl.pallas_call(functools.partial(stage_kernel, list(chunks), final), out_...  4.78 us
    ppermute x4, waiting for transfers between devices, swap(): return lax.ppermute(piece, 'rep', [(0, 1), (1, 0)])  1.03 us
    unnamed x7, local copies, waits for them, and re-layouts  0.78 us
    ppermute x4, starting transfers between devices, swap(): return lax.ppermute(piece, 'rep', [(0, 1), (1, 0)])  0.65 us
  transfers between devices with their start and end apart: 12, of which 5 were waited for; matrix products, arithmetic and copies ran while one was open for 0% of the time, Pallas kernels for 4%

profile of v3, /device:TPU:0, one launch (start us, length us, event | category | flops | bytes accessed | tf_op | source)
XLA Modules:
  0.0 27.0 jit_solution(17751610902134823685)
XLA Ops:
  0.6 4.1 %collective-permute-start.2 = (bf16[128,512]{1,0:T(8,128)(2,1)}, bf16[128,512]{1,0:T(8,128)(2,1)S(1)}, u32[]{:S(2)}, u32[]{:S(2)}) collective-permute-start(bf16[128,512]{1,0:T(8,128)(2,1)} %own_ref.3), channel_id=1, source_target_pairs={{0,16},{1,25},{2,18},{3,27},{4,20},{5,29},{6,22},{7,31},{8,24},{9,... | collective-permute-start | bytes 393224 | tf_op jit(solution)/shard_map/ppermute | solution.py:93
  4.7 1.5 %collective-permute-start = (bf16[128,512]{1,0:T(8,128)(2,1)}, bf16[128,512]{1,0:T(8,128)(2,1)S(1)}, u32[]{:S(2)}, u32[]{:S(2)}) collective-permute-start(bf16[128,512]{1,0:T(8,128)(2,1)} %own_ref.3), channel_id=1, source_target_pairs={{0,2},{1,5},{2,0},{3,7},{4,6},{5,1},{6,4},{7,3},{8,10},{9,13},{10,... | collective-permute-start | bytes 393224 | tf_op jit(solution)/shard_map/ppermute | solution.py:93
  6.2 1.5 %collective-permute-start.1 = (bf16[128,512]{1,0:T(8,128)(2,1)}, bf16[128,512]{1,0:T(8,128)(2,1)S(1)}, u32[]{:S(2)}, u32[]{:S(2)}) collective-permute-start(bf16[128,512]{1,0:T(8,128)(2,1)} %own_ref.3), channel_id=1, source_target_pairs={{0,6},{1,9},{2,4},{3,11},{4,2},{5,13},{6,0},{7,15},{8,14},{9,1},{1... | collective-permute-start | bytes 393224 | tf_op jit(solution)/shard_map/ppermute | solution.py:93
  7.7 3.8 %collective-permute-done.2 = bf16[128,512]{1,0:T(8,128)(2,1)S(1)} collective-permute-done((bf16[128,512]{1,0:T(8,128)(2,1)}, bf16[128,512]{1,0:T(8,128)(2,1)S(1)}, u32[]{:S(2)}, u32[]{:S(2)}) %collective-permute-start.2) | collective-permute-done | bytes 131104 | tf_op jit(solution)/shard_map/ppermute | solution.py:93
  11.5 1.5 %collective-permute-start.4 = (bf16[128,512]{1,0:T(8,128)(2,1)S(1)}, bf16[128,512]{1,0:T(8,128)(2,1)S(1)}, u32[]{:S(2)}, u32[]{:S(2)}) collective-permute-start(bf16[128,512]{1,0:T(8,128)(2,1)S(1)} %collective-permute-done.2), channel_id=1, source_target_pairs={{0,2},{1,5},{2,0},{3,7},{4,6},{5,1},{6,4},{7,3},{8,10},{9,13},{10,... | collective-permute-start | bytes 393224 | tf_op jit(solution)/shard_map/ppermute | solution.py:93
  13.0 0.0 collective-permute-done
  13.0 0.0 collective-permute-done.1
  13.1 0.1 collective-permute-start.3
  13.2 1.5 %collective-permute-start.8 = (bf16[128,512]{1,0:T(8,128)(2,1)S(1)}, bf16[128,512]{1,0:T(8,128)(2,1)S(1)}, u32[]{:S(2)}, u32[]{:S(2)}) collective-permute-start(bf16[128,512]{1,0:T(8,128)(2,1)S(1)} %collective-permute-done.2), channel_id=1, source_target_pairs={{0,4},{1,3},{2,6},{3,1},{4,0},{5,7},{6,2},{7,5},{8,12},{9,11},{10,... | collective-permute-start | bytes 393224 | tf_op jit(solution)/shard_map/ppermute | solution.py:93
  14.6 1.0 %collective-permute-start.6 = (bf16[128,512]{1,0:T(8,128)(2,1)S(1)}, bf16[128,512]{1,0:T(8,128)(2,1)S(1)}, u32[]{:S(2)}, u32[]{:S(2)}) collective-permute-start(bf16[128,512]{1,0:T(8,128)(2,1)S(1)} %collective-permute-done), channel_id=1, source_target_pairs={{0,8},{1,9},{2,10},{3,11},{4,12},{5,13},{6,14},{7,15},{8,0},{9,1},... | collective-permute-start | bytes 393224 | tf_op jit(solution)/shard_map/ppermute | solution.py:93
  15.6 1.1 %collective-permute-start.7 = (bf16[128,512]{1,0:T(8,128)(2,1)S(1)}, bf16[128,512]{1,0:T(8,128)(2,1)S(1)}, u32[]{:S(2)}, u32[]{:S(2)}) collective-permute-start(bf16[128,512]{1,0:T(8,128)(2,1)S(1)} %collective-permute-done.1), channel_id=1, source_target_pairs={{0,8},{1,7},{2,10},{3,5},{4,12},{5,3},{6,14},{7,1},{8,0},{9,15},{1... | collective-permute-start | bytes 393224 | tf_op jit(solution)/shard_map/ppermute | solution.py:93
  16.7 0.0 collective-permute-done.4
  16.7 1.4 %collective-permute-start.5 = (bf16[128,512]{1,0:T(8,128)(2,1)S(1)}, bf16[128,512]{1,0:T(8,128)(2,1)S(1)}, u32[]{:S(2)}, u32[]{:S(2)}) collective-permute-start(bf16[128,512]{1,0:T(8,128)(2,1)S(1)} %collective-permute-done.4), channel_id=1, source_target_pairs={{0,4},{1,3},{2,6},{3,1},{4,0},{5,7},{6,2},{7,5},{8,12},{9,11},{10,... | collective-permute-start | bytes 393224 | tf_op jit(solution)/shard_map/ppermute | solution.py:93
  18.1 0.0 copy-start
  18.1 0.0 collective-permute-done.8
  18.2 0.0 copy-start.1
  18.2 0.1 collective-permute-start.9
  18.3 0.0 collective-permute-done.3.refs_2_
  18.3 0.7 %copy-done = bf16[128,512]{1,0:T(8,128)(2,1)S(1)} copy-done((bf16[128,512]{1,0:T(8,128)(2,1)S(1)}, bf16[128,512]{1,0:T(8,128)(2,1)}, u32[]{:S(2)}) %copy-start) | copy-done | bytes 131096
  19.0 0.0 copy-done.1
  19.0 1.1 %shard_map.41 = (bf16[896,512]{1,0:T(8,128)(2,1)S(1)}, f32[128,896]{1,0:T(8,128)S(1)}, f32[8,896]{1,0:T(8,128)S(1)}, f32[128,128]{1,0:T(8,128)S(1)}) custom-call(s32[1,128]{1,0:T(1,128)S(1)} %bitcast.2, bf16[128,512]{1,0:T(8,128)(2,1)S(1)} %copy-done, bf16[128,512]{1,0:T(8,128)(2,1)S(1)} %copy-done, ...), custom_call_target="tpu_custom_call" | custom-call | flops 1000 | tf_op jit(solution)/shard_map/pallas_call | solution.py:351
  20.1 0.0 collective-permute-done.6.refs_6_
  20.1 0.9 %collective-permute-done.7.refs_10_ = bf16[128,512]{1,0:T(8,128)(2,1)S(1)} collective-permute-done((bf16[128,512]{1,0:T(8,128)(2,1)S(1)}, bf16[128,512]{1,0:T(8,128)(2,1)S(1)}, u32[]{:S(2)}, u32[]{:S(2)}) %collective-permute-start.7) | collective-permute-done | bytes 131104 | tf_op jit(solution)/shard_map/ppermute | solution.py:93
  21.0 0.7 %collective-permute-done.5.refs_8_ = bf16[128,512]{1,0:T(8,128)(2,1)S(1)} collective-permute-done((bf16[128,512]{1,0:T(8,128)(2,1)S(1)}, bf16[128,512]{1,0:T(8,128)(2,1)S(1)}, u32[]{:S(2)}, u32[]{:S(2)}) %collective-permute-start.5) | collective-permute-done | bytes 131104 | tf_op jit(solution)/shard_map/ppermute | solution.py:93
  21.7 0.0 collective-permute-start.10
  21.7 0.5 %collective-permute-start.11 = (bf16[128,512]{1,0:T(8,128)(2,1)S(1)}, bf16[128,512]{1,0:T(8,128)(2,1)S(1)}, u32[]{:S(2)}, u32[]{:S(2)}) collective-permute-start(bf16[128,512]{1,0:T(8,128)(2,1)S(1)} %collective-permute-done.5.refs_8_), channel_id=1, source_target_pairs={{0,1},{1,0},{2,3},{3,2},{4,5},{5,4},{6,7},{7,6},{8,9},{9,8},{10,11... | collective-permute-start | bytes 393224 | tf_op jit(solution)/shard_map/ppermute | solution.py:97
  22.2 0.0 collective-permute-done.9.refs_5_
  22.2 0.8 %collective-permute-done.10.refs_7_ = bf16[128,512]{1,0:T(8,128)(2,1)S(1)} collective-permute-done((bf16[128,512]{1,0:T(8,128)(2,1)S(1)}, bf16[128,512]{1,0:T(8,128)(2,1)S(1)}, u32[]{:S(2)}, u32[]{:S(2)}) %collective-permute-start.10) | collective-permute-done | bytes 131104 | tf_op jit(solution)/shard_map/ppermute | solution.py:97
  23.1 0.2 collective-permute-done.11.refs_9_
  23.3 3.7 %shard_map.42 = (f32[128,512]{1,0:T(8,128)}, f32[1,128]{1,0:T(1,128)}) custom-call(s32[1,128]{1,0:T(1,128)S(1)} %bitcast.3, bf16[128,512]{1,0:T(8,128)(2,1)S(1)} %copy-done, bf16[896,512]{1,0:T(8,128)(2,1)S(1)} %get-tuple-element.12.refs_0_, f32[128,896]{1,0:T(8,128)S(1)} %get-tuple-element.13.refs_1_, f32[8,896]{1,0:T(8,128)S(1)} %get-tuple-element.14.refs_2_, ...), custom_call_target="tpu_custom_call" | custom-call | flops 1000 | tf_op jit(solution)/shard_map/pallas_call | solution.py:351
  (5 shorter events, 0.1 us)
Async XLA Ops:
  0.6 10.9 %collective-permute-start.2 = (bf16[128,512]{1,0:T(8,128)(2,1)}, bf16[128,512]{1,0:T(8,128)(2,1)S(1)}, u32[]{:S(2)}, u32[]{:S(2)}) collective-permute-start(bf16[128,512]{1,0:T(8,128)(2,1)} %own_ref.3), channel_id=1, source_target_pairs={{0,16},{1,25},{2,18},{3,27},{4,20},{5,29},{6,22},{7,31},{8,24},{9,... | collective-permute-start | bytes 393224 | tf_op jit(solution)/shard_map/ppermute | solution.py:93
  4.7 8.3 %collective-permute-start = (bf16[128,512]{1,0:T(8,128)(2,1)}, bf16[128,512]{1,0:T(8,128)(2,1)S(1)}, u32[]{:S(2)}, u32[]{:S(2)}) collective-permute-start(bf16[128,512]{1,0:T(8,128)(2,1)} %own_ref.3), channel_id=1, source_target_pairs={{0,2},{1,5},{2,0},{3,7},{4,6},{5,1},{6,4},{7,3},{8,10},{9,13},{10,... | collective-permute-start | bytes 393224 | tf_op jit(solution)/shard_map/ppermute | solution.py:93
  6.2 6.8 %collective-permute-start.1 = (bf16[128,512]{1,0:T(8,128)(2,1)}, bf16[128,512]{1,0:T(8,128)(2,1)S(1)}, u32[]{:S(2)}, u32[]{:S(2)}) collective-permute-start(bf16[128,512]{1,0:T(8,128)(2,1)} %own_ref.3), channel_id=1, source_target_pairs={{0,6},{1,9},{2,4},{3,11},{4,2},{5,13},{6,0},{7,15},{8,14},{9,1},{1... | collective-permute-start | bytes 393224 | tf_op jit(solution)/shard_map/ppermute | solution.py:93
  11.5 5.2 %collective-permute-start.4 = (bf16[128,512]{1,0:T(8,128)(2,1)S(1)}, bf16[128,512]{1,0:T(8,128)(2,1)S(1)}, u32[]{:S(2)}, u32[]{:S(2)}) collective-permute-start(bf16[128,512]{1,0:T(8,128)(2,1)S(1)} %collective-permute-done.2), channel_id=1, source_target_pairs={{0,2},{1,5},{2,0},{3,7},{4,6},{5,1},{6,4},{7,3},{8,10},{9,13},{10,... | collective-permute-start | bytes 393224 | tf_op jit(solution)/shard_map/ppermute | solution.py:93
  13.1 5.2 %collective-permute-start.3 = (bf16[384,512]{1,0:T(8,128)(2,1)S(1)}, bf16[384,512]{1,0:T(8,128)(2,1)S(1)}, u32[]{:S(2)}, u32[]{:S(2)}) collective-permute-start(bf16[384,512]{1,0:T(8,128)(2,1)S(1)} %constant_dynamic-update-slice_fusion.refs_1_), channel_id=1, source_target_pairs={{0,1},{1,0},{2,3},{3,2},{4,5},{5,4},{6,7},{7,6},{8,9},{9,8},{10,11... | collective-permute-start | bytes 1179656 | tf_op jit(solution)/shard_map/ppermute | solution.py:97
  13.2 5.0 %collective-permute-start.8 = (bf16[128,512]{1,0:T(8,128)(2,1)S(1)}, bf16[128,512]{1,0:T(8,128)(2,1)S(1)}, u32[]{:S(2)}, u32[]{:S(2)}) collective-permute-start(bf16[128,512]{1,0:T(8,128)(2,1)S(1)} %collective-permute-done.2), channel_id=1, source_target_pairs={{0,4},{1,3},{2,6},{3,1},{4,0},{5,7},{6,2},{7,5},{8,12},{9,11},{10,... | collective-permute-start | bytes 393224 | tf_op jit(solution)/shard_map/ppermute | solution.py:93
  14.6 5.5 %collective-permute-start.6 = (bf16[128,512]{1,0:T(8,128)(2,1)S(1)}, bf16[128,512]{1,0:T(8,128)(2,1)S(1)}, u32[]{:S(2)}, u32[]{:S(2)}) collective-permute-start(bf16[128,512]{1,0:T(8,128)(2,1)S(1)} %collective-permute-done), channel_id=1, source_target_pairs={{0,8},{1,9},{2,10},{3,11},{4,12},{5,13},{6,14},{7,15},{8,0},{9,1},... | collective-permute-start | bytes 393224 | tf_op jit(solution)/shard_map/ppermute | solution.py:93
  15.6 5.4 %collective-permute-start.7 = (bf16[128,512]{1,0:T(8,128)(2,1)S(1)}, bf16[128,512]{1,0:T(8,128)(2,1)S(1)}, u32[]{:S(2)}, u32[]{:S(2)}) collective-permute-start(bf16[128,512]{1,0:T(8,128)(2,1)S(1)} %collective-permute-done.1), channel_id=1, source_target_pairs={{0,8},{1,7},{2,10},{3,5},{4,12},{5,3},{6,14},{7,1},{8,0},{9,15},{1... | collective-permute-start | bytes 393224 | tf_op jit(solution)/shard_map/ppermute | solution.py:93
  16.7 5.0 %collective-permute-start.5 = (bf16[128,512]{1,0:T(8,128)(2,1)S(1)}, bf16[128,512]{1,0:T(8,128)(2,1)S(1)}, u32[]{:S(2)}, u32[]{:S(2)}) collective-permute-start(bf16[128,512]{1,0:T(8,128)(2,1)S(1)} %collective-permute-done.4), channel_id=1, source_target_pairs={{0,4},{1,3},{2,6},{3,1},{4,0},{5,7},{6,2},{7,5},{8,12},{9,11},{10,... | collective-permute-start | bytes 393224 | tf_op jit(solution)/shard_map/ppermute | solution.py:93
  18.1 0.9 %copy-start = (bf16[128,512]{1,0:T(8,128)(2,1)S(1)}, bf16[128,512]{1,0:T(8,128)(2,1)}, u32[]{:S(2)}) copy-start(bf16[128,512]{1,0:T(8,128)(2,1)} %own_ref.3) | copy-start | bytes 393220
  18.2 0.8 %copy-start.1 = (s32[128]{0:T(128)S(1)}, s32[128]{0:T(128)}, u32[]{:S(2)}) copy-start(s32[128]{0:T(128)} %param.3) | copy-start | bytes 1540
  18.2 4.0 %collective-permute-start.9 = (bf16[256,512]{1,0:T(8,128)(2,1)S(1)}, bf16[256,512]{1,0:T(8,128)(2,1)S(1)}, u32[]{:S(2)}, u32[]{:S(2)}) collective-permute-start(bf16[256,512]{1,0:T(8,128)(2,1)S(1)} %constant_dynamic-update-slice_fusion.3.refs_4_), channel_id=1, source_target_pairs={{0,1},{1,0},{2,3},{3,2},{4,5},{5,4},{6,7},{7,6},{8,9},{9,8},{10,11... | collective-permute-start | bytes 786440 | tf_op jit(solution)/shard_map/ppermute | solution.py:97
  21.7 1.3 %collective-permute-start.10 = (bf16[128,512]{1,0:T(8,128)(2,1)S(1)}, bf16[128,512]{1,0:T(8,128)(2,1)S(1)}, u32[]{:S(2)}, u32[]{:S(2)}) collective-permute-start(bf16[128,512]{1,0:T(8,128)(2,1)S(1)} %collective-permute-done.6.refs_6_), channel_id=1, source_target_pairs={{0,1},{1,0},{2,3},{3,2},{4,5},{5,4},{6,7},{7,6},{8,9},{9,8},{10,11... | collective-permute-start | bytes 393224 | tf_op jit(solution)/shard_map/ppermute | solution.py:97
  21.7 1.5 %collective-permute-start.11 = (bf16[128,512]{1,0:T(8,128)(2,1)S(1)}, bf16[128,512]{1,0:T(8,128)(2,1)S(1)}, u32[]{:S(2)}, u32[]{:S(2)}) collective-permute-start(bf16[128,512]{1,0:T(8,128)(2,1)S(1)} %collective-permute-done.5.refs_8_), channel_id=1, source_target_pairs={{0,1},{1,0},{2,3},{3,2},{4,5},{5,4},{6,7},{7,6},{8,9},{9,8},{10,11... | collective-permute-start | bytes 393224 | tf_op jit(solution)/shard_map/ppermute | solution.py:97

commit v4 on v3

--- a/solution.py
+++ b/solution.py
@@ -119,33 +119,38 @@
 
 
 def gather_rows(feats):
+    share = feats.shape[0] // 2
+    layer = lax.axis_index("rep")
+
+    def tie(value, *others):
+        return lax.optimization_barrier((value, *others))
+
+    def both(piece, chunks):
+        return [(piece, chunks), (swap(piece), [chunk.swapped() for chunk in chunks])]
+
     far = send(feats, Z2, Z3)
     near = send(feats, X, Y)
     cross = send(feats, XY, Z1)
-    side = send(near, Z1)
-    side_xy = send(cross, Z1, XY)
-    far_x, far_y = send(far, X, Y), send(far, Y, X)
+    far, near = tie(far, near)
+    side_in = near
+    side = send(side_in, Z1)
+    far_x = send(far, X, Y)
+    far_f = far
     far_xy = send(far_x, Y, X)
-
-    def both(piece, chunks):
-        return [(piece, chunks), (swap(piece), [chunk.swapped() for chunk in chunks])]
-
-    def split(piece, first, second):
-        share = piece.shape[0] // 2
-        halves = [(swap(piece[k * share : (k + 1) * share]), [Chunk((second, first), (k, k))]) for k in range(2)]
-        return [(piece, whole(first, second))] + halves
-
+    far_y = send(far_f, Y, X)
+    cross_in = cross
+    side_xy = send(cross_in, Z1, XY)
     early = both(join(near, cross, far), whole(X, Y) + whole(XY, Z1) + whole(Z2, Z3))
 
-    def late():
-        return both(join(far_x, far_y), whole(X ^ Z2, Y ^ Z3) + whole(Y ^ Z2, X ^ Z3))
-
     def last(sums):
-        g, s, sx, hits = lax.optimization_barrier((far_xy, side, side_xy, sums[1]))
-        sums = [sums[0], hits]
-        return late() + both(s, whole(X ^ Z1, Y ^ Z1)) + both(g, whole(XY ^ Z2, XY ^ Z3)) + [(sx, whole(XY ^ Z1, XY ^ Z1))], sums
-
-    return [[(feats, whole(0, 0))] + early, last]
+        g, s, fy = far_xy, side, far_y
+        sx = side_xy
+        g, s, sx, hits = tie(far_xy, side, side_xy, sums[1])
+        rest.extend(both(s, whole(X ^ Z1, Y ^ Z1)) + both(g, whole(XY ^ Z2, XY ^ Z3)) + [(sx, whole(XY ^ Z1, XY ^ Z1))])
+        return both(join(far_x, fy), whole(X ^ Z2, Y ^ Z3) + whole(Y ^ Z2, X ^ Z3)), [sums[0], hits]
+
+    rest = []
+    return [[(feats, whole(0, 0))] + early, last, lambda sums: (rest, sums)]
 
 
 def normalized(raw):

time: 27.1 us -> 26.5 us (0.978)
  waiting for transfers between devices: 6.52 us -> 5.5 us
  Pallas kernels: 4.78 us -> 5.15 us
    ppermute x4, waiting for transfers between devices: 1.03 us -> 0.01 us  [swap(): return lax.ppermute(piece, 'rep', [(0, 1), (1, 0)])]
    pallas_call x2 -> x3, Pallas kernels: 4.78 us -> 5.15 us  [whole_plan(): pl.pallas_call(functools.partial(stage_kernel, list(chunks), final), out_...]
  transfers between devices with their start and end apart: 12 -> 12, of which waited for: 5 -> 3; matrix products, arithmetic and copies ran while one was open for 0% -> 0% of each run, Pallas kernels for 4% -> 8%
where the time goes in v4:
time: 26.5 us; the launch traced here: 26.3 us
  starting transfers between devices  14.1 us (53%)
  waiting for transfers between devices  5.5 us (21%)
  Pallas kernels  5.15 us (19%)
  local copies, waits for them, and re-layouts  0.8 us (3%)
  between operations  0.73 us (3%)
    ppermute x8, starting transfers between devices, send(): return lax.ppermute(piece, ('batch', 'rep'), pairs)  13.5 us
    ppermute x8, waiting for transfers between devices, send(): return lax.ppermute(piece, ('batch', 'rep'), pairs)  5.49 us
    pallas_call x3, Pallas kernels, whole_plan(): pl.pallas_call(functools.partial(stage_kernel, list(chunks), final), out_...  5.15 us
    unnamed x7, local copies, waits for them, and re-layouts  0.78 us
    ppermute x4, starting transfers between devices, swap(): return lax.ppermute(piece, 'rep', [(0, 1), (1, 0)])  0.65 us
  transfers between devices with their start and end apart: 12, of which 3 were waited for; matrix products, arithmetic and copies ran while one was open for 0% of the time, Pallas kernels for 8%

profile of v4, /device:TPU:0, one launch (start us, length us, event | category | flops | bytes accessed | tf_op | source)
XLA Modules:
  0.0 26.3 jit_solution(2825112218424504094)
XLA Ops:
  0.6 4.1 %collective-permute-start = (bf16[128,512]{1,0:T(8,128)(2,1)}, bf16[128,512]{1,0:T(8,128)(2,1)S(1)}, u32[]{:S(2)}, u32[]{:S(2)}) collective-permute-start(bf16[128,512]{1,0:T(8,128)(2,1)} %own_ref.5), channel_id=1, source_target_pairs={{0,16},{1,25},{2,18},{3,27},{4,20},{5,29},{6,22},{7,31},{8,24},{9,... | collective-permute-start | bytes 393224 | tf_op jit(solution)/shard_map/ppermute | solution.py:93
  4.7 1.5 %collective-permute-start.1 = (bf16[128,512]{1,0:T(8,128)(2,1)}, bf16[128,512]{1,0:T(8,128)(2,1)S(1)}, u32[]{:S(2)}, u32[]{:S(2)}) collective-permute-start(bf16[128,512]{1,0:T(8,128)(2,1)} %own_ref.5), channel_id=1, source_target_pairs={{0,2},{1,5},{2,0},{3,7},{4,6},{5,1},{6,4},{7,3},{8,10},{9,13},{10,... | collective-permute-start | bytes 393224 | tf_op jit(solution)/shard_map/ppermute | solution.py:93
  6.2 1.5 %collective-permute-start.2 = (bf16[128,512]{1,0:T(8,128)(2,1)}, bf16[128,512]{1,0:T(8,128)(2,1)S(1)}, u32[]{:S(2)}, u32[]{:S(2)}) collective-permute-start(bf16[128,512]{1,0:T(8,128)(2,1)} %own_ref.5), channel_id=1, source_target_pairs={{0,6},{1,9},{2,4},{3,11},{4,2},{5,13},{6,0},{7,15},{8,14},{9,1},{1... | collective-permute-start | bytes 393224 | tf_op jit(solution)/shard_map/ppermute | solution.py:93
  7.7 3.8 %collective-permute-done = bf16[128,512]{1,0:T(8,128)(2,1)S(1)} collective-permute-done((bf16[128,512]{1,0:T(8,128)(2,1)}, bf16[128,512]{1,0:T(8,128)(2,1)S(1)}, u32[]{:S(2)}, u32[]{:S(2)}) %collective-permute-start) | collective-permute-done | bytes 131104 | tf_op jit(solution)/shard_map/ppermute | solution.py:93
  11.5 0.0 collective-permute-done.1
  11.5 1.5 %collective-permute-start.4 = (bf16[128,512]{1,0:T(8,128)(2,1)S(1)}, bf16[128,512]{1,0:T(8,128)(2,1)S(1)}, u32[]{:S(2)}, u32[]{:S(2)}) collective-permute-start(bf16[128,512]{1,0:T(8,128)(2,1)S(1)} %collective-permute-done), channel_id=1, source_target_pairs={{0,2},{1,5},{2,0},{3,7},{4,6},{5,1},{6,4},{7,3},{8,10},{9,13},{10,... | collective-permute-start | bytes 393224 | tf_op jit(solution)/shard_map/ppermute | solution.py:93
  13.0 0.0 collective-permute-done.2
  13.1 0.1 collective-permute-start.3
  13.2 1.5 %collective-permute-start.8 = (bf16[128,512]{1,0:T(8,128)(2,1)S(1)}, bf16[128,512]{1,0:T(8,128)(2,1)S(1)}, u32[]{:S(2)}, u32[]{:S(2)}) collective-permute-start(bf16[128,512]{1,0:T(8,128)(2,1)S(1)} %collective-permute-done), channel_id=1, source_target_pairs={{0,4},{1,3},{2,6},{3,1},{4,0},{5,7},{6,2},{7,5},{8,12},{9,11},{10,... | collective-permute-start | bytes 393224 | tf_op jit(solution)/shard_map/ppermute | solution.py:93
  14.6 1.0 %collective-permute-start.6 = (bf16[128,512]{1,0:T(8,128)(2,1)S(1)}, bf16[128,512]{1,0:T(8,128)(2,1)S(1)}, u32[]{:S(2)}, u32[]{:S(2)}) collective-permute-start(bf16[128,512]{1,0:T(8,128)(2,1)S(1)} %collective-permute-done.1), channel_id=1, source_target_pairs={{0,8},{1,9},{2,10},{3,11},{4,12},{5,13},{6,14},{7,15},{8,0},{9,1},... | collective-permute-start | bytes 393224 | tf_op jit(solution)/shard_map/ppermute | solution.py:93
  15.6 1.1 %collective-permute-start.7 = (bf16[128,512]{1,0:T(8,128)(2,1)S(1)}, bf16[128,512]{1,0:T(8,128)(2,1)S(1)}, u32[]{:S(2)}, u32[]{:S(2)}) collective-permute-start(bf16[128,512]{1,0:T(8,128)(2,1)S(1)} %collective-permute-done.2), channel_id=1, source_target_pairs={{0,8},{1,7},{2,10},{3,5},{4,12},{5,3},{6,14},{7,1},{8,0},{9,15},{1... | collective-permute-start | bytes 393224 | tf_op jit(solution)/shard_map/ppermute | solution.py:93
  16.7 0.0 collective-permute-done.4
  16.7 1.4 %collective-permute-start.5 = (bf16[128,512]{1,0:T(8,128)(2,1)S(1)}, bf16[128,512]{1,0:T(8,128)(2,1)S(1)}, u32[]{:S(2)}, u32[]{:S(2)}) collective-permute-start(bf16[128,512]{1,0:T(8,128)(2,1)S(1)} %collective-permute-done.4), channel_id=1, source_target_pairs={{0,4},{1,3},{2,6},{3,1},{4,0},{5,7},{6,2},{7,5},{8,12},{9,11},{10,... | collective-permute-start | bytes 393224 | tf_op jit(solution)/shard_map/ppermute | solution.py:93
  18.1 0.0 copy-start
  18.1 0.0 collective-permute-done.8
  18.2 0.0 copy-start.1
  18.2 0.1 collective-permute-start.9
  18.3 0.0 collective-permute-done.3.refs_2_
  18.3 0.7 %copy-done = bf16[128,512]{1,0:T(8,128)(2,1)S(1)} copy-done((bf16[128,512]{1,0:T(8,128)(2,1)S(1)}, bf16[128,512]{1,0:T(8,128)(2,1)}, u32[]{:S(2)}) %copy-start) | copy-done | bytes 131096
  19.0 0.0 copy-done.1
  19.0 1.1 %shard_map.41 = (bf16[896,512]{1,0:T(8,128)(2,1)S(1)}, f32[128,896]{1,0:T(8,128)S(1)}, f32[8,896]{1,0:T(8,128)S(1)}, f32[128,128]{1,0:T(8,128)S(1)}) custom-call(s32[1,128]{1,0:T(1,128)S(1)} %bitcast.2, bf16[128,512]{1,0:T(8,128)(2,1)S(1)} %copy-done, bf16[128,512]{1,0:T(8,128)(2,1)S(1)} %copy-done, ...), custom_call_target="tpu_custom_call" | custom-call | flops 1000 | tf_op jit(solution)/shard_map/pallas_call | solution.py:356
  20.1 0.0 collective-permute-done.6.refs_6_
  20.1 0.9 %collective-permute-done.7.refs_10_ = bf16[128,512]{1,0:T(8,128)(2,1)S(1)} collective-permute-done((bf16[128,512]{1,0:T(8,128)(2,1)S(1)}, bf16[128,512]{1,0:T(8,128)(2,1)S(1)}, u32[]{:S(2)}, u32[]{:S(2)}) %collective-permute-start.7) | collective-permute-done | bytes 131104 | tf_op jit(solution)/shard_map/ppermute | solution.py:93
  21.0 0.7 %collective-permute-done.5.refs_8_ = bf16[128,512]{1,0:T(8,128)(2,1)S(1)} collective-permute-done((bf16[128,512]{1,0:T(8,128)(2,1)S(1)}, bf16[128,512]{1,0:T(8,128)(2,1)S(1)}, u32[]{:S(2)}, u32[]{:S(2)}) %collective-permute-start.5) | collective-permute-done | bytes 131104 | tf_op jit(solution)/shard_map/ppermute | solution.py:93
  21.7 0.0 collective-permute-start.10
  21.7 0.5 %collective-permute-start.11 = (bf16[128,512]{1,0:T(8,128)(2,1)S(1)}, bf16[128,512]{1,0:T(8,128)(2,1)S(1)}, u32[]{:S(2)}, u32[]{:S(2)}) collective-permute-start(bf16[128,512]{1,0:T(8,128)(2,1)S(1)} %collective-permute-done.5.refs_8_), channel_id=1, source_target_pairs={{0,1},{1,0},{2,3},{3,2},{4,5},{5,4},{6,7},{7,6},{8,9},{9,8},{10,11... | collective-permute-start | bytes 393224 | tf_op jit(solution)/shard_map/ppermute | solution.py:97
  22.2 0.0 collective-permute-done.9.refs_4_
  22.2 1.1 %shard_map.42 = (bf16[512,512]{1,0:T(8,128)(2,1)S(1)}, f32[128,512]{1,0:T(8,128)S(1)}, f32[8,1408]{1,0:T(8,128)S(1)}, f32[128,128]{1,0:T(8,128)S(1)}) custom-call(s32[1,128]{1,0:T(1,128)S(1)} %bitcast.3, bf16[128,512]{1,0:T(8,128)(2,1)S(1)} %copy-done, bf16[896,512]{1,0:T(8,128)(2,1)S(1)} %get-tuple-element.20.refs_0_, ...), custom_call_target="tpu_custom_call" | custom-call | flops 1000 | tf_op jit(solution)/shard_map/pallas_call | solution.py:356
  23.3 0.0 collective-permute-done.10.refs_7_
  23.3 0.0 collective-permute-done.11.refs_9_
  23.4 3.0 %shard_map.43 = (f32[128,512]{1,0:T(8,128)}, f32[1,128]{1,0:T(1,128)}) custom-call(s32[1,128]{1,0:T(1,128)S(1)} %bitcast.4, bf16[128,512]{1,0:T(8,128)(2,1)S(1)} %copy-done, bf16[896,512]{1,0:T(8,128)(2,1)S(1)} %get-tuple-element.20.refs_0_, bf16[512,512]{1,0:T(8,128)(2,1)S(1)} %get-tuple-element.24.refs_1_, f32[128,896]{1,0:T(8,128)S(1)} %get-tuple-element.25.refs_2_, ...), custom_call_target="tpu_custom_call" | custom-call | flops 1000 | tf_op jit(solution)/shard_map/pallas_call | solution.py:356
  (5 shorter events, 0.1 us)
Async XLA Ops:
  0.6 10.9 %collective-permute-start = (bf16[128,512]{1,0:T(8,128)(2,1)}, bf16[128,512]{1,0:T(8,128)(2,1)S(1)}, u32[]{:S(2)}, u32[]{:S(2)}) collective-permute-start(bf16[128,512]{1,0:T(8,128)(2,1)} %own_ref.5), channel_id=1, source_target_pairs={{0,16},{1,25},{2,18},{3,27},{4,20},{5,29},{6,22},{7,31},{8,24},{9,... | collective-permute-start | bytes 393224 | tf_op jit(solution)/shard_map/ppermute | solution.py:93
  4.7 6.8 %collective-permute-start.1 = (bf16[128,512]{1,0:T(8,128)(2,1)}, bf16[128,512]{1,0:T(8,128)(2,1)S(1)}, u32[]{:S(2)}, u32[]{:S(2)}) collective-permute-start(bf16[128,512]{1,0:T(8,128)(2,1)} %own_ref.5), channel_id=1, source_target_pairs={{0,2},{1,5},{2,0},{3,7},{4,6},{5,1},{6,4},{7,3},{8,10},{9,13},{10,... | collective-permute-start | bytes 393224 | tf_op jit(solution)/shard_map/ppermute | solution.py:93
  6.2 6.8 %collective-permute-start.2 = (bf16[128,512]{1,0:T(8,128)(2,1)}, bf16[128,512]{1,0:T(8,128)(2,1)S(1)}, u32[]{:S(2)}, u32[]{:S(2)}) collective-permute-start(bf16[128,512]{1,0:T(8,128)(2,1)} %own_ref.5), channel_id=1, source_target_pairs={{0,6},{1,9},{2,4},{3,11},{4,2},{5,13},{6,0},{7,15},{8,14},{9,1},{1... | collective-permute-start | bytes 393224 | tf_op jit(solution)/shard_map/ppermute | solution.py:93
  11.5 5.2 %collective-permute-start.4 = (bf16[128,512]{1,0:T(8,128)(2,1)S(1)}, bf16[128,512]{1,0:T(8,128)(2,1)S(1)}, u32[]{:S(2)}, u32[]{:S(2)}) collective-permute-start(bf16[128,512]{1,0:T(8,128)(2,1)S(1)} %collective-permute-done), channel_id=1, source_target_pairs={{0,2},{1,5},{2,0},{3,7},{4,6},{5,1},{6,4},{7,3},{8,10},{9,13},{10,... | collective-permute-start | bytes 393224 | tf_op jit(solution)/shard_map/ppermute | solution.py:93
  13.1 5.2 %collective-permute-start.3 = (bf16[384,512]{1,0:T(8,128)(2,1)S(1)}, bf16[384,512]{1,0:T(8,128)(2,1)S(1)}, u32[]{:S(2)}, u32[]{:S(2)}) collective-permute-start(bf16[384,512]{1,0:T(8,128)(2,1)S(1)} %constant_dynamic-update-slice_fusion.refs_1_), channel_id=1, source_target_pairs={{0,1},{1,0},{2,3},{3,2},{4,5},{5,4},{6,7},{7,6},{8,9},{9,8},{10,11... | collective-permute-start | bytes 1179656 | tf_op jit(solution)/shard_map/ppermute | solution.py:97
  13.2 5.0 %collective-permute-start.8 = (bf16[128,512]{1,0:T(8,128)(2,1)S(1)}, bf16[128,512]{1,0:T(8,128)(2,1)S(1)}, u32[]{:S(2)}, u32[]{:S(2)}) collective-permute-start(bf16[128,512]{1,0:T(8,128)(2,1)S(1)} %collective-permute-done), channel_id=1, source_target_pairs={{0,4},{1,3},{2,6},{3,1},{4,0},{5,7},{6,2},{7,5},{8,12},{9,11},{10,... | collective-permute-start | bytes 393224 | tf_op jit(solution)/shard_map/ppermute | solution.py:93
  14.6 5.5 %collective-permute-start.6 = (bf16[128,512]{1,0:T(8,128)(2,1)S(1)}, bf16[128,512]{1,0:T(8,128)(2,1)S(1)}, u32[]{:S(2)}, u32[]{:S(2)}) collective-permute-start(bf16[128,512]{1,0:T(8,128)(2,1)S(1)} %collective-permute-done.1), channel_id=1, source_target_pairs={{0,8},{1,9},{2,10},{3,11},{4,12},{5,13},{6,14},{7,15},{8,0},{9,1},... | collective-permute-start | bytes 393224 | tf_op jit(solution)/shard_map/ppermute | solution.py:93
  15.6 5.4 %collective-permute-start.7 = (bf16[128,512]{1,0:T(8,128)(2,1)S(1)}, bf16[128,512]{1,0:T(8,128)(2,1)S(1)}, u32[]{:S(2)}, u32[]{:S(2)}) collective-permute-start(bf16[128,512]{1,0:T(8,128)(2,1)S(1)} %collective-permute-done.2), channel_id=1, source_target_pairs={{0,8},{1,7},{2,10},{3,5},{4,12},{5,3},{6,14},{7,1},{8,0},{9,15},{1... | collective-permute-start | bytes 393224 | tf_op jit(solution)/shard_map/ppermute | solution.py:93
  16.7 5.0 %collective-permute-start.5 = (bf16[128,512]{1,0:T(8,128)(2,1)S(1)}, bf16[128,512]{1,0:T(8,128)(2,1)S(1)}, u32[]{:S(2)}, u32[]{:S(2)}) collective-permute-start(bf16[128,512]{1,0:T(8,128)(2,1)S(1)} %collective-permute-done.4), channel_id=1, source_target_pairs={{0,4},{1,3},{2,6},{3,1},{4,0},{5,7},{6,2},{7,5},{8,12},{9,11},{10,... | collective-permute-start | bytes 393224 | tf_op jit(solution)/shard_map/ppermute | solution.py:93
  18.1 0.9 %copy-start = (bf16[128,512]{1,0:T(8,128)(2,1)S(1)}, bf16[128,512]{1,0:T(8,128)(2,1)}, u32[]{:S(2)}) copy-start(bf16[128,512]{1,0:T(8,128)(2,1)} %own_ref.5) | copy-start | bytes 393220
  18.2 0.8 %copy-start.1 = (s32[128]{0:T(128)S(1)}, s32[128]{0:T(128)}, u32[]{:S(2)}) copy-start(s32[128]{0:T(128)} %param.3) | copy-start | bytes 1540
  18.2 4.0 %collective-permute-start.9 = (bf16[256,512]{1,0:T(8,128)(2,1)S(1)}, bf16[256,512]{1,0:T(8,128)(2,1)S(1)}, u32[]{:S(2)}, u32[]{:S(2)}) collective-permute-start(bf16[256,512]{1,0:T(8,128)(2,1)S(1)} %constant_dynamic-update-slice_fusion.3.refs_3_), channel_id=1, source_target_pairs={{0,1},{1,0},{2,3},{3,2},{4,5},{5,4},{6,7},{7,6},{8,9},{9,8},{10,11... | collective-permute-start | bytes 786440 | tf_op jit(solution)/shard_map/ppermute | solution.py:97
  21.7 1.6 %collective-permute-start.10 = (bf16[128,512]{1,0:T(8,128)(2,1)S(1)}, bf16[128,512]{1,0:T(8,128)(2,1)S(1)}, u32[]{:S(2)}, u32[]{:S(2)}) collective-permute-start(bf16[128,512]{1,0:T(8,128)(2,1)S(1)} %collective-permute-done.6.refs_6_), channel_id=1, source_target_pairs={{0,1},{1,0},{2,3},{3,2},{4,5},{5,4},{6,7},{7,6},{8,9},{9,8},{10,11... | collective-permute-start | bytes 393224 | tf_op jit(solution)/shard_map/ppermute | solution.py:97
  21.7 1.6 %collective-permute-start.11 = (bf16[128,512]{1,0:T(8,128)(2,1)S(1)}, bf16[128,512]{1,0:T(8,128)(2,1)S(1)}, u32[]{:S(2)}, u32[]{:S(2)}) collective-permute-start(bf16[128,512]{1,0:T(8,128)(2,1)S(1)} %collective-permute-done.5.refs_8_), channel_id=1, source_target_pairs={{0,1},{1,0},{2,3},{3,2},{4,5},{5,4},{6,7},{7,6},{8,9},{9,8},{10,11... | collective-permute-start | bytes 393224 | tf_op jit(solution)/shard_map/ppermute | solution.py:97

commit v5 on v3

--- a/solution.py
+++ b/solution.py
@@ -126,26 +126,44 @@
     side_xy = send(cross, Z1, XY)
     far_x, far_y = send(far, X, Y), send(far, Y, X)
     far_xy = send(far_x, Y, X)
+    held = {}
+
+    def tie(value, *others):
+        return lax.optimization_barrier((value, *others))
 
     def both(piece, chunks):
         return [(piece, chunks), (swap(piece), [chunk.swapped() for chunk in chunks])]
 
-    def split(piece, first, second):
-        share = piece.shape[0] // 2
-        halves = [(swap(piece[k * share : (k + 1) * share]), [Chunk((second, first), (k, k))]) for k in range(2)]
-        return [(piece, whole(first, second))] + halves
-
-    early = both(join(near, cross, far), whole(X, Y) + whole(XY, Z1) + whole(Z2, Z3))
-
-    def late():
-        return both(join(far_x, far_y), whole(X ^ Z2, Y ^ Z3) + whole(Y ^ Z2, X ^ Z3))
+    NC, CC, FC = whole(X, Y), whole(XY, Z1), whole(Z2, Z3)
+    EC = whole(X ^ Z2, Y ^ Z3)
+    YC = whole(Y ^ Z2, X ^ Z3)
+    GC = whole(XY ^ Z2, XY ^ Z3)
+    SC = whole(X ^ Z1, Y ^ Z1)
+    SX = whole(XY ^ Z1, XY ^ Z1)
+
+    def other(piece, chunks):
+        return both(piece, chunks)[1]
+
+    pair = join(far_x, far_y)
+    early = both(join(near, cross, far), NC + CC + FC) + [(pair, EC + YC)]
+
+    def second(sums):
+        s, sx, g, hits = side, side_xy, far_xy, sums[1]
+        s, sx, hits = tie(s, sx, hits)
+        held.update(s=s, sx=sx, g=g)
+        return [(s, SC), (sx, SX)], [sums[0], hits]
+
+    def third(sums):
+        s, sx, g, hits = held["s"], held["sx"], held["g"], sums[1]
+        g, s, hits = tie(g, s, hits)
+        held.update(s=s, sx=sx, g=g)
+        return [other(pair, EC + YC)], [sums[0], hits]
 
     def last(sums):
-        g, s, sx, hits = lax.optimization_barrier((far_xy, side, side_xy, sums[1]))
-        sums = [sums[0], hits]
-        return late() + both(s, whole(X ^ Z1, Y ^ Z1)) + both(g, whole(XY ^ Z2, XY ^ Z3)) + [(sx, whole(XY ^ Z1, XY ^ Z1))], sums
-
-    return [[(feats, whole(0, 0))] + early, last]
+        s, sx, g = held["s"], held["sx"], held["g"]
+        return both(g, GC) + [other(s, SC)], sums
+
+    return [[(feats, whole(0, 0))] + early, second, third, last]
 
 
 def normalized(raw):
@@ -290,10 +308,11 @@
                 denom[:, shift(j, old)] += fold_rows(weight)
             denom[:, shift(i, start)] += fold_rows(row_sum.T)
         start += old_embed.shape[0]
-    for i in spans(new, block):
+    small = rows if final and new <= 3 * rows else block
+    for i in spans(new, small):
         left = embed[i, :]
         row_sum = jnp.zeros((left.shape[0], 128), jnp.float32)
-        for j in spans(new, block):
+        for j in spans(new, small):
             if j.start < i.start:
                 continue
             score, weight = weigh(left, embed[j, :])

time: 27.1 us -> 26.1 us (0.963)
  waiting for transfers between devices: 6.52 us -> 5.28 us
  Pallas kernels: 4.78 us -> 5.68 us
  local copies, waits for them, and re-layouts: 0.8 us -> 0.06 us
    pallas_call x2 -> x4, Pallas kernels: 4.78 us -> 5.68 us  [whole_plan(): pl.pallas_call(functools.partial(stage_kernel, list(chunks), final), out_...]
    ppermute x4, waiting for transfers between devices: 1.03 us -> 0.15 us  [swap(): return lax.ppermute(piece, 'rep', [(0, 1), (1, 0)])]
    unnamed x7, local copies, waits for them, and re-layouts: 0.78 us -> 0.04 us
    ppermute x8, waiting for transfers between devices: 5.49 us -> 5.13 us  [send(): return lax.ppermute(piece, ('batch', 'rep'), pairs)]
  transfers between devices with their start and end apart: 12 -> 12, of which waited for: 5 -> 4; matrix products, arithmetic and copies ran while one was open for 0% -> 0% of each run, Pallas kernels for 4% -> 12%
where the time goes in v5:
time: 26.1 us; the launch traced here: 26 us
  starting transfers between devices  14.2 us (54%)
  Pallas kernels  5.68 us (22%)
  waiting for transfers between devices  5.28 us (20%)
  between operations  0.76 us (3%)
    ppermute x8, starting transfers between devices, send(): return lax.ppermute(piece, ('batch', 'rep'), pairs)  13.5 us
    pallas_call x4, Pallas kernels, whole_plan(): pl.pallas_call(functools.partial(stage_kernel, list(chunks), final), out_...  5.68 us
    ppermute x8, waiting for transfers between devices, send(): return lax.ppermute(piece, ('batch', 'rep'), pairs)  5.13 us
    ppermute x4, starting transfers between devices, swap(): return lax.ppermute(piece, 'rep', [(0, 1), (1, 0)])  0.71 us
  transfers between devices with their start and end apart: 12, of which 4 were waited for; matrix products, arithmetic and copies ran while one was open for 0% of the time, Pallas kernels for 12%

profile of v5, /device:TPU:0, one launch (start us, length us, event | category | flops | bytes accessed | tf_op | source)
XLA Modules:
  0.0 26.0 jit_solution(7792658740290302701)
XLA Ops:
  0.6 0.0 copy-start
  0.6 0.0 copy-start.1
  0.6 4.1 %collective-permute-start.2 = (bf16[128,512]{1,0:T(8,128)(2,1)}, bf16[128,512]{1,0:T(8,128)(2,1)S(1)}, u32[]{:S(2)}, u32[]{:S(2)}) collective-permute-start(bf16[128,512]{1,0:T(8,128)(2,1)} %own_ref.7), channel_id=1, source_target_pairs={{0,16},{1,25},{2,18},{3,27},{4,20},{5,29},{6,22},{7,31},{8,24},{9,... | collective-permute-start | bytes 393224 | tf_op jit(solution)/shard_map/ppermute | solution.py:93
  4.8 1.5 %collective-permute-start = (bf16[128,512]{1,0:T(8,128)(2,1)}, bf16[128,512]{1,0:T(8,128)(2,1)S(1)}, u32[]{:S(2)}, u32[]{:S(2)}) collective-permute-start(bf16[128,512]{1,0:T(8,128)(2,1)} %own_ref.7), channel_id=1, source_target_pairs={{0,2},{1,5},{2,0},{3,7},{4,6},{5,1},{6,4},{7,3},{8,10},{9,13},{10,... | collective-permute-start | bytes 393224 | tf_op jit(solution)/shard_map/ppermute | solution.py:93
  6.2 1.5 %collective-permute-start.1 = (bf16[128,512]{1,0:T(8,128)(2,1)}, bf16[128,512]{1,0:T(8,128)(2,1)S(1)}, u32[]{:S(2)}, u32[]{:S(2)}) collective-permute-start(bf16[128,512]{1,0:T(8,128)(2,1)} %own_ref.7), channel_id=1, source_target_pairs={{0,6},{1,9},{2,4},{3,11},{4,2},{5,13},{6,0},{7,15},{8,14},{9,1},{1... | collective-permute-start | bytes 393224 | tf_op jit(solution)/shard_map/ppermute | solution.py:93
  7.7 3.8 %collective-permute-done.2 = bf16[128,512]{1,0:T(8,128)(2,1)S(1)} collective-permute-done((bf16[128,512]{1,0:T(8,128)(2,1)}, bf16[128,512]{1,0:T(8,128)(2,1)S(1)}, u32[]{:S(2)}, u32[]{:S(2)}) %collective-permute-start.2) | collective-permute-done | bytes 131104 | tf_op jit(solution)/shard_map/ppermute | solution.py:93
  11.5 1.5 %collective-permute-start.4 = (bf16[128,512]{1,0:T(8,128)(2,1)S(1)}, bf16[128,512]{1,0:T(8,128)(2,1)S(1)}, u32[]{:S(2)}, u32[]{:S(2)}) collective-permute-start(bf16[128,512]{1,0:T(8,128)(2,1)S(1)} %collective-permute-done.2), channel_id=1, source_target_pairs={{0,2},{1,5},{2,0},{3,7},{4,6},{5,1},{6,4},{7,3},{8,10},{9,13},{10,... | collective-permute-start | bytes 393224 | tf_op jit(solution)/shard_map/ppermute | solution.py:93
  13.0 0.0 collective-permute-done
  13.0 0.0 collective-permute-done.1
  13.1 0.1 collective-permute-start.3
  13.2 1.5 %collective-permute-start.5 = (bf16[128,512]{1,0:T(8,128)(2,1)S(1)}, bf16[128,512]{1,0:T(8,128)(2,1)S(1)}, u32[]{:S(2)}, u32[]{:S(2)}) collective-permute-start(bf16[128,512]{1,0:T(8,128)(2,1)S(1)} %collective-permute-done.2), channel_id=1, source_target_pairs={{0,4},{1,3},{2,6},{3,1},{4,0},{5,7},{6,2},{7,5},{8,12},{9,11},{10,... | collective-permute-start | bytes 393224 | tf_op jit(solution)/shard_map/ppermute | solution.py:93
  14.7 1.0 %collective-permute-start.6 = (bf16[128,512]{1,0:T(8,128)(2,1)S(1)}, bf16[128,512]{1,0:T(8,128)(2,1)S(1)}, u32[]{:S(2)}, u32[]{:S(2)}) collective-permute-start(bf16[128,512]{1,0:T(8,128)(2,1)S(1)} %collective-permute-done), channel_id=1, source_target_pairs={{0,8},{1,9},{2,10},{3,11},{4,12},{5,13},{6,14},{7,15},{8,0},{9,1},... | collective-permute-start | bytes 393224 | tf_op jit(solution)/shard_map/ppermute | solution.py:93
  15.6 1.1 %collective-permute-start.7 = (bf16[128,512]{1,0:T(8,128)(2,1)S(1)}, bf16[128,512]{1,0:T(8,128)(2,1)S(1)}, u32[]{:S(2)}, u32[]{:S(2)}) collective-permute-start(bf16[128,512]{1,0:T(8,128)(2,1)S(1)} %collective-permute-done.1), channel_id=1, source_target_pairs={{0,8},{1,7},{2,10},{3,5},{4,12},{5,3},{6,14},{7,1},{8,0},{9,15},{1... | collective-permute-start | bytes 393224 | tf_op jit(solution)/shard_map/ppermute | solution.py:93
  16.7 0.0 collective-permute-done.4
  16.7 1.4 %collective-permute-start.8 = (bf16[128,512]{1,0:T(8,128)(2,1)S(1)}, bf16[128,512]{1,0:T(8,128)(2,1)S(1)}, u32[]{:S(2)}, u32[]{:S(2)}) collective-permute-start(bf16[128,512]{1,0:T(8,128)(2,1)S(1)} %collective-permute-done.4), channel_id=1, source_target_pairs={{0,4},{1,3},{2,6},{3,1},{4,0},{5,7},{6,2},{7,5},{8,12},{9,11},{10,... | collective-permute-start | bytes 393224 | tf_op jit(solution)/shard_map/ppermute | solution.py:93
  18.2 0.1 collective-permute-done.5
  18.2 0.1 collective-permute-start.9
  18.3 0.0 collective-permute-done.3.refs_2_
  18.3 0.0 copy-done
  18.3 0.0 copy-done.1
  18.3 1.5 %shard_map.41 = (bf16[1152,512]{1,0:T(8,128)(2,1)S(1)}, f32[128,1152]{1,0:T(8,128)S(1)}, f32[8,1152]{1,0:T(8,128)S(1)}, f32[128,128]{1,0:T(8,128)S(1)}) custom-call(s32[1,128]{1,0:T(1,128)S(1)} %bitcast.2, bf16[128,512]{1,0:T(8,128)(2,1)S(1)} %copy-done, bf16[128,512]{1,0:T(8,128)(2,1)S(1)} %copy-done, ...), custom_call_target="tpu_custom_call" | custom-call | flops 1000 | tf_op jit(solution)/shard_map/pallas_call | solution.py:370
  19.8 0.0 collective-permute-done.6.refs_3_
  19.8 1.2 %collective-permute-done.7.refs_4_ = bf16[128,512]{1,0:T(8,128)(2,1)S(1)} collective-permute-done((bf16[128,512]{1,0:T(8,128)(2,1)S(1)}, bf16[128,512]{1,0:T(8,128)(2,1)S(1)}, u32[]{:S(2)}, u32[]{:S(2)}) %collective-permute-start.7) | collective-permute-done | bytes 131104 | tf_op jit(solution)/shard_map/ppermute | solution.py:93
  21.0 0.7 %shard_map.42 = (bf16[256,512]{1,0:T(8,128)(2,1)S(1)}, f32[128,256]{1,0:T(8,128)S(1)}, f32[8,1408]{1,0:T(8,128)S(1)}, f32[128,128]{1,0:T(8,128)S(1)}) custom-call(s32[1,128]{1,0:T(1,128)S(1)} %bitcast.3, bf16[128,512]{1,0:T(8,128)(2,1)S(1)} %copy-done, bf16[1152,512]{1,0:T(8,128)(2,1)S(1)} %get-tuple-element.22.refs_0_, ...), custom_call_target="tpu_custom_call" | custom-call | flops 1000 | tf_op jit(solution)/shard_map/pallas_call | solution.py:370
  21.8 0.0 collective-permute-done.8.refs_8_
  21.8 0.1 collective-permute-start.10
  21.9 0.5 %collective-permute-start.11 = (bf16[128,512]{1,0:T(8,128)(2,1)S(1)}, bf16[128,512]{1,0:T(8,128)(2,1)S(1)}, u32[]{:S(2)}, u32[]{:S(2)}) collective-permute-start(bf16[128,512]{1,0:T(8,128)(2,1)S(1)} %collective-permute-done.6.refs_3_), channel_id=1, source_target_pairs={{0,1},{1,0},{2,3},{3,2},{4,5},{5,4},{6,7},{7,6},{8,9},{9,8},{10,11... | collective-permute-start | bytes 393224 | tf_op jit(solution)/shard_map/ppermute | solution.py:97
  22.4 0.0 collective-permute-done.9.refs_4_
  22.4 0.9 %shard_map.43 = (bf16[256,512]{1,0:T(8,128)(2,1)S(1)}, f32[128,256]{1,0:T(8,128)S(1)}, f32[8,1664]{1,0:T(8,128)S(1)}, f32[128,128]{1,0:T(8,128)S(1)}) custom-call(s32[1,128]{1,0:T(1,128)S(1)} %bitcast.4, bf16[128,512]{1,0:T(8,128)(2,1)S(1)} %copy-done, bf16[1152,512]{1,0:T(8,128)(2,1)S(1)} %get-tuple-element.22.refs_0_, ...), custom_call_target="tpu_custom_call" | custom-call | flops 1000 | tf_op jit(solution)/shard_map/pallas_call | solution.py:370
  23.2 0.0 collective-permute-done.10.refs_9_
  23.2 0.1 collective-permute-done.11.refs_10_
  23.4 2.6 %shard_map.44 = (f32[128,512]{1,0:T(8,128)}, f32[1,128]{1,0:T(1,128)}) custom-call(s32[1,128]{1,0:T(1,128)S(1)} %bitcast.5, bf16[128,512]{1,0:T(8,128)(2,1)S(1)} %copy-done, bf16[1152,512]{1,0:T(8,128)(2,1)S(1)} %get-tuple-element.22.refs_0_, bf16[256,512]{1,0:T(8,128)(2,1)S(1)} %get-tuple-element.28.refs_1_, ...), custom_call_target="tpu_custom_call" | custom-call | flops 1000 | tf_op jit(solution)/shard_map/pallas_call | solution.py:370
  (5 shorter events, 0.1 us)
Async XLA Ops:
  0.6 17.7 %copy-start = (bf16[128,512]{1,0:T(8,128)(2,1)S(1)}, bf16[128,512]{1,0:T(8,128)(2,1)}, u32[]{:S(2)}) copy-start(bf16[128,512]{1,0:T(8,128)(2,1)} %own_ref.7) | copy-start | bytes 393220
  0.6 17.7 %copy-start.1 = (s32[128]{0:T(128)S(1)}, s32[128]{0:T(128)}, u32[]{:S(2)}) copy-start(s32[128]{0:T(128)} %param.3) | copy-start | bytes 1540
  0.6 10.9 %collective-permute-start.2 = (bf16[128,512]{1,0:T(8,128)(2,1)}, bf16[128,512]{1,0:T(8,128)(2,1)S(1)}, u32[]{:S(2)}, u32[]{:S(2)}) collective-permute-start(bf16[128,512]{1,0:T(8,128)(2,1)} %own_ref.7), channel_id=1, source_target_pairs={{0,16},{1,25},{2,18},{3,27},{4,20},{5,29},{6,22},{7,31},{8,24},{9,... | collective-permute-start | bytes 393224 | tf_op jit(solution)/shard_map/ppermute | solution.py:93
  4.8 8.3 %collective-permute-start = (bf16[128,512]{1,0:T(8,128)(2,1)}, bf16[128,512]{1,0:T(8,128)(2,1)S(1)}, u32[]{:S(2)}, u32[]{:S(2)}) collective-permute-start(bf16[128,512]{1,0:T(8,128)(2,1)} %own_ref.7), channel_id=1, source_target_pairs={{0,2},{1,5},{2,0},{3,7},{4,6},{5,1},{6,4},{7,3},{8,10},{9,13},{10,... | collective-permute-start | bytes 393224 | tf_op jit(solution)/shard_map/ppermute | solution.py:93
  6.2 6.8 %collective-permute-start.1 = (bf16[128,512]{1,0:T(8,128)(2,1)}, bf16[128,512]{1,0:T(8,128)(2,1)S(1)}, u32[]{:S(2)}, u32[]{:S(2)}) collective-permute-start(bf16[128,512]{1,0:T(8,128)(2,1)} %own_ref.7), channel_id=1, source_target_pairs={{0,6},{1,9},{2,4},{3,11},{4,2},{5,13},{6,0},{7,15},{8,14},{9,1},{1... | collective-permute-start | bytes 393224 | tf_op jit(solution)/shard_map/ppermute | solution.py:93
  11.5 5.2 %collective-permute-start.4 = (bf16[128,512]{1,0:T(8,128)(2,1)S(1)}, bf16[128,512]{1,0:T(8,128)(2,1)S(1)}, u32[]{:S(2)}, u32[]{:S(2)}) collective-permute-start(bf16[128,512]{1,0:T(8,128)(2,1)S(1)} %collective-permute-done.2), channel_id=1, source_target_pairs={{0,2},{1,5},{2,0},{3,7},{4,6},{5,1},{6,4},{7,3},{8,10},{9,13},{10,... | collective-permute-start | bytes 393224 | tf_op jit(solution)/shard_map/ppermute | solution.py:93
  13.1 5.2 %collective-permute-start.3 = (bf16[384,512]{1,0:T(8,128)(2,1)S(1)}, bf16[384,512]{1,0:T(8,128)(2,1)S(1)}, u32[]{:S(2)}, u32[]{:S(2)}) collective-permute-start(bf16[384,512]{1,0:T(8,128)(2,1)S(1)} %constant_dynamic-update-slice_fusion.refs_1_), channel_id=1, source_target_pairs={{0,1},{1,0},{2,3},{3,2},{4,5},{5,4},{6,7},{7,6},{8,9},{9,8},{10,11... | collective-permute-start | bytes 1179656 | tf_op jit(solution)/shard_map/ppermute | solution.py:97
  13.2 5.0 %collective-permute-start.5 = (bf16[128,512]{1,0:T(8,128)(2,1)S(1)}, bf16[128,512]{1,0:T(8,128)(2,1)S(1)}, u32[]{:S(2)}, u32[]{:S(2)}) collective-permute-start(bf16[128,512]{1,0:T(8,128)(2,1)S(1)} %collective-permute-done.2), channel_id=1, source_target_pairs={{0,4},{1,3},{2,6},{3,1},{4,0},{5,7},{6,2},{7,5},{8,12},{9,11},{10,... | collective-permute-start | bytes 393224 | tf_op jit(solution)/shard_map/ppermute | solution.py:93
  14.7 5.1 %collective-permute-start.6 = (bf16[128,512]{1,0:T(8,128)(2,1)S(1)}, bf16[128,512]{1,0:T(8,128)(2,1)S(1)}, u32[]{:S(2)}, u32[]{:S(2)}) collective-permute-start(bf16[128,512]{1,0:T(8,128)(2,1)S(1)} %collective-permute-done), channel_id=1, source_target_pairs={{0,8},{1,9},{2,10},{3,11},{4,12},{5,13},{6,14},{7,15},{8,0},{9,1},... | collective-permute-start | bytes 393224 | tf_op jit(solution)/shard_map/ppermute | solution.py:93
  15.6 5.4 %collective-permute-start.7 = (bf16[128,512]{1,0:T(8,128)(2,1)S(1)}, bf16[128,512]{1,0:T(8,128)(2,1)S(1)}, u32[]{:S(2)}, u32[]{:S(2)}) collective-permute-start(bf16[128,512]{1,0:T(8,128)(2,1)S(1)} %collective-permute-done.1), channel_id=1, source_target_pairs={{0,8},{1,7},{2,10},{3,5},{4,12},{5,3},{6,14},{7,1},{8,0},{9,15},{1... | collective-permute-start | bytes 393224 | tf_op jit(solution)/shard_map/ppermute | solution.py:93
  16.7 5.1 %collective-permute-start.8 = (bf16[128,512]{1,0:T(8,128)(2,1)S(1)}, bf16[128,512]{1,0:T(8,128)(2,1)S(1)}, u32[]{:S(2)}, u32[]{:S(2)}) collective-permute-start(bf16[128,512]{1,0:T(8,128)(2,1)S(1)} %collective-permute-done.4), channel_id=1, source_target_pairs={{0,4},{1,3},{2,6},{3,1},{4,0},{5,7},{6,2},{7,5},{8,12},{9,11},{10,... | collective-permute-start | bytes 393224 | tf_op jit(solution)/shard_map/ppermute | solution.py:93
  18.2 4.1 %collective-permute-start.9 = (bf16[256,512]{1,0:T(8,128)(2,1)S(1)}, bf16[256,512]{1,0:T(8,128)(2,1)S(1)}, u32[]{:S(2)}, u32[]{:S(2)}) collective-permute-start(bf16[256,512]{1,0:T(8,128)(2,1)S(1)} %constant_dynamic-update-slice_fusion.3.refs_3_), channel_id=1, source_target_pairs={{0,1},{1,0},{2,3},{3,2},{4,5},{5,4},{6,7},{7,6},{8,9},{9,8},{10,11... | collective-permute-start | bytes 786440 | tf_op jit(solution)/shard_map/ppermute | solution.py:97
  21.8 1.4 %collective-permute-start.10 = (bf16[128,512]{1,0:T(8,128)(2,1)S(1)}, bf16[128,512]{1,0:T(8,128)(2,1)S(1)}, u32[]{:S(2)}, u32[]{:S(2)}) collective-permute-start(bf16[128,512]{1,0:T(8,128)(2,1)S(1)} %collective-permute-done.8.refs_8_), channel_id=1, source_target_pairs={{0,1},{1,0},{2,3},{3,2},{4,5},{5,4},{6,7},{7,6},{8,9},{9,8},{10,11... | collective-permute-start | bytes 393224 | tf_op jit(solution)/shard_map/ppermute | solution.py:97
  21.9 1.5 %collective-permute-start.11 = (bf16[128,512]{1,0:T(8,128)(2,1)S(1)}, bf16[128,512]{1,0:T(8,128)(2,1)S(1)}, u32[]{:S(2)}, u32[]{:S(2)}) collective-permute-start(bf16[128,512]{1,0:T(8,128)(2,1)S(1)} %collective-permute-done.6.refs_3_), channel_id=1, source_target_pairs={{0,1},{1,0},{2,3},{3,2},{4,5},{5,4},{6,7},{7,6},{8,9},{9,8},{10,11... | collective-permute-start | bytes 393224 | tf_op jit(solution)/shard_map/ppermute | solution.py:97

commit v6 on v2

--- a/solution.py
+++ b/solution.py
@@ -102,39 +102,53 @@
 
 
 class Chunk:
-    def __init__(self, offsets, parts=None):
+    def __init__(self, *offsets):
         self.offsets = offsets
-        self.parts = parts
 
     def swapped(self):
-        return Chunk(self.offsets[::-1], self.parts and self.parts[::-1])
-
-
-def halves(first, second, *within):
-    return [Chunk((first ^ w, second ^ w), (0, 1)) for w in within]
-
-
-def whole(first, second):
-    return [Chunk((first, second))]
+        return Chunk(*self.offsets[::-1])
+
+
+def tie(*values):
+    return lax.optimization_barrier(values)
 
 
 def gather_rows(feats):
     far = send(feats, Z2, Z3)
     near = send(feats, X, Y)
     cross = send(feats, XY, Z1)
+    far, near = tie(far, near)
     side = send(near, Z1)
     side_xy = send(cross, Z1, XY)
     far_x, far_y = send(far, X, Y), send(far, Y, X)
-    far_xy = send(far, XY)
-
-    def both(piece, chunks):
-        return [(piece, chunks), (swap(piece), [chunk.swapped() for chunk in chunks])]
-
-    early = both(join(near, cross, far), whole(X, Y) + whole(XY, Z1) + whole(Z2, Z3))
-    middle = both(side, whole(X ^ Z1, Y ^ Z1))
-    late = both(join(far_x, far_y), whole(X ^ Z2, Y ^ Z3) + whole(Y ^ Z2, X ^ Z3))
-    last = both(far_xy, whole(XY ^ Z2, XY ^ Z3))
-    return [[(feats, whole(0, 0))] + early, middle + late + last + [(side_xy, whole(XY ^ Z1, XY ^ Z1))]]
+    far_xy = send(far_x, Y, X)
+    early = join(near, cross, far)
+    pair = join(far_x, far_y)
+    early_chunks = [Chunk(X, Y), Chunk(XY, Z1), Chunk(Z2, Z3)]
+    pair_chunks = [Chunk(X ^ Z2, Y ^ Z3), Chunk(Y ^ Z2, X ^ Z3)]
+    far_xy_chunks = [Chunk(XY ^ Z2, XY ^ Z3)]
+    side_chunks = [Chunk(X ^ Z1, Y ^ Z1)]
+    held = {}
+
+    def other(piece, chunks):
+        return swap(piece), [chunk.swapped() for chunk in chunks]
+
+    def first(sums):
+        return [(feats, [Chunk(0, 0)]), (early, early_chunks), other(early, early_chunks), (pair, pair_chunks)], sums
+
+    def second(sums):
+        held["side"], piece, hits = tie(side, side_xy, sums[1])
+        return [(held["side"], side_chunks), (piece, [Chunk(XY ^ Z1, XY ^ Z1)])], [sums[0], hits]
+
+    def third(sums):
+        held["far_xy"], held["side"], hits = tie(far_xy, held["side"], sums[1])
+        return [(held["far_xy"], far_xy_chunks), other(pair, pair_chunks)], [sums[0], hits]
+
+    def last(sums):
+        piece = held["far_xy"]
+        return [other(piece, far_xy_chunks), other(held["side"], side_chunks)], sums
+
+    return [first, second, third, last]
 
 
 def normalized(raw):
@@ -168,23 +182,7 @@
     layer = lax.axis_index("rep")
     block = lax.axis_index("batch")
     lane = lax.broadcasted_iota(jnp.int32, (1, rows), 1)
-    share = rows // 2
-
-    def base(chunk):
-        first = (block ^ jnp.where(layer == 0, *chunk.offsets)) * rows
-        return first if chunk.parts is None else first + jnp.where(layer == 0, *chunk.parts) * share
-
-    ids = []
-    waiting = []
-    for chunk in chunks:
-        if chunk.parts is None:
-            ids.append(lane + base(chunk))
-        else:
-            waiting.append(base(chunk))
-        if len(waiting) == 2:
-            ids.append(lane + jnp.where(lane < share, waiting[0], waiting[1] - share))
-            waiting = []
-    return ids
+    return [lane + (block ^ jnp.where(layer == 0, *chunk.offsets)) * rows for chunk in chunks]
 
 
 def spans(total, block):
@@ -268,7 +266,7 @@
 
     start = 0
     for old_embed in old_embeds:
-        for i in spans(old_embed.shape[0], block):
+        for i in spans(old_embed.shape[0], 2 * block):
             left = old_embed[i, :]
             row_sum = jnp.zeros((left.shape[0], 128), jnp.float32)
             for j in spans(new, block):
@@ -280,10 +278,11 @@
                 denom[:, shift(j, old)] += fold_rows(weight)
             denom[:, shift(i, start)] += fold_rows(row_sum.T)
         start += old_embed.shape[0]
-    for i in spans(new, block):
+    small = rows if final and new <= 3 * rows else block
+    for i in spans(new, small):
         left = embed[i, :]
         row_sum = jnp.zeros((left.shape[0], 128), jnp.float32)
-        for j in spans(new, block):
+        for j in spans(new, small):
             if j.start < i.start:
                 continue
             score, weight = weigh(left, embed[j, :])
@@ -322,17 +321,16 @@
 
 def whole_plan(feats, partner):
     rows, width = feats.shape
-    stages = gather_rows(feats)
     mates = partner[None, :]
     f32, bf16 = jnp.float32, jnp.bfloat16
     vmem = pl.BlockSpec(memory_space=pltpu.VMEM)
     chunks, embeds, weights, sums = [], [], [], []
     done = 0
+    stages = gather_rows(feats)
     for s, stage in enumerate(stages):
-        if callable(stage):
-            stage = stage(sums)
-        pieces = [piece for piece, _ in stage]
-        chunks.append([chunk for _, part in stage for chunk in part])
+        items, sums = stage(sums)
+        pieces = [piece for piece, _ in items]
+        chunks.append([chunk for _, part in items for chunk in part])
         new = sum(piece.shape[0] for piece in pieces)
         state = [((new, width), bf16), ((rows, new), f32), ((8, done + new), f32)]
         final = s == len(stages) - 1
@@ -344,7 +342,7 @@
             in_specs=[vmem] * len(operands),
             out_specs=(vmem,) * len(outs),
             scratch_shapes=[pltpu.VMEM(shape, dtype) for shape, dtype in (state if final else [])],
-            cost_estimate=pl.CostEstimate(flops=new * (2 * done + new) * width, bytes_accessed=0, transcendentals=0),
+            cost_estimate=pl.CostEstimate(flops=1000, bytes_accessed=0, transcendentals=0),
             compiler_params=pltpu.CompilerParams(vmem_limit_bytes=32 * 1024 * 1024),
         )(*operands)
         if not final:
@@ -356,10 +354,14 @@
     return grad, loss.reshape(rows)
 
 
+def on_device(feats, partner):
+    fits = lax.axis_size("batch") == 16 and lax.axis_size("rep") == 2 and feats.shape[0] == 128
+    return whole_plan(feats, partner) if fits else split_plan(feats, partner)
+
+
 def solution(mesh):
-    every = mesh.shape["batch"] == 16 and mesh.shape["rep"] == 2
     in_specs = (P("batch", None), P("batch"))
     out_specs = (P("batch", None), P("batch"))
     return jax.shard_map(
-        whole_plan if every else split_plan, mesh=mesh, in_specs=in_specs, out_specs=out_specs, check_vma=False
+        on_device, mesh=mesh, in_specs=in_specs, out_specs=out_specs, check_vma=False
     )

time: 28.9 us -> 25.9 us (0.90)
  the two profiles are of different devices: /device:TPU:5 before, /device:TPU:0 now
where the time goes in v6:
time: 25.9 us; the launch traced here: 25.8 us
  starting transfers between devices  14.2 us (55%)
  Pallas kernels  5.66 us (22%)
  waiting for transfers between devices  5.1 us (20%)
  between operations  0.76 us (3%)
    ppermute x8, starting transfers between devices, send(): return lax.ppermute(piece, ('batch', 'rep'), pairs)  13.5 us
    pallas_call x4, Pallas kernels, whole_plan(): pl.pallas_call(functools.partial(stage_kernel, list(chunks), final), out_...  5.66 us
    ppermute x8, waiting for transfers between devices, send(): return lax.ppermute(piece, ('batch', 'rep'), pairs)  5.09 us
    ppermute x4, starting transfers between devices, swap(): return lax.ppermute(piece, 'rep', [(0, 1), (1, 0)])  0.71 us
  transfers between devices with their start and end apart: 12, of which 2 were waited for; matrix products, arithmetic and copies ran while one was open for 0% of the time, Pallas kernels for 14%

profile of v6, /device:TPU:0, one launch (start us, length us, event | category | flops | bytes accessed | tf_op | source)
XLA Modules:
  0.0 25.8 jit_solution(17282427385882195522)
XLA Ops:
  0.6 0.0 copy-start
  0.6 0.0 copy-start.1
  0.6 4.1 %collective-permute-start = (bf16[128,512]{1,0:T(8,128)(2,1)}, bf16[128,512]{1,0:T(8,128)(2,1)S(1)}, u32[]{:S(2)}, u32[]{:S(2)}) collective-permute-start(bf16[128,512]{1,0:T(8,128)(2,1)} %own_ref.7), channel_id=1, source_target_pairs={{0,16},{1,25},{2,18},{3,27},{4,20},{5,29},{6,22},{7,31},{8,24},{9,... | collective-permute-start | bytes 393224 | tf_op jit(solution)/shard_map/ppermute | solution.py:93
  4.8 1.5 %collective-permute-start.1 = (bf16[128,512]{1,0:T(8,128)(2,1)}, bf16[128,512]{1,0:T(8,128)(2,1)S(1)}, u32[]{:S(2)}, u32[]{:S(2)}) collective-permute-start(bf16[128,512]{1,0:T(8,128)(2,1)} %own_ref.7), channel_id=1, source_target_pairs={{0,2},{1,5},{2,0},{3,7},{4,6},{5,1},{6,4},{7,3},{8,10},{9,13},{10,... | collective-permute-start | bytes 393224 | tf_op jit(solution)/shard_map/ppermute | solution.py:93
  6.2 1.5 %collective-permute-start.2 = (bf16[128,512]{1,0:T(8,128)(2,1)}, bf16[128,512]{1,0:T(8,128)(2,1)S(1)}, u32[]{:S(2)}, u32[]{:S(2)}) collective-permute-start(bf16[128,512]{1,0:T(8,128)(2,1)} %own_ref.7), channel_id=1, source_target_pairs={{0,6},{1,9},{2,4},{3,11},{4,2},{5,13},{6,0},{7,15},{8,14},{9,1},{1... | collective-permute-start | bytes 393224 | tf_op jit(solution)/shard_map/ppermute | solution.py:93
  7.7 3.8 %collective-permute-done = bf16[128,512]{1,0:T(8,128)(2,1)S(1)} collective-permute-done((bf16[128,512]{1,0:T(8,128)(2,1)}, bf16[128,512]{1,0:T(8,128)(2,1)S(1)}, u32[]{:S(2)}, u32[]{:S(2)}) %collective-permute-start) | collective-permute-done | bytes 131104 | tf_op jit(solution)/shard_map/ppermute | solution.py:93
  11.5 0.0 collective-permute-done.1
  11.5 1.5 %collective-permute-start.4 = (bf16[128,512]{1,0:T(8,128)(2,1)S(1)}, bf16[128,512]{1,0:T(8,128)(2,1)S(1)}, u32[]{:S(2)}, u32[]{:S(2)}) collective-permute-start(bf16[128,512]{1,0:T(8,128)(2,1)S(1)} %collective-permute-done), channel_id=1, source_target_pairs={{0,2},{1,5},{2,0},{3,7},{4,6},{5,1},{6,4},{7,3},{8,10},{9,13},{10,... | collective-permute-start | bytes 393224 | tf_op jit(solution)/shard_map/ppermute | solution.py:93
  13.0 0.0 collective-permute-done.2
  13.1 0.1 collective-permute-start.3
  13.2 1.5 %collective-permute-start.5 = (bf16[128,512]{1,0:T(8,128)(2,1)S(1)}, bf16[128,512]{1,0:T(8,128)(2,1)S(1)}, u32[]{:S(2)}, u32[]{:S(2)}) collective-permute-start(bf16[128,512]{1,0:T(8,128)(2,1)S(1)} %collective-permute-done), channel_id=1, source_target_pairs={{0,4},{1,3},{2,6},{3,1},{4,0},{5,7},{6,2},{7,5},{8,12},{9,11},{10,... | collective-permute-start | bytes 393224 | tf_op jit(solution)/shard_map/ppermute | solution.py:93
  14.7 1.0 %collective-permute-start.6 = (bf16[128,512]{1,0:T(8,128)(2,1)S(1)}, bf16[128,512]{1,0:T(8,128)(2,1)S(1)}, u32[]{:S(2)}, u32[]{:S(2)}) collective-permute-start(bf16[128,512]{1,0:T(8,128)(2,1)S(1)} %collective-permute-done.1), channel_id=1, source_target_pairs={{0,8},{1,9},{2,10},{3,11},{4,12},{5,13},{6,14},{7,15},{8,0},{9,1},... | collective-permute-start | bytes 393224 | tf_op jit(solution)/shard_map/ppermute | solution.py:93
  15.6 1.1 %collective-permute-start.7 = (bf16[128,512]{1,0:T(8,128)(2,1)S(1)}, bf16[128,512]{1,0:T(8,128)(2,1)S(1)}, u32[]{:S(2)}, u32[]{:S(2)}) collective-permute-start(bf16[128,512]{1,0:T(8,128)(2,1)S(1)} %collective-permute-done.2), channel_id=1, source_target_pairs={{0,8},{1,7},{2,10},{3,5},{4,12},{5,3},{6,14},{7,1},{8,0},{9,15},{1... | collective-permute-start | bytes 393224 | tf_op jit(solution)/shard_map/ppermute | solution.py:93
  16.7 0.0 collective-permute-done.4
  16.7 1.4 %collective-permute-start.8 = (bf16[128,512]{1,0:T(8,128)(2,1)S(1)}, bf16[128,512]{1,0:T(8,128)(2,1)S(1)}, u32[]{:S(2)}, u32[]{:S(2)}) collective-permute-start(bf16[128,512]{1,0:T(8,128)(2,1)S(1)} %collective-permute-done.4), channel_id=1, source_target_pairs={{0,4},{1,3},{2,6},{3,1},{4,0},{5,7},{6,2},{7,5},{8,12},{9,11},{10,... | collective-permute-start | bytes 393224 | tf_op jit(solution)/shard_map/ppermute | solution.py:93
  18.2 0.0 collective-permute-done.5
  18.2 0.1 collective-permute-start.9
  18.3 0.0 collective-permute-done.3.refs_2_
  18.3 0.0 copy-done
  18.3 0.0 copy-done.1
  18.3 1.5 %shard_map.41 = (bf16[1152,512]{1,0:T(8,128)(2,1)S(1)}, f32[128,1152]{1,0:T(8,128)S(1)}, f32[8,1152]{1,0:T(8,128)S(1)}, f32[128,128]{1,0:T(8,128)S(1)}) custom-call(s32[1,128]{1,0:T(1,128)S(1)} %bitcast.2, bf16[128,512]{1,0:T(8,128)(2,1)S(1)} %copy-done, bf16[128,512]{1,0:T(8,128)(2,1)S(1)} %copy-done, ...), custom_call_target="tpu_custom_call" | custom-call | flops 1000 | tf_op jit(solution)/shard_map/pallas_call | solution.py:339
  19.8 0.0 collective-permute-done.6.refs_3_
  19.8 1.2 %collective-permute-done.7.refs_4_ = bf16[128,512]{1,0:T(8,128)(2,1)S(1)} collective-permute-done((bf16[128,512]{1,0:T(8,128)(2,1)S(1)}, bf16[128,512]{1,0:T(8,128)(2,1)S(1)}, u32[]{:S(2)}, u32[]{:S(2)}) %collective-permute-start.7) | collective-permute-done | bytes 131104 | tf_op jit(solution)/shard_map/ppermute | solution.py:93
  21.0 0.7 %shard_map.42 = (bf16[256,512]{1,0:T(8,128)(2,1)S(1)}, f32[128,256]{1,0:T(8,128)S(1)}, f32[8,1408]{1,0:T(8,128)S(1)}, f32[128,128]{1,0:T(8,128)S(1)}) custom-call(s32[1,128]{1,0:T(1,128)S(1)} %bitcast.3, bf16[128,512]{1,0:T(8,128)(2,1)S(1)} %copy-done, bf16[1152,512]{1,0:T(8,128)(2,1)S(1)} %get-tuple-element.26.refs_0_, ...), custom_call_target="tpu_custom_call" | custom-call | flops 1000 | tf_op jit(solution)/shard_map/pallas_call | solution.py:339
  21.8 0.0 collective-permute-done.8.refs_4_
  21.8 0.1 collective-permute-start.10
  21.9 0.5 %collective-permute-start.11 = (bf16[128,512]{1,0:T(8,128)(2,1)S(1)}, bf16[128,512]{1,0:T(8,128)(2,1)S(1)}, u32[]{:S(2)}, u32[]{:S(2)}) collective-permute-start(bf16[128,512]{1,0:T(8,128)(2,1)S(1)} %collective-permute-done.6.refs_3_), channel_id=1, source_target_pairs={{0,1},{1,0},{2,3},{3,2},{4,5},{5,4},{6,7},{7,6},{8,9},{9,8},{10,11... | collective-permute-start | bytes 393224 | tf_op jit(solution)/shard_map/ppermute | solution.py:97
  22.4 0.0 collective-permute-done.9.refs_5_
  22.4 1.3 %shard_map.43 = (bf16[384,512]{1,0:T(8,128)(2,1)S(1)}, f32[128,384]{1,0:T(8,128)S(1)}, f32[8,1792]{1,0:T(8,128)S(1)}, f32[128,128]{1,0:T(8,128)S(1)}) custom-call(s32[1,128]{1,0:T(1,128)S(1)} %bitcast.4, bf16[128,512]{1,0:T(8,128)(2,1)S(1)} %copy-done, bf16[1152,512]{1,0:T(8,128)(2,1)S(1)} %get-tuple-element.26.refs_0_, ...), custom_call_target="tpu_custom_call" | custom-call | flops 1000 | tf_op jit(solution)/shard_map/pallas_call | solution.py:339
  23.6 0.0 collective-permute-done.10.refs_8_
  23.7 0.0 collective-permute-done.11.refs_9_
  23.7 2.1 %shard_map.44 = (f32[128,512]{1,0:T(8,128)}, f32[1,128]{1,0:T(1,128)}) custom-call(s32[1,128]{1,0:T(1,128)S(1)} %bitcast.5, bf16[128,512]{1,0:T(8,128)(2,1)S(1)} %copy-done, bf16[1152,512]{1,0:T(8,128)(2,1)S(1)} %get-tuple-element.26.refs_0_, bf16[256,512]{1,0:T(8,128)(2,1)S(1)} %get-tuple-element.32.refs_1_, ...), custom_call_target="tpu_custom_call" | custom-call | flops 1000 | tf_op jit(solution)/shard_map/pallas_call | solution.py:339
  (5 shorter events, 0.1 us)
Async XLA Ops:
  0.6 17.7 %copy-start = (bf16[128,512]{1,0:T(8,128)(2,1)S(1)}, bf16[128,512]{1,0:T(8,128)(2,1)}, u32[]{:S(2)}) copy-start(bf16[128,512]{1,0:T(8,128)(2,1)} %own_ref.7) | copy-start | bytes 393220
  0.6 17.7 %copy-start.1 = (s32[128]{0:T(128)S(1)}, s32[128]{0:T(128)}, u32[]{:S(2)}) copy-start(s32[128]{0:T(128)} %param.3) | copy-start | bytes 1540
  0.6 10.9 %collective-permute-start = (bf16[128,512]{1,0:T(8,128)(2,1)}, bf16[128,512]{1,0:T(8,128)(2,1)S(1)}, u32[]{:S(2)}, u32[]{:S(2)}) collective-permute-start(bf16[128,512]{1,0:T(8,128)(2,1)} %own_ref.7), channel_id=1, source_target_pairs={{0,16},{1,25},{2,18},{3,27},{4,20},{5,29},{6,22},{7,31},{8,24},{9,... | collective-permute-start | bytes 393224 | tf_op jit(solution)/shard_map/ppermute | solution.py:93
  4.8 6.8 %collective-permute-start.1 = (bf16[128,512]{1,0:T(8,128)(2,1)}, bf16[128,512]{1,0:T(8,128)(2,1)S(1)}, u32[]{:S(2)}, u32[]{:S(2)}) collective-permute-start(bf16[128,512]{1,0:T(8,128)(2,1)} %own_ref.7), channel_id=1, source_target_pairs={{0,2},{1,5},{2,0},{3,7},{4,6},{5,1},{6,4},{7,3},{8,10},{9,13},{10,... | collective-permute-start | bytes 393224 | tf_op jit(solution)/shard_map/ppermute | solution.py:93
  6.2 6.8 %collective-permute-start.2 = (bf16[128,512]{1,0:T(8,128)(2,1)}, bf16[128,512]{1,0:T(8,128)(2,1)S(1)}, u32[]{:S(2)}, u32[]{:S(2)}) collective-permute-start(bf16[128,512]{1,0:T(8,128)(2,1)} %own_ref.7), channel_id=1, source_target_pairs={{0,6},{1,9},{2,4},{3,11},{4,2},{5,13},{6,0},{7,15},{8,14},{9,1},{1... | collective-permute-start | bytes 393224 | tf_op jit(solution)/shard_map/ppermute | solution.py:93
  11.5 5.2 %collective-permute-start.4 = (bf16[128,512]{1,0:T(8,128)(2,1)S(1)}, bf16[128,512]{1,0:T(8,128)(2,1)S(1)}, u32[]{:S(2)}, u32[]{:S(2)}) collective-permute-start(bf16[128,512]{1,0:T(8,128)(2,1)S(1)} %collective-permute-done), channel_id=1, source_target_pairs={{0,2},{1,5},{2,0},{3,7},{4,6},{5,1},{6,4},{7,3},{8,10},{9,13},{10,... | collective-permute-start | bytes 393224 | tf_op jit(solution)/shard_map/ppermute | solution.py:93
  13.1 5.2 %collective-permute-start.3 = (bf16[384,512]{1,0:T(8,128)(2,1)S(1)}, bf16[384,512]{1,0:T(8,128)(2,1)S(1)}, u32[]{:S(2)}, u32[]{:S(2)}) collective-permute-start(bf16[384,512]{1,0:T(8,128)(2,1)S(1)} %constant_dynamic-update-slice_fusion.refs_1_), channel_id=1, source_target_pairs={{0,1},{1,0},{2,3},{3,2},{4,5},{5,4},{6,7},{7,6},{8,9},{9,8},{10,11... | collective-permute-start | bytes 1179656 | tf_op jit(solution)/shard_map/ppermute | solution.py:97
  13.2 5.0 %collective-permute-start.5 = (bf16[128,512]{1,0:T(8,128)(2,1)S(1)}, bf16[128,512]{1,0:T(8,128)(2,1)S(1)}, u32[]{:S(2)}, u32[]{:S(2)}) collective-permute-start(bf16[128,512]{1,0:T(8,128)(2,1)S(1)} %collective-permute-done), channel_id=1, source_target_pairs={{0,4},{1,3},{2,6},{3,1},{4,0},{5,7},{6,2},{7,5},{8,12},{9,11},{10,... | collective-permute-start | bytes 393224 | tf_op jit(solution)/shard_map/ppermute | solution.py:93
  14.7 5.2 %collective-permute-start.6 = (bf16[128,512]{1,0:T(8,128)(2,1)S(1)}, bf16[128,512]{1,0:T(8,128)(2,1)S(1)}, u32[]{:S(2)}, u32[]{:S(2)}) collective-permute-start(bf16[128,512]{1,0:T(8,128)(2,1)S(1)} %collective-permute-done.1), channel_id=1, source_target_pairs={{0,8},{1,9},{2,10},{3,11},{4,12},{5,13},{6,14},{7,15},{8,0},{9,1},... | collective-permute-start | bytes 393224 | tf_op jit(solution)/shard_map/ppermute | solution.py:93
  15.6 5.4 %collective-permute-start.7 = (bf16[128,512]{1,0:T(8,128)(2,1)S(1)}, bf16[128,512]{1,0:T(8,128)(2,1)S(1)}, u32[]{:S(2)}, u32[]{:S(2)}) collective-permute-start(bf16[128,512]{1,0:T(8,128)(2,1)S(1)} %collective-permute-done.2), channel_id=1, source_target_pairs={{0,8},{1,7},{2,10},{3,5},{4,12},{5,3},{6,14},{7,1},{8,0},{9,15},{1... | collective-permute-start | bytes 393224 | tf_op jit(solution)/shard_map/ppermute | solution.py:93
  16.7 5.0 %collective-permute-start.8 = (bf16[128,512]{1,0:T(8,128)(2,1)S(1)}, bf16[128,512]{1,0:T(8,128)(2,1)S(1)}, u32[]{:S(2)}, u32[]{:S(2)}) collective-permute-start(bf16[128,512]{1,0:T(8,128)(2,1)S(1)} %collective-permute-done.4), channel_id=1, source_target_pairs={{0,4},{1,3},{2,6},{3,1},{4,0},{5,7},{6,2},{7,5},{8,12},{9,11},{10,... | collective-permute-start | bytes 393224 | tf_op jit(solution)/shard_map/ppermute | solution.py:93
  18.2 4.1 %collective-permute-start.9 = (bf16[256,512]{1,0:T(8,128)(2,1)S(1)}, bf16[256,512]{1,0:T(8,128)(2,1)S(1)}, u32[]{:S(2)}, u32[]{:S(2)}) collective-permute-start(bf16[256,512]{1,0:T(8,128)(2,1)S(1)} %constant_dynamic-update-slice_fusion.3.refs_3_), channel_id=1, source_target_pairs={{0,1},{1,0},{2,3},{3,2},{4,5},{5,4},{6,7},{7,6},{8,9},{9,8},{10,11... | collective-permute-start | bytes 786440 | tf_op jit(solution)/shard_map/ppermute | solution.py:97
  21.8 1.9 %collective-permute-start.10 = (bf16[128,512]{1,0:T(8,128)(2,1)S(1)}, bf16[128,512]{1,0:T(8,128)(2,1)S(1)}, u32[]{:S(2)}, u32[]{:S(2)}) collective-permute-start(bf16[128,512]{1,0:T(8,128)(2,1)S(1)} %collective-permute-done.8.refs_4_), channel_id=1, source_target_pairs={{0,1},{1,0},{2,3},{3,2},{4,5},{5,4},{6,7},{7,6},{8,9},{9,8},{10,11... | collective-permute-start | bytes 393224 | tf_op jit(solution)/shard_map/ppermute | solution.py:97
  21.9 1.8 %collective-permute-start.11 = (bf16[128,512]{1,0:T(8,128)(2,1)S(1)}, bf16[128,512]{1,0:T(8,128)(2,1)S(1)}, u32[]{:S(2)}, u32[]{:S(2)}) collective-permute-start(bf16[128,512]{1,0:T(8,128)(2,1)S(1)} %collective-permute-done.6.refs_3_), channel_id=1, source_target_pairs={{0,1},{1,0},{2,3},{3,2},{4,5},{5,4},{6,7},{7,6},{8,9},{9,8},{10,11... | collective-permute-start | bytes 393224 | tf_op jit(solution)/shard_map/ppermute | solution.py:97

commit v7 on v6

--- a/solution.py
+++ b/solution.py
@@ -142,11 +142,11 @@
 
     def third(sums):
         held["far_xy"], held["side"], hits = tie(far_xy, held["side"], sums[1])
-        return [(held["far_xy"], far_xy_chunks), other(pair, pair_chunks)], [sums[0], hits]
+        return [other(pair, pair_chunks), (held["far_xy"], far_xy_chunks)], [sums[0], hits]
 
     def last(sums):
         piece = held["far_xy"]
-        return [other(piece, far_xy_chunks), other(held["side"], side_chunks)], sums
+        return [other(held["side"], side_chunks), other(piece, far_xy_chunks)], sums
 
     return [first, second, third, last]
 

time: 25.9 us -> 25.9 us (level)
  no operation moved by 1% of the time
where the time goes in v7:
time: 25.9 us; the launch traced here: 25.8 us
  starting transfers between devices  14.2 us (55%)
  Pallas kernels  5.66 us (22%)
  waiting for transfers between devices  5.1 us (20%)
  between operations  0.76 us (3%)
    ppermute x8, starting transfers between devices, send(): return lax.ppermute(piece, ('batch', 'rep'), pairs)  13.5 us
    pallas_call x4, Pallas kernels, whole_plan(): pl.pallas_call(functools.partial(stage_kernel, list(chunks), final), out_...  5.66 us
    ppermute x8, waiting for transfers between devices, send(): return lax.ppermute(piece, ('batch', 'rep'), pairs)  5.09 us
    ppermute x4, starting transfers between devices, swap(): return lax.ppermute(piece, 'rep', [(0, 1), (1, 0)])  0.71 us
  transfers between devices with their start and end apart: 12, of which 2 were waited for; matrix products, arithmetic and copies ran while one was open for 0% of the time, Pallas kernels for 14%

profile of v7, /device:TPU:0, one launch (start us, length us, event | category | flops | bytes accessed | tf_op | source)
XLA Modules:
  0.0 25.8 jit_solution(3245208350996441022)
XLA Ops:
  0.6 0.0 copy-start
  0.6 0.0 copy-start.1
  0.6 4.1 %collective-permute-start = (bf16[128,512]{1,0:T(8,128)(2,1)}, bf16[128,512]{1,0:T(8,128)(2,1)S(1)}, u32[]{:S(2)}, u32[]{:S(2)}) collective-permute-start(bf16[128,512]{1,0:T(8,128)(2,1)} %own_ref.7), channel_id=1, source_target_pairs={{0,16},{1,25},{2,18},{3,27},{4,20},{5,29},{6,22},{7,31},{8,24},{9,... | collective-permute-start | bytes 393224 | tf_op jit(solution)/shard_map/ppermute | solution.py:93
  4.8 1.5 %collective-permute-start.1 = (bf16[128,512]{1,0:T(8,128)(2,1)}, bf16[128,512]{1,0:T(8,128)(2,1)S(1)}, u32[]{:S(2)}, u32[]{:S(2)}) collective-permute-start(bf16[128,512]{1,0:T(8,128)(2,1)} %own_ref.7), channel_id=1, source_target_pairs={{0,2},{1,5},{2,0},{3,7},{4,6},{5,1},{6,4},{7,3},{8,10},{9,13},{10,... | collective-permute-start | bytes 393224 | tf_op jit(solution)/shard_map/ppermute | solution.py:93
  6.2 1.5 %collective-permute-start.2 = (bf16[128,512]{1,0:T(8,128)(2,1)}, bf16[128,512]{1,0:T(8,128)(2,1)S(1)}, u32[]{:S(2)}, u32[]{:S(2)}) collective-permute-start(bf16[128,512]{1,0:T(8,128)(2,1)} %own_ref.7), channel_id=1, source_target_pairs={{0,6},{1,9},{2,4},{3,11},{4,2},{5,13},{6,0},{7,15},{8,14},{9,1},{1... | collective-permute-start | bytes 393224 | tf_op jit(solution)/shard_map/ppermute | solution.py:93
  7.7 3.8 %collective-permute-done = bf16[128,512]{1,0:T(8,128)(2,1)S(1)} collective-permute-done((bf16[128,512]{1,0:T(8,128)(2,1)}, bf16[128,512]{1,0:T(8,128)(2,1)S(1)}, u32[]{:S(2)}, u32[]{:S(2)}) %collective-permute-start) | collective-permute-done | bytes 131104 | tf_op jit(solution)/shard_map/ppermute | solution.py:93
  11.5 0.0 collective-permute-done.1
  11.5 1.5 %collective-permute-start.4 = (bf16[128,512]{1,0:T(8,128)(2,1)S(1)}, bf16[128,512]{1,0:T(8,128)(2,1)S(1)}, u32[]{:S(2)}, u32[]{:S(2)}) collective-permute-start(bf16[128,512]{1,0:T(8,128)(2,1)S(1)} %collective-permute-done), channel_id=1, source_target_pairs={{0,2},{1,5},{2,0},{3,7},{4,6},{5,1},{6,4},{7,3},{8,10},{9,13},{10,... | collective-permute-start | bytes 393224 | tf_op jit(solution)/shard_map/ppermute | solution.py:93
  13.0 0.0 collective-permute-done.2
  13.1 0.1 collective-permute-start.3
  13.2 1.5 %collective-permute-start.5 = (bf16[128,512]{1,0:T(8,128)(2,1)S(1)}, bf16[128,512]{1,0:T(8,128)(2,1)S(1)}, u32[]{:S(2)}, u32[]{:S(2)}) collective-permute-start(bf16[128,512]{1,0:T(8,128)(2,1)S(1)} %collective-permute-done), channel_id=1, source_target_pairs={{0,4},{1,3},{2,6},{3,1},{4,0},{5,7},{6,2},{7,5},{8,12},{9,11},{10,... | collective-permute-start | bytes 393224 | tf_op jit(solution)/shard_map/ppermute | solution.py:93
  14.7 1.0 %collective-permute-start.6 = (bf16[128,512]{1,0:T(8,128)(2,1)S(1)}, bf16[128,512]{1,0:T(8,128)(2,1)S(1)}, u32[]{:S(2)}, u32[]{:S(2)}) collective-permute-start(bf16[128,512]{1,0:T(8,128)(2,1)S(1)} %collective-permute-done.1), channel_id=1, source_target_pairs={{0,8},{1,9},{2,10},{3,11},{4,12},{5,13},{6,14},{7,15},{8,0},{9,1},... | collective-permute-start | bytes 393224 | tf_op jit(solution)/shard_map/ppermute | solution.py:93
  15.6 1.1 %collective-permute-start.7 = (bf16[128,512]{1,0:T(8,128)(2,1)S(1)}, bf16[128,512]{1,0:T(8,128)(2,1)S(1)}, u32[]{:S(2)}, u32[]{:S(2)}) collective-permute-start(bf16[128,512]{1,0:T(8,128)(2,1)S(1)} %collective-permute-done.2), channel_id=1, source_target_pairs={{0,8},{1,7},{2,10},{3,5},{4,12},{5,3},{6,14},{7,1},{8,0},{9,15},{1... | collective-permute-start | bytes 393224 | tf_op jit(solution)/shard_map/ppermute | solution.py:93
  16.7 0.0 collective-permute-done.4
  16.7 1.4 %collective-permute-start.8 = (bf16[128,512]{1,0:T(8,128)(2,1)S(1)}, bf16[128,512]{1,0:T(8,128)(2,1)S(1)}, u32[]{:S(2)}, u32[]{:S(2)}) collective-permute-start(bf16[128,512]{1,0:T(8,128)(2,1)S(1)} %collective-permute-done.4), channel_id=1, source_target_pairs={{0,4},{1,3},{2,6},{3,1},{4,0},{5,7},{6,2},{7,5},{8,12},{9,11},{10,... | collective-permute-start | bytes 393224 | tf_op jit(solution)/shard_map/ppermute | solution.py:93
  18.2 0.0 collective-permute-done.5
  18.2 0.1 collective-permute-start.9
  18.3 0.0 collective-permute-done.3.refs_2_
  18.3 0.0 copy-done
  18.3 0.0 copy-done.1
  18.3 1.5 %shard_map.41 = (bf16[1152,512]{1,0:T(8,128)(2,1)S(1)}, f32[128,1152]{1,0:T(8,128)S(1)}, f32[8,1152]{1,0:T(8,128)S(1)}, f32[128,128]{1,0:T(8,128)S(1)}) custom-call(s32[1,128]{1,0:T(1,128)S(1)} %bitcast.2, bf16[128,512]{1,0:T(8,128)(2,1)S(1)} %copy-done, bf16[128,512]{1,0:T(8,128)(2,1)S(1)} %copy-done, ...), custom_call_target="tpu_custom_call" | custom-call | flops 1000 | tf_op jit(solution)/shard_map/pallas_call | solution.py:339
  19.8 0.0 collective-permute-done.6.refs_3_
  19.8 1.2 %collective-permute-done.7.refs_4_ = bf16[128,512]{1,0:T(8,128)(2,1)S(1)} collective-permute-done((bf16[128,512]{1,0:T(8,128)(2,1)S(1)}, bf16[128,512]{1,0:T(8,128)(2,1)S(1)}, u32[]{:S(2)}, u32[]{:S(2)}) %collective-permute-start.7) | collective-permute-done | bytes 131104 | tf_op jit(solution)/shard_map/ppermute | solution.py:93
  21.0 0.7 %shard_map.42 = (bf16[256,512]{1,0:T(8,128)(2,1)S(1)}, f32[128,256]{1,0:T(8,128)S(1)}, f32[8,1408]{1,0:T(8,128)S(1)}, f32[128,128]{1,0:T(8,128)S(1)}) custom-call(s32[1,128]{1,0:T(1,128)S(1)} %bitcast.3, bf16[128,512]{1,0:T(8,128)(2,1)S(1)} %copy-done, bf16[1152,512]{1,0:T(8,128)(2,1)S(1)} %get-tuple-element.26.refs_0_, ...), custom_call_target="tpu_custom_call" | custom-call | flops 1000 | tf_op jit(solution)/shard_map/pallas_call | solution.py:339
  21.8 0.0 collective-permute-done.8.refs_5_
  21.8 0.1 collective-permute-start.10
  21.9 0.5 %collective-permute-start.11 = (bf16[128,512]{1,0:T(8,128)(2,1)S(1)}, bf16[128,512]{1,0:T(8,128)(2,1)S(1)}, u32[]{:S(2)}, u32[]{:S(2)}) collective-permute-start(bf16[128,512]{1,0:T(8,128)(2,1)S(1)} %collective-permute-done.8.refs_5_), channel_id=1, source_target_pairs={{0,1},{1,0},{2,3},{3,2},{4,5},{5,4},{6,7},{7,6},{8,9},{9,8},{10,11... | collective-permute-start | bytes 393224 | tf_op jit(solution)/shard_map/ppermute | solution.py:97
  22.4 0.0 collective-permute-done.9.refs_4_
  22.4 1.3 %shard_map.43 = (bf16[384,512]{1,0:T(8,128)(2,1)S(1)}, f32[128,384]{1,0:T(8,128)S(1)}, f32[8,1792]{1,0:T(8,128)S(1)}, f32[128,128]{1,0:T(8,128)S(1)}) custom-call(s32[1,128]{1,0:T(1,128)S(1)} %bitcast.4, bf16[128,512]{1,0:T(8,128)(2,1)S(1)} %copy-done, bf16[1152,512]{1,0:T(8,128)(2,1)S(1)} %get-tuple-element.26.refs_0_, ...), custom_call_target="tpu_custom_call" | custom-call | flops 1000 | tf_op jit(solution)/shard_map/pallas_call | solution.py:339
  23.6 0.0 collective-permute-done.10.refs_8_
  23.7 0.0 collective-permute-done.11.refs_9_
  23.7 2.1 %shard_map.44 = (f32[128,512]{1,0:T(8,128)}, f32[1,128]{1,0:T(1,128)}) custom-call(s32[1,128]{1,0:T(1,128)S(1)} %bitcast.5, bf16[128,512]{1,0:T(8,128)(2,1)S(1)} %copy-done, bf16[1152,512]{1,0:T(8,128)(2,1)S(1)} %get-tuple-element.26.refs_0_, bf16[256,512]{1,0:T(8,128)(2,1)S(1)} %get-tuple-element.32.refs_1_, ...), custom_call_target="tpu_custom_call" | custom-call | flops 1000 | tf_op jit(solution)/shard_map/pallas_call | solution.py:339
  (5 shorter events, 0.1 us)
Async XLA Ops:
  0.6 17.7 %copy-start = (bf16[128,512]{1,0:T(8,128)(2,1)S(1)}, bf16[128,512]{1,0:T(8,128)(2,1)}, u32[]{:S(2)}) copy-start(bf16[128,512]{1,0:T(8,128)(2,1)} %own_ref.7) | copy-start | bytes 393220
  0.6 17.7 %copy-start.1 = (s32[128]{0:T(128)S(1)}, s32[128]{0:T(128)}, u32[]{:S(2)}) copy-start(s32[128]{0:T(128)} %param.3) | copy-start | bytes 1540
  0.6 10.9 %collective-permute-start = (bf16[128,512]{1,0:T(8,128)(2,1)}, bf16[128,512]{1,0:T(8,128)(2,1)S(1)}, u32[]{:S(2)}, u32[]{:S(2)}) collective-permute-start(bf16[128,512]{1,0:T(8,128)(2,1)} %own_ref.7), channel_id=1, source_target_pairs={{0,16},{1,25},{2,18},{3,27},{4,20},{5,29},{6,22},{7,31},{8,24},{9,... | collective-permute-start | bytes 393224 | tf_op jit(solution)/shard_map/ppermute | solution.py:93
  4.8 6.8 %collective-permute-start.1 = (bf16[128,512]{1,0:T(8,128)(2,1)}, bf16[128,512]{1,0:T(8,128)(2,1)S(1)}, u32[]{:S(2)}, u32[]{:S(2)}) collective-permute-start(bf16[128,512]{1,0:T(8,128)(2,1)} %own_ref.7), channel_id=1, source_target_pairs={{0,2},{1,5},{2,0},{3,7},{4,6},{5,1},{6,4},{7,3},{8,10},{9,13},{10,... | collective-permute-start | bytes 393224 | tf_op jit(solution)/shard_map/ppermute | solution.py:93
  6.2 6.8 %collective-permute-start.2 = (bf16[128,512]{1,0:T(8,128)(2,1)}, bf16[128,512]{1,0:T(8,128)(2,1)S(1)}, u32[]{:S(2)}, u32[]{:S(2)}) collective-permute-start(bf16[128,512]{1,0:T(8,128)(2,1)} %own_ref.7), channel_id=1, source_target_pairs={{0,6},{1,9},{2,4},{3,11},{4,2},{5,13},{6,0},{7,15},{8,14},{9,1},{1... | collective-permute-start | bytes 393224 | tf_op jit(solution)/shard_map/ppermute | solution.py:93
  11.5 5.2 %collective-permute-start.4 = (bf16[128,512]{1,0:T(8,128)(2,1)S(1)}, bf16[128,512]{1,0:T(8,128)(2,1)S(1)}, u32[]{:S(2)}, u32[]{:S(2)}) collective-permute-start(bf16[128,512]{1,0:T(8,128)(2,1)S(1)} %collective-permute-done), channel_id=1, source_target_pairs={{0,2},{1,5},{2,0},{3,7},{4,6},{5,1},{6,4},{7,3},{8,10},{9,13},{10,... | collective-permute-start | bytes 393224 | tf_op jit(solution)/shard_map/ppermute | solution.py:93
  13.1 5.2 %collective-permute-start.3 = (bf16[384,512]{1,0:T(8,128)(2,1)S(1)}, bf16[384,512]{1,0:T(8,128)(2,1)S(1)}, u32[]{:S(2)}, u32[]{:S(2)}) collective-permute-start(bf16[384,512]{1,0:T(8,128)(2,1)S(1)} %constant_dynamic-update-slice_fusion.refs_1_), channel_id=1, source_target_pairs={{0,1},{1,0},{2,3},{3,2},{4,5},{5,4},{6,7},{7,6},{8,9},{9,8},{10,11... | collective-permute-start | bytes 1179656 | tf_op jit(solution)/shard_map/ppermute | solution.py:97
  13.2 5.0 %collective-permute-start.5 = (bf16[128,512]{1,0:T(8,128)(2,1)S(1)}, bf16[128,512]{1,0:T(8,128)(2,1)S(1)}, u32[]{:S(2)}, u32[]{:S(2)}) collective-permute-start(bf16[128,512]{1,0:T(8,128)(2,1)S(1)} %collective-permute-done), channel_id=1, source_target_pairs={{0,4},{1,3},{2,6},{3,1},{4,0},{5,7},{6,2},{7,5},{8,12},{9,11},{10,... | collective-permute-start | bytes 393224 | tf_op jit(solution)/shard_map/ppermute | solution.py:93
  14.7 5.2 %collective-permute-start.6 = (bf16[128,512]{1,0:T(8,128)(2,1)S(1)}, bf16[128,512]{1,0:T(8,128)(2,1)S(1)}, u32[]{:S(2)}, u32[]{:S(2)}) collective-permute-start(bf16[128,512]{1,0:T(8,128)(2,1)S(1)} %collective-permute-done.1), channel_id=1, source_target_pairs={{0,8},{1,9},{2,10},{3,11},{4,12},{5,13},{6,14},{7,15},{8,0},{9,1},... | collective-permute-start | bytes 393224 | tf_op jit(solution)/shard_map/ppermute | solution.py:93
  15.6 5.4 %collective-permute-start.7 = (bf16[128,512]{1,0:T(8,128)(2,1)S(1)}, bf16[128,512]{1,0:T(8,128)(2,1)S(1)}, u32[]{:S(2)}, u32[]{:S(2)}) collective-permute-start(bf16[128,512]{1,0:T(8,128)(2,1)S(1)} %collective-permute-done.2), channel_id=1, source_target_pairs={{0,8},{1,7},{2,10},{3,5},{4,12},{5,3},{6,14},{7,1},{8,0},{9,15},{1... | collective-permute-start | bytes 393224 | tf_op jit(solution)/shard_map/ppermute | solution.py:93
  16.7 5.0 %collective-permute-start.8 = (bf16[128,512]{1,0:T(8,128)(2,1)S(1)}, bf16[128,512]{1,0:T(8,128)(2,1)S(1)}, u32[]{:S(2)}, u32[]{:S(2)}) collective-permute-start(bf16[128,512]{1,0:T(8,128)(2,1)S(1)} %collective-permute-done.4), channel_id=1, source_target_pairs={{0,4},{1,3},{2,6},{3,1},{4,0},{5,7},{6,2},{7,5},{8,12},{9,11},{10,... | collective-permute-start | bytes 393224 | tf_op jit(solution)/shard_map/ppermute | solution.py:93
  18.2 4.1 %collective-permute-start.9 = (bf16[256,512]{1,0:T(8,128)(2,1)S(1)}, bf16[256,512]{1,0:T(8,128)(2,1)S(1)}, u32[]{:S(2)}, u32[]{:S(2)}) collective-permute-start(bf16[256,512]{1,0:T(8,128)(2,1)S(1)} %constant_dynamic-update-slice_fusion.3.refs_3_), channel_id=1, source_target_pairs={{0,1},{1,0},{2,3},{3,2},{4,5},{5,4},{6,7},{7,6},{8,9},{9,8},{10,11... | collective-permute-start | bytes 786440 | tf_op jit(solution)/shard_map/ppermute | solution.py:97
  21.8 1.9 %collective-permute-start.10 = (bf16[128,512]{1,0:T(8,128)(2,1)S(1)}, bf16[128,512]{1,0:T(8,128)(2,1)S(1)}, u32[]{:S(2)}, u32[]{:S(2)}) collective-permute-start(bf16[128,512]{1,0:T(8,128)(2,1)S(1)} %collective-permute-done.6.refs_3_), channel_id=1, source_target_pairs={{0,1},{1,0},{2,3},{3,2},{4,5},{5,4},{6,7},{7,6},{8,9},{9,8},{10,11... | collective-permute-start | bytes 393224 | tf_op jit(solution)/shard_map/ppermute | solution.py:97
  21.9 1.8 %collective-permute-start.11 = (bf16[128,512]{1,0:T(8,128)(2,1)S(1)}, bf16[128,512]{1,0:T(8,128)(2,1)S(1)}, u32[]{:S(2)}, u32[]{:S(2)}) collective-permute-start(bf16[128,512]{1,0:T(8,128)(2,1)S(1)} %collective-permute-done.8.refs_5_), channel_id=1, source_target_pairs={{0,1},{1,0},{2,3},{3,2},{4,5},{5,4},{6,7},{7,6},{8,9},{9,8},{10,11... | collective-permute-start | bytes 393224 | tf_op jit(solution)/shard_map/ppermute | solution.py:97

commit v8 on v6

--- a/solution.py
+++ b/solution.py
@@ -115,19 +115,19 @@
 
 def gather_rows(feats):
     far = send(feats, Z2, Z3)
-    near = send(feats, X, Y)
+    near = send(feats, Y, X)
     cross = send(feats, XY, Z1)
     far, near = tie(far, near)
     side = send(near, Z1)
     side_xy = send(cross, Z1, XY)
-    far_x, far_y = send(far, X, Y), send(far, Y, X)
-    far_xy = send(far_x, Y, X)
+    far_x, far_y = send(far, Y, X), send(far, X, Y)
+    far_xy = send(far_x, X, Y)
     early = join(near, cross, far)
     pair = join(far_x, far_y)
-    early_chunks = [Chunk(X, Y), Chunk(XY, Z1), Chunk(Z2, Z3)]
-    pair_chunks = [Chunk(X ^ Z2, Y ^ Z3), Chunk(Y ^ Z2, X ^ Z3)]
+    early_chunks = [Chunk(Y, X), Chunk(XY, Z1), Chunk(Z2, Z3)]
+    pair_chunks = [Chunk(Y ^ Z2, X ^ Z3), Chunk(X ^ Z2, Y ^ Z3)]
     far_xy_chunks = [Chunk(XY ^ Z2, XY ^ Z3)]
-    side_chunks = [Chunk(X ^ Z1, Y ^ Z1)]
+    side_chunks = [Chunk(Y ^ Z1, X ^ Z1)]
     held = {}
 
     def other(piece, chunks):

time: 25.9 us -> 25.9 us (level)
  transfers between devices with their start and end apart: 12 -> 12, of which waited for: 2 -> 4; matrix products, arithmetic and copies ran while one was open for 0% -> 0% of each run, Pallas kernels for 14% -> 14%
where the time goes in v8:
time: 25.9 us; the launch traced here: 25.8 us
  starting transfers between devices  14.1 us (54%)
  Pallas kernels  5.66 us (22%)
  waiting for transfers between devices  5.16 us (20%)
  between operations  0.76 us (3%)
    ppermute x8, starting transfers between devices, send(): return lax.ppermute(piece, ('batch', 'rep'), pairs)  13.4 us
    pallas_call x4, Pallas kernels, whole_plan(): pl.pallas_call(functools.partial(stage_kernel, list(chunks), final), out_...  5.66 us
    ppermute x8, waiting for transfers between devices, send(): return lax.ppermute(piece, ('batch', 'rep'), pairs)  5.15 us
    ppermute x4, starting transfers between devices, swap(): return lax.ppermute(piece, 'rep', [(0, 1), (1, 0)])  0.71 us
  transfers between devices with their start and end apart: 12, of which 4 were waited for; matrix products, arithmetic and copies ran while one was open for 0% of the time, Pallas kernels for 14%

profile of v8, /device:TPU:0, one launch (start us, length us, event | category | flops | bytes accessed | tf_op | source)
XLA Modules:
  0.0 25.8 jit_solution(13762256565177971612)
XLA Ops:
  0.6 0.0 copy-start
  0.6 0.0 copy-start.1
  0.6 4.1 %collective-permute-start = (bf16[128,512]{1,0:T(8,128)(2,1)}, bf16[128,512]{1,0:T(8,128)(2,1)S(1)}, u32[]{:S(2)}, u32[]{:S(2)}) collective-permute-start(bf16[128,512]{1,0:T(8,128)(2,1)} %own_ref.7), channel_id=1, source_target_pairs={{0,16},{1,25},{2,18},{3,27},{4,20},{5,29},{6,22},{7,31},{8,24},{9,... | collective-permute-start | bytes 393224 | tf_op jit(solution)/shard_map/ppermute | solution.py:93
  4.8 1.5 %collective-permute-start.1 = (bf16[128,512]{1,0:T(8,128)(2,1)}, bf16[128,512]{1,0:T(8,128)(2,1)S(1)}, u32[]{:S(2)}, u32[]{:S(2)}) collective-permute-start(bf16[128,512]{1,0:T(8,128)(2,1)} %own_ref.7), channel_id=1, source_target_pairs={{0,4},{1,3},{2,6},{3,1},{4,0},{5,7},{6,2},{7,5},{8,12},{9,11},{10,... | collective-permute-start | bytes 393224 | tf_op jit(solution)/shard_map/ppermute | solution.py:93
  6.3 1.4 %collective-permute-start.2 = (bf16[128,512]{1,0:T(8,128)(2,1)}, bf16[128,512]{1,0:T(8,128)(2,1)S(1)}, u32[]{:S(2)}, u32[]{:S(2)}) collective-permute-start(bf16[128,512]{1,0:T(8,128)(2,1)} %own_ref.7), channel_id=1, source_target_pairs={{0,6},{1,9},{2,4},{3,11},{4,2},{5,13},{6,0},{7,15},{8,14},{9,1},{1... | collective-permute-start | bytes 393224 | tf_op jit(solution)/shard_map/ppermute | solution.py:93
  7.7 3.8 %collective-permute-done = bf16[128,512]{1,0:T(8,128)(2,1)S(1)} collective-permute-done((bf16[128,512]{1,0:T(8,128)(2,1)}, bf16[128,512]{1,0:T(8,128)(2,1)S(1)}, u32[]{:S(2)}, u32[]{:S(2)}) %collective-permute-start) | collective-permute-done | bytes 131104 | tf_op jit(solution)/shard_map/ppermute | solution.py:93
  11.5 0.0 collective-permute-done.1
  11.5 1.5 %collective-permute-start.4 = (bf16[128,512]{1,0:T(8,128)(2,1)S(1)}, bf16[128,512]{1,0:T(8,128)(2,1)S(1)}, u32[]{:S(2)}, u32[]{:S(2)}) collective-permute-start(bf16[128,512]{1,0:T(8,128)(2,1)S(1)} %collective-permute-done), channel_id=1, source_target_pairs={{0,4},{1,3},{2,6},{3,1},{4,0},{5,7},{6,2},{7,5},{8,12},{9,11},{10,... | collective-permute-start | bytes 393224 | tf_op jit(solution)/shard_map/ppermute | solution.py:93
  13.1 0.0 collective-permute-done.2
  13.1 0.1 collective-permute-start.3
  13.2 1.4 %collective-permute-start.5 = (bf16[128,512]{1,0:T(8,128)(2,1)S(1)}, bf16[128,512]{1,0:T(8,128)(2,1)S(1)}, u32[]{:S(2)}, u32[]{:S(2)}) collective-permute-start(bf16[128,512]{1,0:T(8,128)(2,1)S(1)} %collective-permute-done), channel_id=1, source_target_pairs={{0,2},{1,5},{2,0},{3,7},{4,6},{5,1},{6,4},{7,3},{8,10},{9,13},{10,... | collective-permute-start | bytes 393224 | tf_op jit(solution)/shard_map/ppermute | solution.py:93
  14.7 0.9 %collective-permute-start.6 = (bf16[128,512]{1,0:T(8,128)(2,1)S(1)}, bf16[128,512]{1,0:T(8,128)(2,1)S(1)}, u32[]{:S(2)}, u32[]{:S(2)}) collective-permute-start(bf16[128,512]{1,0:T(8,128)(2,1)S(1)} %collective-permute-done.1), channel_id=1, source_target_pairs={{0,8},{1,9},{2,10},{3,11},{4,12},{5,13},{6,14},{7,15},{8,0},{9,1},... | collective-permute-start | bytes 393224 | tf_op jit(solution)/shard_map/ppermute | solution.py:93
  15.6 1.1 %collective-permute-start.7 = (bf16[128,512]{1,0:T(8,128)(2,1)S(1)}, bf16[128,512]{1,0:T(8,128)(2,1)S(1)}, u32[]{:S(2)}, u32[]{:S(2)}) collective-permute-start(bf16[128,512]{1,0:T(8,128)(2,1)S(1)} %collective-permute-done.2), channel_id=1, source_target_pairs={{0,8},{1,7},{2,10},{3,5},{4,12},{5,3},{6,14},{7,1},{8,0},{9,15},{1... | collective-permute-start | bytes 393224 | tf_op jit(solution)/shard_map/ppermute | solution.py:93
  16.7 0.1 collective-permute-done.4
  16.8 1.4 %collective-permute-start.8 = (bf16[128,512]{1,0:T(8,128)(2,1)S(1)}, bf16[128,512]{1,0:T(8,128)(2,1)S(1)}, u32[]{:S(2)}, u32[]{:S(2)}) collective-permute-start(bf16[128,512]{1,0:T(8,128)(2,1)S(1)} %collective-permute-done.4), channel_id=1, source_target_pairs={{0,2},{1,5},{2,0},{3,7},{4,6},{5,1},{6,4},{7,3},{8,10},{9,13},{10,... | collective-permute-start | bytes 393224 | tf_op jit(solution)/shard_map/ppermute | solution.py:93
  18.2 0.2 collective-permute-done.5
  18.4 0.1 collective-permute-start.9
  18.5 0.0 collective-permute-done.3.refs_2_
  18.5 0.0 copy-done
  18.5 0.0 copy-done.1
  18.5 1.5 %shard_map.41 = (bf16[1152,512]{1,0:T(8,128)(2,1)S(1)}, f32[128,1152]{1,0:T(8,128)S(1)}, f32[8,1152]{1,0:T(8,128)S(1)}, f32[128,128]{1,0:T(8,128)S(1)}) custom-call(s32[1,128]{1,0:T(1,128)S(1)} %bitcast.2, bf16[128,512]{1,0:T(8,128)(2,1)S(1)} %copy-done, bf16[128,512]{1,0:T(8,128)(2,1)S(1)} %copy-done, ...), custom_call_target="tpu_custom_call" | custom-call | flops 1000 | tf_op jit(solution)/shard_map/pallas_call | solution.py:339
  20.0 0.0 collective-permute-done.6.refs_3_
  20.1 1.0 %collective-permute-done.7.refs_4_ = bf16[128,512]{1,0:T(8,128)(2,1)S(1)} collective-permute-done((bf16[128,512]{1,0:T(8,128)(2,1)S(1)}, bf16[128,512]{1,0:T(8,128)(2,1)S(1)}, u32[]{:S(2)}, u32[]{:S(2)}) %collective-permute-start.7) | collective-permute-done | bytes 131104 | tf_op jit(solution)/shard_map/ppermute | solution.py:93
  21.0 0.7 %shard_map.42 = (bf16[256,512]{1,0:T(8,128)(2,1)S(1)}, f32[128,256]{1,0:T(8,128)S(1)}, f32[8,1408]{1,0:T(8,128)S(1)}, f32[128,128]{1,0:T(8,128)S(1)}) custom-call(s32[1,128]{1,0:T(1,128)S(1)} %bitcast.3, bf16[128,512]{1,0:T(8,128)(2,1)S(1)} %copy-done, bf16[1152,512]{1,0:T(8,128)(2,1)S(1)} %get-tuple-element.26.refs_0_, ...), custom_call_target="tpu_custom_call" | custom-call | flops 1000 | tf_op jit(solution)/shard_map/pallas_call | solution.py:339
  21.8 0.0 collective-permute-done.8.refs_4_
  21.8 0.1 collective-permute-start.10
  21.9 0.5 %collective-permute-start.11 = (bf16[128,512]{1,0:T(8,128)(2,1)S(1)}, bf16[128,512]{1,0:T(8,128)(2,1)S(1)}, u32[]{:S(2)}, u32[]{:S(2)}) collective-permute-start(bf16[128,512]{1,0:T(8,128)(2,1)S(1)} %collective-permute-done.6.refs_3_), channel_id=1, source_target_pairs={{0,1},{1,0},{2,3},{3,2},{4,5},{5,4},{6,7},{7,6},{8,9},{9,8},{10,11... | collective-permute-start | bytes 393224 | tf_op jit(solution)/shard_map/ppermute | solution.py:97
  22.4 0.0 collective-permute-done.9.refs_5_
  22.4 1.3 %shard_map.43 = (bf16[384,512]{1,0:T(8,128)(2,1)S(1)}, f32[128,384]{1,0:T(8,128)S(1)}, f32[8,1792]{1,0:T(8,128)S(1)}, f32[128,128]{1,0:T(8,128)S(1)}) custom-call(s32[1,128]{1,0:T(1,128)S(1)} %bitcast.4, bf16[128,512]{1,0:T(8,128)(2,1)S(1)} %copy-done, bf16[1152,512]{1,0:T(8,128)(2,1)S(1)} %get-tuple-element.26.refs_0_, ...), custom_call_target="tpu_custom_call" | custom-call | flops 1000 | tf_op jit(solution)/shard_map/pallas_call | solution.py:339
  23.6 0.0 collective-permute-done.10.refs_8_
  23.7 0.0 collective-permute-done.11.refs_9_
  23.7 2.1 %shard_map.44 = (f32[128,512]{1,0:T(8,128)}, f32[1,128]{1,0:T(1,128)}) custom-call(s32[1,128]{1,0:T(1,128)S(1)} %bitcast.5, bf16[128,512]{1,0:T(8,128)(2,1)S(1)} %copy-done, bf16[1152,512]{1,0:T(8,128)(2,1)S(1)} %get-tuple-element.26.refs_0_, bf16[256,512]{1,0:T(8,128)(2,1)S(1)} %get-tuple-element.32.refs_1_, ...), custom_call_target="tpu_custom_call" | custom-call | flops 1000 | tf_op jit(solution)/shard_map/pallas_call | solution.py:339
  (5 shorter events, 0.1 us)
Async XLA Ops:
  0.6 17.9 %copy-start = (bf16[128,512]{1,0:T(8,128)(2,1)S(1)}, bf16[128,512]{1,0:T(8,128)(2,1)}, u32[]{:S(2)}) copy-start(bf16[128,512]{1,0:T(8,128)(2,1)} %own_ref.7) | copy-start | bytes 393220
  0.6 17.9 %copy-start.1 = (s32[128]{0:T(128)S(1)}, s32[128]{0:T(128)}, u32[]{:S(2)}) copy-start(s32[128]{0:T(128)} %param.3) | copy-start | bytes 1540
  0.6 10.9 %collective-permute-start = (bf16[128,512]{1,0:T(8,128)(2,1)}, bf16[128,512]{1,0:T(8,128)(2,1)S(1)}, u32[]{:S(2)}, u32[]{:S(2)}) collective-permute-start(bf16[128,512]{1,0:T(8,128)(2,1)} %own_ref.7), channel_id=1, source_target_pairs={{0,16},{1,25},{2,18},{3,27},{4,20},{5,29},{6,22},{7,31},{8,24},{9,... | collective-permute-start | bytes 393224 | tf_op jit(solution)/shard_map/ppermute | solution.py:93
  4.8 6.8 %collective-permute-start.1 = (bf16[128,512]{1,0:T(8,128)(2,1)}, bf16[128,512]{1,0:T(8,128)(2,1)S(1)}, u32[]{:S(2)}, u32[]{:S(2)}) collective-permute-start(bf16[128,512]{1,0:T(8,128)(2,1)} %own_ref.7), channel_id=1, source_target_pairs={{0,4},{1,3},{2,6},{3,1},{4,0},{5,7},{6,2},{7,5},{8,12},{9,11},{10,... | collective-permute-start | bytes 393224 | tf_op jit(solution)/shard_map/ppermute | solution.py:93
  6.3 6.8 %collective-permute-start.2 = (bf16[128,512]{1,0:T(8,128)(2,1)}, bf16[128,512]{1,0:T(8,128)(2,1)S(1)}, u32[]{:S(2)}, u32[]{:S(2)}) collective-permute-start(bf16[128,512]{1,0:T(8,128)(2,1)} %own_ref.7), channel_id=1, source_target_pairs={{0,6},{1,9},{2,4},{3,11},{4,2},{5,13},{6,0},{7,15},{8,14},{9,1},{1... | collective-permute-start | bytes 393224 | tf_op jit(solution)/shard_map/ppermute | solution.py:93
  11.5 5.2 %collective-permute-start.4 = (bf16[128,512]{1,0:T(8,128)(2,1)S(1)}, bf16[128,512]{1,0:T(8,128)(2,1)S(1)}, u32[]{:S(2)}, u32[]{:S(2)}) collective-permute-start(bf16[128,512]{1,0:T(8,128)(2,1)S(1)} %collective-permute-done), channel_id=1, source_target_pairs={{0,4},{1,3},{2,6},{3,1},{4,0},{5,7},{6,2},{7,5},{8,12},{9,11},{10,... | collective-permute-start | bytes 393224 | tf_op jit(solution)/shard_map/ppermute | solution.py:93
  13.1 5.4 %collective-permute-start.3 = (bf16[384,512]{1,0:T(8,128)(2,1)S(1)}, bf16[384,512]{1,0:T(8,128)(2,1)S(1)}, u32[]{:S(2)}, u32[]{:S(2)}) collective-permute-start(bf16[384,512]{1,0:T(8,128)(2,1)S(1)} %constant_dynamic-update-slice_fusion.refs_1_), channel_id=1, source_target_pairs={{0,1},{1,0},{2,3},{3,2},{4,5},{5,4},{6,7},{7,6},{8,9},{9,8},{10,11... | collective-permute-start | bytes 1179656 | tf_op jit(solution)/shard_map/ppermute | solution.py:97
  13.2 5.2 %collective-permute-start.5 = (bf16[128,512]{1,0:T(8,128)(2,1)S(1)}, bf16[128,512]{1,0:T(8,128)(2,1)S(1)}, u32[]{:S(2)}, u32[]{:S(2)}) collective-permute-start(bf16[128,512]{1,0:T(8,128)(2,1)S(1)} %collective-permute-done), channel_id=1, source_target_pairs={{0,2},{1,5},{2,0},{3,7},{4,6},{5,1},{6,4},{7,3},{8,10},{9,13},{10,... | collective-permute-start | bytes 393224 | tf_op jit(solution)/shard_map/ppermute | solution.py:93
  14.7 5.4 %collective-permute-start.6 = (bf16[128,512]{1,0:T(8,128)(2,1)S(1)}, bf16[128,512]{1,0:T(8,128)(2,1)S(1)}, u32[]{:S(2)}, u32[]{:S(2)}) collective-permute-start(bf16[128,512]{1,0:T(8,128)(2,1)S(1)} %collective-permute-done.1), channel_id=1, source_target_pairs={{0,8},{1,9},{2,10},{3,11},{4,12},{5,13},{6,14},{7,15},{8,0},{9,1},... | collective-permute-start | bytes 393224 | tf_op jit(solution)/shard_map/ppermute | solution.py:93
  15.6 5.4 %collective-permute-start.7 = (bf16[128,512]{1,0:T(8,128)(2,1)S(1)}, bf16[128,512]{1,0:T(8,128)(2,1)S(1)}, u32[]{:S(2)}, u32[]{:S(2)}) collective-permute-start(bf16[128,512]{1,0:T(8,128)(2,1)S(1)} %collective-permute-done.2), channel_id=1, source_target_pairs={{0,8},{1,7},{2,10},{3,5},{4,12},{5,3},{6,14},{7,1},{8,0},{9,15},{1... | collective-permute-start | bytes 393224 | tf_op jit(solution)/shard_map/ppermute | solution.py:93
  16.8 5.0 %collective-permute-start.8 = (bf16[128,512]{1,0:T(8,128)(2,1)S(1)}, bf16[128,512]{1,0:T(8,128)(2,1)S(1)}, u32[]{:S(2)}, u32[]{:S(2)}) collective-permute-start(bf16[128,512]{1,0:T(8,128)(2,1)S(1)} %collective-permute-done.4), channel_id=1, source_target_pairs={{0,2},{1,5},{2,0},{3,7},{4,6},{5,1},{6,4},{7,3},{8,10},{9,13},{10,... | collective-permute-start | bytes 393224 | tf_op jit(solution)/shard_map/ppermute | solution.py:93
  18.4 3.9 %collective-permute-start.9 = (bf16[256,512]{1,0:T(8,128)(2,1)S(1)}, bf16[256,512]{1,0:T(8,128)(2,1)S(1)}, u32[]{:S(2)}, u32[]{:S(2)}) collective-permute-start(bf16[256,512]{1,0:T(8,128)(2,1)S(1)} %constant_dynamic-update-slice_fusion.3.refs_3_), channel_id=1, source_target_pairs={{0,1},{1,0},{2,3},{3,2},{4,5},{5,4},{6,7},{7,6},{8,9},{9,8},{10,11... | collective-permute-start | bytes 786440 | tf_op jit(solution)/shard_map/ppermute | solution.py:97
  21.8 1.9 %collective-permute-start.10 = (bf16[128,512]{1,0:T(8,128)(2,1)S(1)}, bf16[128,512]{1,0:T(8,128)(2,1)S(1)}, u32[]{:S(2)}, u32[]{:S(2)}) collective-permute-start(bf16[128,512]{1,0:T(8,128)(2,1)S(1)} %collective-permute-done.8.refs_4_), channel_id=1, source_target_pairs={{0,1},{1,0},{2,3},{3,2},{4,5},{5,4},{6,7},{7,6},{8,9},{9,8},{10,11... | collective-permute-start | bytes 393224 | tf_op jit(solution)/shard_map/ppermute | solution.py:97
  21.9 1.8 %collective-permute-start.11 = (bf16[128,512]{1,0:T(8,128)(2,1)S(1)}, bf16[128,512]{1,0:T(8,128)(2,1)S(1)}, u32[]{:S(2)}, u32[]{:S(2)}) collective-permute-start(bf16[128,512]{1,0:T(8,128)(2,1)S(1)} %collective-permute-done.6.refs_3_), channel_id=1, source_target_pairs={{0,1},{1,0},{2,3},{3,2},{4,5},{5,4},{6,7},{7,6},{8,9},{9,8},{10,11... | collective-permute-start | bytes 393224 | tf_op jit(solution)/shard_map/ppermute | solution.py:97
